TPU v7x, 32 devices: a whole 2x2x4 slice. The times are simulated.
32 devices in a mesh: user: 8 (over y, x, core), item: 4 (over z).
Axes of the slice: x: 2, y: 2, z: 4, core: 2. Of those that a mesh axis runs over, the one named last changes fastest.
Arguments:
- user_pred: bfloat16 [8192, 128], P('user'), may hold values from -1.75 to 1.75
- user_imp: bfloat16 [8192, 128], P('user'), may hold values from -1.75 to 1.75
- item_pred: bfloat16 [1024, 128], P('item'), may hold values from -1.75 to 1.75
- item_imp: bfloat16 [1024, 128], P('item'), may hold values from -1.75 to 1.75
- uno_user: int32 [8, 4, 64], P('user', 'item'), may hold values from 0 to 7
- uno_item: int32 [8, 4, 64], P('user', 'item'), may hold values from 0 to 1
- obs_user: int32 [8, 4, 16], P('user', 'item'), may hold values from 0 to 7
- obs_item: int32 [8, 4, 16], P('user', 'item'), may hold values from 0 to 1
- obs_count: int32 [8, 4, 4], P('user', 'item'), may hold values from 0 to 4
- obs_label: int32 [8, 4, 16, 128, 128], P('user', 'item'), may hold values from 0 to 2
- obs_prop: bfloat16 [8, 4, 16, 128, 128], P('user', 'item'), may hold values from 0.099609375 to 1
Outputs:
- user_pred_grad: float32 [8192, 128], P(('user', 'item'))
- user_imp_grad: float32 [8192, 128], P(('user', 'item'))
- item_pred_grad: float32 [1024, 128], P(('item', 'user'))
- item_imp_grad: float32 [1024, 128], P(('item', 'user'))
Inputs may be any that keep to these rules, and one draw needn't show every extreme that they name: `uno_item`: each device's unobserved slots come in equal groups, one group for each item shard in order. Each device's observed slots come in equal groups of 16 / number of item indices, one group for each item shard in order; only the first obs_count slots of a group hold tiles.
All inputs are finite; a program needn't handle non-finite values.
Results may differ from a plain program's by a relative error of at most 0.0027.
Values may be sent and summed in bfloat16 or wider, within the bound.
No kernel may reach another device: no remote copies, remote signals or barrier semaphores. Data moves between devices by JAX's collectives and lax.ppermute only.
A program may use at most 64 MiB of HBM per device.

v0:
```python
import jax
import jax.numpy as jnp
from jax import lax
from jax.sharding import PartitionSpec as P

loss_weight = 0.015625


def shifted(x, axis, by):
    length = lax.axis_size(axis)
    return lax.ppermute(x, axis, [(i, (i + by) % length) for i in range(length)])


def product(form, first, second):
    return jnp.einsum(form, first, second, preferred_element_type=jnp.float32)


def segments(form, onehot, values):
    return jnp.einsum(form, onehot, values, precision=lax.Precision.HIGHEST)


def shards(
    user_pred,
    user_imp,
    item_pred,
    item_imp,
    uno_user,
    uno_item,
    obs_user,
    obs_item,
    obs_count,
    obs_label,
    obs_prop,
):
    item_ways = lax.axis_size("item")
    position = lax.axis_index("item")
    tile_size = obs_label.shape[-1]
    rank_size = user_pred.shape[1]
    user_rows = user_pred.shape[0]
    shard_rows = item_pred.shape[0]
    user_blocks = user_rows // tile_size
    item_blocks = shard_rows // tile_size
    own_pred = user_pred.reshape(user_blocks, tile_size, rank_size)
    own_imp = user_imp.reshape(user_blocks, tile_size, rank_size)
    uno_users = uno_user.reshape(item_ways, -1)
    uno_items = uno_item.reshape(item_ways, -1)
    obs_users = obs_user.reshape(item_ways, -1)
    obs_items = obs_item.reshape(item_ways, -1)
    counts = obs_count.reshape(item_ways)
    labels = obs_label.reshape(item_ways, -1, tile_size, tile_size)
    propens = obs_prop.reshape(item_ways, -1, tile_size, tile_size)
    obs_slots = obs_users.shape[1]
    user_range = jnp.arange(user_blocks, dtype=jnp.int32)[:, None]
    item_range = jnp.arange(item_blocks, dtype=jnp.int32)[:, None]

    def select_row(table, shard):
        return lax.dynamic_index_in_dim(table, shard, 0, keepdims=False)

    def shard_terms(piece, shard):
        blocks = piece.reshape(2, item_blocks, tile_size, rank_size)
        user_ids = select_row(uno_users, shard)
        item_ids = select_row(uno_items, shard)
        user_tiles = own_pred[user_ids]
        item_tiles = blocks[0][item_ids]
        logits = product("tar,tbr->tab", user_tiles, item_tiles)
        imputed = product("tar,tbr->tab", own_imp[user_ids], blocks[1][item_ids])
        grads = ((jax.nn.sigmoid(logits) - jax.nn.sigmoid(imputed)) * loss_weight).astype(
            jnp.bfloat16
        )
        user_delta = product("tab,tbr->tar", grads, item_tiles)
        item_delta = product("tab,tar->tbr", grads, user_tiles)
        ouser_ids = select_row(obs_users, shard)
        oitem_ids = select_row(obs_items, shard)
        ou_tiles = own_pred[ouser_ids]
        ox_tiles = own_imp[ouser_ids]
        ov_tiles = blocks[0][oitem_ids]
        oy_tiles = blocks[1][oitem_ids]
        ologits = product("tar,tbr->tab", ou_tiles, ov_tiles)
        oimputed = product("tar,tbr->tab", ox_tiles, oy_tiles)
        predicted = jax.nn.sigmoid(ologits)
        imputes = jax.nn.sigmoid(oimputed)
        valid = (jnp.arange(obs_slots, dtype=jnp.int32) < select_row(counts, shard)).astype(
            jnp.float32
        )[:, None, None]
        state_tile = select_row(labels, shard)
        seen = (state_tile > 0).astype(jnp.float32)
        clicks = (state_tile == 2).astype(jnp.float32)
        weight = valid * seen / select_row(propens, shard).astype(jnp.float32)
        ograds = (
            (valid * (predicted - imputes) + weight * (imputes - clicks)) * loss_weight
        ).astype(jnp.bfloat16)
        ohgrads = (
            2.0
            * weight
            * (imputes - clicks)
            * ologits
            * ologits
            * imputes
            * (1.0 - imputes)
            * loss_weight
        ).astype(jnp.bfloat16)
        user_onehot = (user_ids[None, :] == user_range).astype(jnp.float32)
        ouser_onehot = (ouser_ids[None, :] == user_range).astype(jnp.float32)
        item_onehot = (item_ids[None, :] == item_range).astype(jnp.float32)
        oitem_onehot = (oitem_ids[None, :] == item_range).astype(jnp.float32)
        user_pred_term = segments("kt,tar->kar", user_onehot, user_delta) + segments(
            "kt,tar->kar", ouser_onehot, product("tab,tbr->tar", ograds, ov_tiles)
        )
        user_imp_term = segments(
            "kt,tar->kar", ouser_onehot, product("tab,tbr->tar", ohgrads, oy_tiles)
        )
        item_pred_term = segments("kt,tbr->kbr", item_onehot, item_delta) + segments(
            "kt,tbr->kbr", oitem_onehot, product("tab,tar->tbr", ograds, ou_tiles)
        )
        item_imp_term = segments(
            "kt,tbr->kbr", oitem_onehot, product("tab,tar->tbr", ohgrads, ox_tiles)
        )
        user_term = jnp.stack([user_pred_term, user_imp_term]).reshape(2, user_rows, rank_size)
        item_term = jnp.stack([item_pred_term, item_imp_term]).reshape(2, shard_rows, rank_size)
        return (user_term, item_term)

    def add_items(item_acc, item_term):
        return item_acc + item_term

    def advance(cycle_step, carried_state):
        piece, user_acc, item_acc = carried_state
        shard = (position - cycle_step) % item_ways
        user_term, item_term = shard_terms(piece, shard)
        item_acc = add_items(item_acc, item_term)
        item_acc = shifted(item_acc, "item", 1)
        piece = shifted(piece, "item", 1)
        return (piece, user_acc + user_term, item_acc)

    start_piece = jnp.stack([item_pred, item_imp])
    user_zeros = jnp.zeros((2, user_rows, rank_size), jnp.float32)
    item_zeros = jnp.zeros((2, shard_rows, rank_size), jnp.float32)
    final_state = lax.fori_loop(0, item_ways - 1, advance, (start_piece, user_zeros, item_zeros))
    piece, user_acc, item_acc = final_state
    shard = (position - (item_ways - 1)) % item_ways
    user_term, item_term = shard_terms(piece, shard)
    item_acc = add_items(item_acc, item_term)
    item_acc = shifted(item_acc, "item", 1)
    user_acc, item_acc = (user_acc + user_term, item_acc)
    user_share = lax.psum_scatter(user_acc, "item", scatter_dimension=1, tiled=True)
    item_share = lax.psum_scatter(item_acc, "user", scatter_dimension=1, tiled=True)
    return (user_share[0], user_share[1], item_share[0], item_share[1])


def solution(mesh):
    in_specs = (
        P("user", None),
        P("user", None),
        P("item", None),
        P("item", None),
        P("user", "item", None),
        P("user", "item", None),
        P("user", "item", None),
        P("user", "item", None),
        P("user", "item", None),
        P("user", "item", None, None, None),
        P("user", "item", None, None, None),
    )
    out_specs = (
        P(("user", "item"), None),
        P(("user", "item"), None),
        P(("item", "user"), None),
        P(("item", "user"), None),
    )
    return jax.shard_map(shards, mesh=mesh, in_specs=in_specs, out_specs=out_specs, check_vma=False)
```

profile of v0, /device:TPU:0, one launch (start us, length us, event | category | flops | bytes accessed | tf_op | source)
XLA Modules:
  0.0 199.4 jit_solution(9404014628354273622)
XLA Ops:
  7.9 0.7 reduce.12
  9.2 0.7 reduce.13
  11.2 0.7 reduce.14
  12.5 0.7 reduce.15
  13.3 2.4 %gather_fusion.8 = bf16[16,128,128]{2,1,0:T(8,128)(2,1)} fusion(bf16[8,128,128]{2,1,0:T(8,128)(2,1)} %bitcast.271, s32[1024]{0:T(1024)S(1)} %pad_clamp_fusion.7), kind=kCustom, calls=%fused_computation.8 | custom fusion | bytes 1048640 | tf_op jit(solution)/shard_map/gather | solution.py:63
  15.7 1.4 gather_fusion.10
  17.1 0.7 pad_maximum_fusion
  18.3 0.7 broadcast_in_dim.15
  19.0 85.4 %while.21 = (s32[]{:T(128)}, bf16[2,256,128]{2,1,0:T(8,128)(2,1)}, f32[2,1024,128]{2,1,0:T(8,128)S(1)}, f32[2,256,128]{2,1,0:T(8,128)}, s32[]{:T(128)}, /*index=...) while((s32[]{:T(128)}, bf16[2,256,128]{2,1,0:T(8,128)(2,1)}, ...), condition=%wide.region_1.2_spmd.clone.clone, body=%wide.region_0.1_spmd.clone.clone.sunk | while | flops 421564800 | bytes 37636340 | solution.py:137
  19.0 0.9 copy.84
  19.9 3.0 %collective-permute-start = (bf16[2,256,128]{2,1,0:T(8,128)(2,1)S(1)}, bf16[2,256,128]{2,1,0:T(8,128)(2,1)}, u32[]{:S(2)}, u32[]{:S(2)}) collective-permute-start(bf16[2,256,128]{2,1,0:T(8,128)(2,1)S(1)} %copy.84), channel_id=1, source_target_pairs={{0,1},{1,2},{2,3},{3,0},{4,5},{5,6},{6,7},{7,4},{8,9},{9,10},{10,1... | collective-permute-start | bytes 393224 | tf_op jit(solution)/shard_map/while/body/eval_jaxpr/ppermute | solution.py:11
  23.0 0.6 gather_fusion.5
  23.7 1.4 gather_fusion.7
  26.9 1.4 gather_fusion.6
  31.7 0.7 dynamic_slice.183
  33.2 1.4 multiply_convert_fusion.3
  34.8 1.1 fusion.262
  36.4 0.9 copy-done.5
  38.1 1.7 maximum_add_fusion.7
  39.8 1.6 collective-permute-start.1
  43.2 1.1 fusion.255
  46.0 3.6 %collective-permute-done.1 = f32[2,256,128]{2,1,0:T(8,128)} collective-permute-done((f32[2,256,128]{2,1,0:T(8,128)}, f32[2,256,128]{2,1,0:T(8,128)}, u32[]{:S(2)}, u32[]{:S(2)}) %collective-permute-start.1) | collective-permute-done | bytes 262176 | tf_op jit(solution)/shard_map/while/body/eval_jaxpr/ppermute | solution.py:11
  49.6 0.7 copy-done.22
  50.3 0.9 copy.84
  51.9 1.4 gather_fusion.7
  54.5 0.6 gather_fusion.4
  55.2 1.4 gather_fusion.6
  59.9 0.7 dynamic_slice.183
  61.4 1.4 multiply_convert_fusion.3
  63.1 1.1 fusion.262
  64.7 0.9 copy-done.5
  66.3 1.7 maximum_add_fusion.7
  68.0 1.3 collective-permute-start.1
  71.2 1.1 fusion.255
  74.0 3.0 %collective-permute-done.1 = f32[2,256,128]{2,1,0:T(8,128)} collective-permute-done((f32[2,256,128]{2,1,0:T(8,128)}, f32[2,256,128]{2,1,0:T(8,128)}, u32[]{:S(2)}, u32[]{:S(2)}) %collective-permute-start.1) | collective-permute-done | bytes 262176 | tf_op jit(solution)/shard_map/while/body/eval_jaxpr/ppermute | solution.py:11
  77.0 0.7 copy-done.22
  77.6 0.9 copy.84
  78.6 0.6 gather_fusion.5
  79.3 1.4 gather_fusion.7
  82.5 1.4 gather_fusion.6
  87.2 0.7 dynamic_slice.183
  88.7 1.4 multiply_convert_fusion.3
  90.4 1.1 fusion.262
  92.0 0.9 copy-done.5
  93.6 1.7 maximum_add_fusion.7
  95.3 0.6 collective-permute-start.1
  97.8 1.1 fusion.255
  100.6 3.2 %collective-permute-done.1 = f32[2,256,128]{2,1,0:T(8,128)} collective-permute-done((f32[2,256,128]{2,1,0:T(8,128)}, f32[2,256,128]{2,1,0:T(8,128)}, u32[]{:S(2)}, u32[]{:S(2)}) %collective-permute-start.1) | collective-permute-done | bytes 262176 | tf_op jit(solution)/shard_map/while/body/eval_jaxpr/ppermute | solution.py:11
  103.8 0.7 copy-done.22
  104.5 0.9 fusion.105
  105.3 0.8 gather_fusion.9
  106.1 1.5 gather_fusion.11
  113.9 0.7 compare_convert_fusion.1
  114.7 1.4 multiply_convert_fusion.1
  117.0 1.1 fusion.66
  119.4 1.0 maximum_add_fusion.3
  121.5 1.1 fusion.68
  123.4 5.2 %collective-permute-done.2 = f32[2,256,128]{2,1,0:T(8,128)S(1)} collective-permute-done((f32[2,256,128]{2,1,0:T(8,128)S(1)}, f32[2,256,128]{2,1,0:T(8,128)S(1)}, u32[]{:S(2)}, u32[]{:S(2)}) %collective-permute-start.2) | collective-permute-done | bytes 262176 | tf_op jit(solution)/shard_map/ppermute | solution.py:11
  128.6 0.7 copy-done.9
  130.2 1.1 maximum_add_fusion.2
  131.3 29.9 %reduce-scatter.5.cloned.1.call-done = f32[2,32,128]{2,1,0:T(8,128)} async-done(((f32[2,256,128]{2,1,0:T(8,128)}), f32[2,32,128]{2,1,0:T(8,128)}) %reduce-scatter.5.cloned.1.call-update) | async-done | bytes 32784 | tf_op jit(solution)/shard_map/reduce_scatter | solution.py:145
  161.3 1.3 slice_bitcast_fusion.2
  162.6 28.2 %reduce-scatter.3.cloned.1.call-done = f32[2,256,128]{2,1,0:T(8,128)} async-done(((f32[2,1024,128]{2,1,0:T(8,128)}), f32[2,256,128]{2,1,0:T(8,128)}) %reduce-scatter.3.cloned.1.call-update) | async-done | bytes 262160 | tf_op jit(solution)/shard_map/reduce_scatter | solution.py:144
  190.8 1.7 slice_bitcast_fusion
  (214 shorter events, 48.0 us)
Async XLA Ops:
  7.2 154.1 %reduce-scatter.5.cloned.1.call-start = ((), (), s32[]{:S(2)}) async-start(), calls=%async_computation.3 | async-start | bytes 294912 | tf_op jit(solution)/shard_map/reduce_scatter | solution.py:145
  7.2 0.7 copy-start.17
  8.6 0.7 copy-start.18
  10.5 0.7 copy-start.19
  11.9 0.7 copy-start.20
  13.3 2.4 %copy-start.1 = (bf16[1024,128]{1,0:T(8,128)(2,1)S(1)}, bf16[1024,128]{1,0:T(8,128)(2,1)}, u32[]{:S(2)}) copy-start(bf16[1024,128]{1,0:T(8,128)(2,1)} %param.14) | copy-start | bytes 786436
  15.7 1.4 copy-start.10
  15.7 1.4 copy-start.11
  17.1 1.9 copy-start
  18.3 0.7 copy-start.21
  19.9 26.0 %collective-permute-start = (bf16[2,256,128]{2,1,0:T(8,128)(2,1)S(1)}, bf16[2,256,128]{2,1,0:T(8,128)(2,1)}, u32[]{:S(2)}, u32[]{:S(2)}) collective-permute-start(bf16[2,256,128]{2,1,0:T(8,128)(2,1)S(1)} %copy.84), channel_id=1, source_target_pairs={{0,1},{1,2},{2,3},{3,0},{4,5},{5,6},{6,7},{7,4},{8,9},{9,10},{10,1... | collective-permute-start | bytes 393224 | tf_op jit(solution)/shard_map/while/body/eval_jaxpr/ppermute | solution.py:11
  29.5 3.6 %copy-start.4 = (bf16[4,128,128]{2,1,0:T(8,128)(2,1)}, bf16[4,128,128]{2,1,0:T(8,128)(2,1)S(1)}, u32[]{:S(2)}) copy-start(bf16[4,128,128]{2,1,0:T(8,128)(2,1)S(1)} %gather_fusion.2) | copy-start | bytes 393220 | tf_op jit(solution)/shard_map/while
  29.5 1.1 copy-start.2
  29.6 1.2 copy-start.3
  36.4 0.9 copy-start.5
  39.8 9.9 %collective-permute-start.1 = (f32[2,256,128]{2,1,0:T(8,128)}, f32[2,256,128]{2,1,0:T(8,128)}, u32[]{:S(2)}, u32[]{:S(2)}) collective-permute-start(f32[2,256,128]{2,1,0:T(8,128)} %maximum_add_fusion.7), channel_id=1, source_target_pairs={{0,1},{1,2},{2,3},{3,0},{4,5},{5,6},{6,7},{7,4},{8,9},{9,10},{10,1... | collective-permute-start | bytes 786440 | tf_op jit(solution)/shard_map/while/body/eval_jaxpr/ppermute | solution.py:11
  42.5 0.7 copy-start.12
  49.6 0.7 copy-start.22
  51.2 22.8 %collective-permute-start = (bf16[2,256,128]{2,1,0:T(8,128)(2,1)S(1)}, bf16[2,256,128]{2,1,0:T(8,128)(2,1)}, u32[]{:S(2)}, u32[]{:S(2)}) collective-permute-start(bf16[2,256,128]{2,1,0:T(8,128)(2,1)S(1)} %copy.84), channel_id=1, source_target_pairs={{0,1},{1,2},{2,3},{3,0},{4,5},{5,6},{6,7},{7,4},{8,9},{9,10},{10,1... | collective-permute-start | bytes 393224 | tf_op jit(solution)/shard_map/while/body/eval_jaxpr/ppermute | solution.py:11
  57.8 3.6 %copy-start.4 = (bf16[4,128,128]{2,1,0:T(8,128)(2,1)}, bf16[4,128,128]{2,1,0:T(8,128)(2,1)S(1)}, u32[]{:S(2)}) copy-start(bf16[4,128,128]{2,1,0:T(8,128)(2,1)S(1)} %gather_fusion.2) | copy-start | bytes 393220 | tf_op jit(solution)/shard_map/while
  57.8 1.1 copy-start.2
  57.8 1.2 copy-start.3
  64.6 0.9 copy-start.5
  68.0 9.0 %collective-permute-start.1 = (f32[2,256,128]{2,1,0:T(8,128)}, f32[2,256,128]{2,1,0:T(8,128)}, u32[]{:S(2)}, u32[]{:S(2)}) collective-permute-start(f32[2,256,128]{2,1,0:T(8,128)} %maximum_add_fusion.7), channel_id=1, source_target_pairs={{0,1},{1,2},{2,3},{3,0},{4,5},{5,6},{6,7},{7,4},{8,9},{9,10},{10,1... | collective-permute-start | bytes 786440 | tf_op jit(solution)/shard_map/while/body/eval_jaxpr/ppermute | solution.py:11
  70.5 0.7 copy-start.12
  77.0 0.7 copy-start.22
  78.5 22.1 %collective-permute-start = (bf16[2,256,128]{2,1,0:T(8,128)(2,1)S(1)}, bf16[2,256,128]{2,1,0:T(8,128)(2,1)}, u32[]{:S(2)}, u32[]{:S(2)}) collective-permute-start(bf16[2,256,128]{2,1,0:T(8,128)(2,1)S(1)} %copy.84), channel_id=1, source_target_pairs={{0,1},{1,2},{2,3},{3,0},{4,5},{5,6},{6,7},{7,4},{8,9},{9,10},{10,1... | collective-permute-start | bytes 393224 | tf_op jit(solution)/shard_map/while/body/eval_jaxpr/ppermute | solution.py:11
  85.1 3.6 %copy-start.4 = (bf16[4,128,128]{2,1,0:T(8,128)(2,1)}, bf16[4,128,128]{2,1,0:T(8,128)(2,1)S(1)}, u32[]{:S(2)}) copy-start(bf16[4,128,128]{2,1,0:T(8,128)(2,1)S(1)} %gather_fusion.2) | copy-start | bytes 393220 | tf_op jit(solution)/shard_map/while
  85.1 1.1 copy-start.2
  85.1 1.2 copy-start.3
  92.0 0.9 copy-start.5
  95.3 8.5 %collective-permute-start.1 = (f32[2,256,128]{2,1,0:T(8,128)}, f32[2,256,128]{2,1,0:T(8,128)}, u32[]{:S(2)}, u32[]{:S(2)}) collective-permute-start(f32[2,256,128]{2,1,0:T(8,128)} %maximum_add_fusion.7), channel_id=1, source_target_pairs={{0,1},{1,2},{2,3},{3,0},{4,5},{5,6},{6,7},{7,4},{8,9},{9,10},{10,1... | collective-permute-start | bytes 786440 | tf_op jit(solution)/shard_map/while/body/eval_jaxpr/ppermute | solution.py:11
  97.2 0.7 copy-start.12
  103.8 0.7 copy-start.22
  107.7 0.6 copy-start.16
  108.3 3.5 %copy-start.6 = (bf16[16,128,128]{2,1,0:T(8,128)(2,1)S(1)}, bf16[16,128,128]{2,1,0:T(8,128)(2,1)}, u32[]{:S(2)}) copy-start(bf16[16,128,128]{2,1,0:T(8,128)(2,1)} %gather_fusion.8) | copy-start | bytes 1572868
  109.4 0.6 copy-start.15
  111.8 1.0 copy-start.7
  111.8 1.2 copy-start.8
  116.4 0.6 copy-start.14
  120.4 8.2 %collective-permute-start.2 = (f32[2,256,128]{2,1,0:T(8,128)S(1)}, f32[2,256,128]{2,1,0:T(8,128)S(1)}, u32[]{:S(2)}, u32[]{:S(2)}) collective-permute-start(f32[2,256,128]{2,1,0:T(8,128)S(1)} %maximum_add_fusion.3), channel_id=1, source_target_pairs={{0,1},{1,2},{2,3},{3,0},{4,5},{5,6},{6,7},{7,4},{8,9},{9,10},{10,1... | collective-permute-start | bytes 786440 | tf_op jit(solution)/shard_map/ppermute | solution.py:11
  120.9 0.6 copy-start.13
  128.6 0.7 copy-start.9
  129.3 61.5 %reduce-scatter.3.cloned.1.call-start = ((), (), s32[]{:S(2)}) async-start(), calls=%async_computation.2 | async-start | bytes 1310720 | tf_op jit(solution)/shard_map/reduce_scatter | solution.py:144
Sparse Core Ops, SparseCore 0:
  129.4 31.7 reduce-scatter.4
  163.7 27.1 reduce-scatter.2
where the time goes:
time: 200 us; the launch traced here: 199 us
  waiting for transfers between devices  73.2 us (37%)
  local copies, waits for them, and re-layouts  55.2 us (28%)
  matrix products  33.7 us (17%)
  other arithmetic  15.1 us (8%)
  between operations  14.4 us (7%)
  starting transfers between devices  6.74 us (3%)
    reduce_scatter x1, waiting for transfers between devices, shards(): lax.psum_scatter(item_acc, 'user', scatter_dimension=1, tiled=True)  29.9 us
    reduce_scatter x1, waiting for transfers between devices, shards(): lax.psum_scatter(user_acc, 'item', scatter_dimension=1, tiled=True)  28.2 us
    dot_general x24, matrix products, segments(): return jnp.einsum(form, onehot, values, precision=lax.Precision.HIGHEST)  17.3 us
    dot_general x40, matrix products, product(): return jnp.einsum(form, first, second, preferred_element_type=jnp.float32)  16.3 us
    ppermute x7, waiting for transfers between devices, shifted(): lax.ppermute(x, axis, [(i, (i + by) % length) for i in range(length)])  15 us
    gather x8, local copies, waits for them, and re-layouts, shard_terms(): imputed = product('tar,tbr->tab', own_imp[user_ids], blocks[1][item_ids])  11.4 us
    while x39, local copies, waits for them, and re-layouts  11.4 us
    ppermute x7, starting transfers between devices, shifted(): lax.ppermute(x, axis, [(i, (i + by) % length) for i in range(length)])  6.66 us
  transfers between devices with their start and end apart: 9, of which 6 were waited for; matrix products, arithmetic and copies ran while one was open for 31% of the time, Pallas kernels for 0%

commit v1 on v0

v1 whole, which is shorter than its diff:
```python
import jax
import jax.numpy as jnp
from jax import lax
from jax.experimental import pallas as pl
from jax.experimental.pallas import tpu as pltpu
from jax.sharding import PartitionSpec as P

loss_weight = 0.015625
cores = 2
vmem_bytes = 48 * 1024 * 1024

VM = pl.BlockSpec(memory_space=pltpu.VMEM)
SM = pl.BlockSpec(memory_space=pltpu.SMEM)


def dot(first, second, dims):
    return lax.dot_general(first, second, (dims, ((), ())), preferred_element_type=jnp.float32)


def rows_by_cols(first, second):
    return dot(first, second, ((1,), (1,)))


def plain(first, second):
    return dot(first, second, ((1,), (0,)))


def over_rows(first, second):
    return dot(first, second, ((0,), (0,)))


def call(body, name, out_shapes, specs, args, cost, scratch=()):
    return pl.pallas_call(
        body,
        out_shape=out_shapes,
        in_specs=specs,
        out_specs=tuple(VM for _ in out_shapes),
        scratch_shapes=list(scratch),
        compiler_params=pltpu.CompilerParams(vmem_limit_bytes=vmem_bytes),
        cost_estimate=pl.CostEstimate(flops=cost[0], bytes_accessed=cost[1], transcendentals=cost[2]),
        name=name,
    )(*args)


def shape(dims, kind):
    return jax.ShapeDtypeStruct(dims, kind)


def shards(
    user_pred,
    user_imp,
    item_pred,
    item_imp,
    uno_user,
    uno_item,
    obs_user,
    obs_item,
    obs_count,
    obs_label,
    obs_prop,
):
    item_ways = lax.axis_size("item")
    user_ways = lax.axis_size("user")
    chips = user_ways // cores
    tile = obs_label.shape[-1]
    rank = user_pred.shape[1]
    user_rows = user_pred.shape[0]
    shard_rows = item_pred.shape[0]
    user_blocks = user_rows // tile
    item_blocks = shard_rows // tile
    pairs = user_blocks * item_blocks
    half = shard_rows // cores
    share = user_rows // item_ways
    item_share = shard_rows // user_ways
    uno_slots = uno_user.shape[-1] // item_ways
    obs_all = obs_user.shape[-1]
    obs_slots = obs_all // item_ways
    peers = item_ways - 1
    f32 = jnp.float32
    bf16 = jnp.bfloat16

    place = jnp.stack([lax.axis_index("item"), lax.axis_index("user")]).astype(jnp.int32)
    uno_user = uno_user.reshape(-1)
    uno_item = uno_item.reshape(-1)
    obs_user = obs_user.reshape(-1)
    obs_item = obs_item.reshape(-1)
    obs_count = obs_count.reshape(-1)
    labels = obs_label.reshape(obs_all, tile, tile)
    propens = obs_prop.reshape(obs_all, tile, tile)

    def item_peer(x, k):
        return lax.ppermute(x, "item", [(i, i ^ k) for i in range(item_ways)])

    def core_peer(x):
        return lax.ppermute(x, "user", [(i, i ^ 1) for i in range(user_ways)])

    def chip_peer(x, k):
        return lax.ppermute(x, "user", [(i, i ^ (cores * k)) for i in range(user_ways)])

    def pack(place_ref, uu_ref, ui_ref, vp_ref, vi_ref, *outs):
        pos = place_ref[0]
        core = lax.rem(place_ref[1], cores)
        start = pl.multiple_of(core * half, half)
        row = lax.broadcasted_iota(jnp.int32, (pairs, rank), 0)
        for k in range(item_ways):
            group = lax.bitwise_xor(pos, k)
            count = jnp.zeros((pairs, rank), f32)
            for s in range(uno_slots):
                at = group * uno_slots + s
                pair = uu_ref[at] * item_blocks + ui_ref[at]
                count = count + jnp.where(row == pair, 1.0, 0.0)
            if k == 0:
                outs[peers][...] = count
            else:
                out = outs[k - 1]
                out[0:half] = vp_ref[pl.ds(start, half)]
                out[half : 2 * half] = vi_ref[pl.ds(start, half)]
                out[2 * half :] = count.astype(bf16)

    packed = call(
        pack,
        "pack",
        tuple(shape((2 * half + pairs, rank), bf16) for _ in range(peers)) + (shape((pairs, rank), f32),),
        [SM, SM, SM, VM, VM],
        (place, uno_user, uno_item, item_pred, item_imp),
        (0, 400000, 0),
    )
    own_count = packed[peers]
    received = [item_peer(packed[k], k + 1) for k in range(peers)]
    swapped = [core_peer(x) for x in received]

    def observed(logits, imputed, weight, used):
        p = jax.nn.sigmoid(logits)
        q = jax.nn.sigmoid(imputed)
        miss = q - jnp.where(weight < 0, 1.0, 0.0)
        term = jnp.abs(weight) * miss
        g = (((p - q) + term) * (used * loss_weight)).astype(bf16)
        h = (2.0 * term * logits * logits * q * (1.0 - q) * (used * loss_weight)).astype(bf16)
        return g, h

    def local(
        place_ref, ou_ref, oi_ref, oc_ref, up_ref, ux_ref, vp_ref, vi_ref, lab_ref, prop_ref,
        utile_ref, itile_ref, uacc_ref, iacc_ref, w_ref,
    ):
        pos = place_ref[0]
        for t in range(obs_all):
            state = lab_ref[t]
            inverse = 1.0 / prop_ref[t].astype(f32)
            w_ref[t] = jnp.where(state == 0, 0.0, jnp.where(state == 2, -inverse, inverse))
        for u in range(user_blocks):
            urows = pl.ds(u * tile, tile)
            for b in range(item_blocks):
                irows = pl.ds(b * tile, tile)
                logits = rows_by_cols(up_ref[urows], vp_ref[irows])
                imputed = rows_by_cols(ux_ref[urows], vi_ref[irows])
                g = ((jax.nn.sigmoid(logits) - jax.nn.sigmoid(imputed)) * loss_weight).astype(bf16)
                utile_ref[u * item_blocks + b] = plain(g, vp_ref[irows])
                itile_ref[u * item_blocks + b] = over_rows(g, up_ref[urows])
        uacc_ref[...] = jnp.zeros_like(uacc_ref)
        iacc_ref[...] = jnp.zeros_like(iacc_ref)
        for s in range(obs_slots):
            at = pos * obs_slots + s
            urows = pl.ds(pl.multiple_of(ou_ref[at] * tile, tile), tile)
            irows = pl.ds(pl.multiple_of(oi_ref[at] * tile, tile), tile)
            used = jnp.where(s < oc_ref[pos], 1.0, 0.0)
            logits = rows_by_cols(up_ref[urows], vp_ref[irows])
            imputed = rows_by_cols(ux_ref[urows], vi_ref[irows])
            g, h = observed(logits, imputed, w_ref[at], used)
            uacc_ref[0, urows] += plain(g, vp_ref[irows])
            uacc_ref[1, urows] += plain(h, vi_ref[irows])
            iacc_ref[0, irows] += over_rows(g, up_ref[urows])
            iacc_ref[1, irows] += over_rows(h, ux_ref[urows])

    utile, itile, uacc, iacc, weights = call(
        local,
        "local_tiles",
        (
            shape((pairs, tile, rank), f32),
            shape((pairs, tile, rank), f32),
            shape((2, user_rows, rank), f32),
            shape((2, shard_rows, rank), f32),
            shape((obs_all, tile, tile), f32),
        ),
        [SM, SM, SM, SM, VM, VM, VM, VM, VM, VM],
        (place, obs_user, obs_item, obs_count, user_pred, user_imp, item_pred, item_imp, labels, propens),
        (4 * pairs * 2 * tile**3, 8000000, 2 * pairs * tile * tile),
    )

    def remote(
        place_ref, ou_ref, oi_ref, oc_ref, up_ref, ux_ref, count_ref, utile_ref, itile_ref, uacc_in, iacc_in, w_ref,
        *refs,
    ):
        recv = refs[:peers]
        swap = refs[peers : 2 * peers]
        outs = refs[2 * peers : 2 * peers + peers + 3]
        vbuf, uacc, iacc = refs[2 * peers + peers + 3 :]
        pos = place_ref[0]
        core = lax.rem(place_ref[1], cores)
        mine = pl.multiple_of(core * half, half)
        other = pl.multiple_of((1 - core) * half, half)
        count = count_ref[...]
        for k in range(peers):
            count = count + recv[k][2 * half :].astype(f32)
            for m in range(2):
                vbuf[k, m, pl.ds(mine, half)] = recv[k][m * half : (m + 1) * half]
                vbuf[k, m, pl.ds(other, half)] = swap[k][m * half : (m + 1) * half]
        own = pl.ds(pl.multiple_of(pos * shard_rows, shard_rows), shard_rows)
        iacc[...] = jnp.zeros_like(iacc)
        iacc[1, own] = iacc_in[1]
        for b in range(item_blocks):
            total = iacc_in[0, b * tile : (b + 1) * tile]
            for u in range(user_blocks):
                t = u * item_blocks + b
                total = total + itile_ref[t] * count[t : t + 1]
            iacc[0, pl.ds(pl.multiple_of(pos * shard_rows + b * tile, tile), tile)] = total
        for u in range(user_blocks):
            total = uacc_in[0, u * tile : (u + 1) * tile]
            for b in range(item_blocks):
                t = u * item_blocks + b
                total = total + utile_ref[t] * count[t : t + 1]
            uacc[0, u * tile : (u + 1) * tile] = total
        uacc[1] = uacc_in[1]
        for k in range(peers):
            group = lax.bitwise_xor(pos, k + 1)
            for s in range(obs_slots):
                at = group * obs_slots + s
                urows = pl.ds(pl.multiple_of(ou_ref[at] * tile, tile), tile)
                brows = pl.ds(pl.multiple_of(oi_ref[at] * tile, tile), tile)
                irows = pl.ds(pl.multiple_of(group * shard_rows + oi_ref[at] * tile, tile), tile)
                used = jnp.where(s < oc_ref[group], 1.0, 0.0)
                logits = rows_by_cols(up_ref[urows], vbuf[k, 0, brows])
                imputed = rows_by_cols(ux_ref[urows], vbuf[k, 1, brows])
                g, h = observed(logits, imputed, w_ref[at], used)
                uacc[0, urows] += plain(g, vbuf[k, 0, brows])
                uacc[1, urows] += plain(h, vbuf[k, 1, brows])
                iacc[0, irows] += over_rows(g, up_ref[urows])
                iacc[1, irows] += over_rows(h, ux_ref[urows])
        for k in range(item_ways):
            rows = pl.ds(pl.multiple_of(lax.bitwise_xor(pos, k) * share, share), share)
            for m in range(2):
                part = uacc[m, rows]
                if k == 0:
                    outs[peers][m * share : (m + 1) * share] = part
                else:
                    outs[k - 1][m * share : (m + 1) * share] = part.astype(bf16)
        send, keep = outs[peers + 1], outs[peers + 2]
        for m in range(2):
            for j in range(item_ways):
                for q in range(chips):
                    at = ((m * item_ways + j) * chips + q) * item_share
                    base = j * shard_rows + q * cores * item_share
                    to_keep = pl.ds(pl.multiple_of(base + core * item_share, item_share), item_share)
                    to_send = pl.ds(pl.multiple_of(base + (1 - core) * item_share, item_share), item_share)
                    keep[at : at + item_share] = iacc[m, to_keep]
                    send[at : at + item_share] = iacc[m, to_send].astype(bf16)

    core_rows = 2 * item_ways * chips * item_share
    results = call(
        remote,
        "remote_tiles",
        tuple(shape((2 * share, rank), bf16) for _ in range(peers))
        + (shape((2 * share, rank), f32), shape((core_rows, rank), bf16), shape((core_rows, rank), f32)),
        [SM, SM, SM, SM] + [VM] * (8 + 2 * peers),
        (
            place, obs_user, obs_item, obs_count, user_pred, user_imp, own_count, utile, itile, uacc, iacc, weights,
            *received, *swapped,
        ),
        (6 * (obs_all - obs_slots) * 2 * tile**3, 8000000, 2 * (obs_all - obs_slots) * tile * tile),
        (
            pltpu.VMEM((peers, 2, shard_rows, rank), bf16),
            pltpu.VMEM((2, user_rows, rank), f32),
            pltpu.VMEM((2, item_ways * shard_rows, rank), f32),
        ),
    )
    user_own, core_send, core_keep = results[peers:]
    core_recv = core_peer(core_send)
    user_recv = [item_peer(results[k], k + 1) for k in range(peers)]

    chip_rows = 2 * item_ways * item_share

    def fold_core(place_ref, keep_ref, recv_ref, *outs):
        chip = lax.div(place_ref[1], cores)
        for k in range(chips):
            peer = lax.bitwise_xor(chip, k)
            for g in range(2 * item_ways):
                rows = pl.ds(pl.multiple_of((g * chips + peer) * item_share, item_share), item_share)
                part = keep_ref[rows] + recv_ref[rows].astype(f32)
                outs[k][g * item_share : (g + 1) * item_share] = part.astype(outs[k].dtype)

    folded = call(
        fold_core,
        "fold_core",
        (shape((chip_rows, rank), f32),) + tuple(shape((chip_rows, rank), bf16) for _ in range(chips - 1)),
        [SM, VM, VM],
        (place, core_keep, core_recv),
        (0, 1000000, 0),
    )
    chip_recv = [chip_peer(folded[k], k) for k in range(1, chips)]

    def fold_chips(place_ref, own_ref, *refs):
        recv = refs[: chips - 1]
        outs = refs[chips - 1 :]
        pos = place_ref[0]
        for k in range(item_ways):
            peer = lax.bitwise_xor(pos, k)
            for m in range(2):
                rows = pl.ds(pl.multiple_of((m * item_ways + peer) * item_share, item_share), item_share)
                part = own_ref[rows]
                for r in recv:
                    part = part + r[rows].astype(f32)
                outs[k][m * item_share : (m + 1) * item_share] = part

    shares = call(
        fold_chips,
        "fold_chips",
        tuple(shape((2 * item_share, rank), f32) for _ in range(item_ways)),
        [SM, VM] + [VM] * (chips - 1),
        (place, folded[0], *chip_recv),
        (0, 300000, 0),
    )
    item_recv = [item_peer(shares[k], k) for k in range(1, item_ways)]

    def finish(user_ref, item_ref, *refs):
        urecv = refs[:peers]
        irecv = refs[peers : 2 * peers]
        outs = refs[2 * peers :]
        for m in range(2):
            part = user_ref[m * share : (m + 1) * share]
            for r in urecv:
                part = part + r[m * share : (m + 1) * share].astype(f32)
            outs[m][...] = part
            part = item_ref[m * item_share : (m + 1) * item_share]
            for r in irecv:
                part = part + r[m * item_share : (m + 1) * item_share]
            outs[2 + m][...] = part

    return call(
        finish,
        "finish",
        (shape((share, rank), f32),) * 2 + (shape((item_share, rank), f32),) * 2,
        [VM] * (2 + 2 * peers),
        (user_own, shares[0], *user_recv, *item_recv),
        (0, 1000000, 0),
    )


def solution(mesh):
    in_specs = (
        P("user", None),
        P("user", None),
        P("item", None),
        P("item", None),
        P("user", "item", None),
        P("user", "item", None),
        P("user", "item", None),
        P("user", "item", None),
        P("user", "item", None),
        P("user", "item", None, None, None),
        P("user", "item", None, None, None),
    )
    out_specs = (
        P(("user", "item"), None),
        P(("user", "item"), None),
        P(("item", "user"), None),
        P(("item", "user"), None),
    )
    return jax.shard_map(shards, mesh=mesh, in_specs=in_specs, out_specs=out_specs, check_vma=False)
```

time: 200 us -> 56.5 us (0.28)
  waiting for transfers between devices: 73.2 us -> 16.3 us
  local copies, waits for them, and re-layouts: 55.2 us -> 6.94 us
  matrix products: 33.7 us -> 0 us
  other arithmetic: 15.1 us -> 0.08 us
  between operations: 14.4 us -> 0.74 us
  Pallas kernels: 0 us -> 13.4 us
  starting transfers between devices: 6.74 us -> 18.7 us
    reduce_scatter x2 -> x0, waiting for transfers between devices: 58.1 us -> none  [the longest x1 29.9 us: shards(): lax.psum_scatter(item_acc, 'user', scatter_dimension=1, tiled=True)]
    dot_general x64 -> x0, matrix products: 33.7 us -> none  [the longest x24 17.3 us: segments(): return jnp.einsum(form, onehot, values, precision=lax.Precision.HIGHEST)]
    gather x32 -> x0, local copies, waits for them, and re-layouts: 27.6 us -> none  [the longest x8 11.4 us: shard_terms(): imputed = product('tar,tbr->tab', own_imp[user_ids], blocks[1][item_ids])]
    pallas_call x0 -> x6, Pallas kernels: none -> 13.4 us  [call(): pl.pallas_call(body, out_shape=out_shapes, in_specs=specs, out_specs=tupl...]
    ppermute x7 -> x16, starting transfers between devices: 6.66 us -> 18.7 us  [the longest x9 14.5 us: item_peer(): return lax.ppermute(x, 'item', [(i, i ^ k) for i in range(item_ways)])]
    while x39 -> x0, local copies, waits for them, and re-layouts: 11.4 us -> none
    add x8 -> x0, other arithmetic: 7.99 us -> none  [the longest x4 5.99 us: add_items(): return item_acc + item_term]
    squeeze x2 -> x0, local copies, waits for them, and re-layouts: 3.03 us -> none  [shards(): return (user_share[0], user_share[1], item_share[0], item_share[1])]
  transfers between devices with their start and end apart: 9 -> 16, of which waited for: 6 -> 7; matrix products, arithmetic and copies ran while one was open for 31% -> 0% of each run, Pallas kernels for 0% -> 12%
where the time goes in v1:
time: 56.5 us; the launch traced here: 56.1 us
  starting transfers between devices  18.7 us (33%)
  waiting for transfers between devices  16.3 us (29%)
  Pallas kernels  13.4 us (24%)
  local copies, waits for them, and re-layouts  6.94 us (12%)
  between operations  0.74 us (1%)
    ppermute x9, starting transfers between devices, item_peer(): return lax.ppermute(x, 'item', [(i, i ^ k) for i in range(item_ways)])  14.5 us
    pallas_call x6, Pallas kernels, call(): pl.pallas_call(body, out_shape=out_shapes, in_specs=specs, out_specs=tupl...  13.4 us
    ppermute x9, waiting for transfers between devices, item_peer(): return lax.ppermute(x, 'item', [(i, i ^ k) for i in range(item_ways)])  10.4 us
    unnamed x28, local copies, waits for them, and re-layouts  6.94 us
    ppermute x3, waiting for transfers between devices, chip_peer(): lax.ppermute(x, 'user', [(i, i ^ cores * k) for i in range(user_ways)])  4.69 us
    ppermute x3, starting transfers between devices, chip_peer(): lax.ppermute(x, 'user', [(i, i ^ cores * k) for i in range(user_ways)])  3.57 us
    ppermute x4, waiting for transfers between devices, core_peer(): return lax.ppermute(x, 'user', [(i, i ^ 1) for i in range(user_ways)])  1.17 us
  transfers between devices with their start and end apart: 16, of which 7 were waited for; matrix products, arithmetic and copies ran while one was open for 0% of the time, Pallas kernels for 12%

profile of v1, /device:TPU:0, one launch (start us, length us, event | category | flops | bytes accessed | tf_op | source)
XLA Modules:
  0.0 56.1 jit_solution(13752793113643242829)
XLA Ops:
  0.6 0.1 pad_add_fusion.place_ref
  0.7 0.0 copy-start.12
  0.7 0.0 copy-start.13
  0.7 0.7 %copy-done.12 = s32[1,1,64]{2,1,0:T(1,128)S(1)} copy-done((s32[1,1,64]{2,1,0:T(1,128)S(1)}, s32[1,1,64]{2,1,0:T(1,128)}, u32[]{:S(2)}) %copy-start.12) | copy-done | bytes 280
  1.4 0.0 copy-done.13
  1.4 0.0 copy-start.5
  1.4 0.8 %copy-done.5 = bf16[256,128]{1,0:T(8,128)(2,1)S(1)} copy-done((bf16[256,128]{1,0:T(8,128)(2,1)S(1)}, bf16[256,128]{1,0:T(8,128)(2,1)}, u32[]{:S(2)}) %copy-start.5) | copy-done | bytes 65560
  2.2 0.0 copy-start.7
  2.2 0.8 %copy-done.7 = bf16[256,128]{1,0:T(8,128)(2,1)S(1)} copy-done((bf16[256,128]{1,0:T(8,128)(2,1)S(1)}, bf16[256,128]{1,0:T(8,128)(2,1)}, u32[]{:S(2)}) %copy-start.7) | copy-done | bytes 65560
  3.1 0.0 copy-start.6
  3.1 0.0 copy-start.8
  3.1 0.7 %pack.1 = (bf16[272,128]{1,0:T(8,128)(2,1)S(1)}, bf16[272,128]{1,0:T(8,128)(2,1)S(1)}, bf16[272,128]{1,0:T(8,128)(2,1)S(1)}, f32[16,128]{1,0:T(8,128)S(1)}) custom-call(s32[2]{0:T(128)S(1)} %pad_add_fusion.place_ref, s32[64]{0:T(128)S(1)} %bitcast.16, s32[64]{0:T(128)S(1)} %bitcast.17, bf16[256,128]{1,0:T(8,128)(2,1)S(1)} %copy-done.5, ...), custom_call_target="tpu_custom_call" | custom-call | bytes 400000 | tf_op jit(solution)/shard_map/pack/pallas_call | solution.py:33
  3.7 3.1 %collective-permute-start = (bf16[272,128]{1,0:T(8,128)(2,1)S(1)}, bf16[272,128]{1,0:T(8,128)(2,1)S(1)}, u32[]{:S(2)}, u32[]{:S(2)}) collective-permute-start(bf16[272,128]{1,0:T(8,128)(2,1)S(1)} %get-tuple-element.33), channel_id=1, source_target_pairs={{0,1},{1,0},{2,3},{3,2},{4,5},{5,4},{6,7},{7,6},{8,9},{9,8},{10,11... | collective-permute-start | bytes 208904 | tf_op jit(solution)/shard_map/ppermute | solution.py:92
  6.8 2.6 %collective-permute-start.1 = (bf16[272,128]{1,0:T(8,128)(2,1)S(1)}, bf16[272,128]{1,0:T(8,128)(2,1)S(1)}, u32[]{:S(2)}, u32[]{:S(2)}) collective-permute-start(bf16[272,128]{1,0:T(8,128)(2,1)S(1)} %get-tuple-element.34), channel_id=1, source_target_pairs={{0,2},{1,3},{2,0},{3,1},{4,6},{5,7},{6,4},{7,5},{8,10},{9,11},{10,... | collective-permute-start | bytes 208904 | tf_op jit(solution)/shard_map/ppermute | solution.py:92
  9.4 0.0 collective-permute-start.2
  9.4 0.0 collective-permute-done.refs_0_
  9.4 0.0 collective-permute-start.3
  9.4 4.9 %collective-permute-done.1.refs_1_ = bf16[272,128]{1,0:T(8,128)(2,1)S(1)} collective-permute-done((bf16[272,128]{1,0:T(8,128)(2,1)S(1)}, bf16[272,128]{1,0:T(8,128)(2,1)S(1)}, u32[]{:S(2)}, u32[]{:S(2)}) %collective-permute-start.1) | collective-permute-done | bytes 69664 | tf_op jit(solution)/shard_map/ppermute | solution.py:92
  14.4 0.0 collective-permute-start.4
  14.4 1.3 %collective-permute-done.2.refs_2_ = bf16[272,128]{1,0:T(8,128)(2,1)S(1)} collective-permute-done((bf16[272,128]{1,0:T(8,128)(2,1)S(1)}, bf16[272,128]{1,0:T(8,128)(2,1)S(1)}, u32[]{:S(2)}, u32[]{:S(2)}) %collective-permute-start.2) | collective-permute-done | bytes 69664 | tf_op jit(solution)/shard_map/ppermute | solution.py:92
  15.6 0.0 collective-permute-start.5
  15.6 0.0 copy-start.9
  15.6 0.0 copy-start.10
  15.6 0.0 copy-start.11
  15.6 0.0 copy-done.6
  15.7 0.0 copy-done.8
  15.7 0.6 %copy-done.9 = s32[1,1,16]{2,1,0:T(1,128)S(1)} copy-done((s32[1,1,16]{2,1,0:T(1,128)S(1)}, s32[1,1,16]{2,1,0:T(1,128)}, u32[]{:S(2)}) %copy-start.9) | copy-done | bytes 88
  16.3 0.0 copy-done.10
  16.3 0.0 copy-done.11
  16.3 0.0 copy-start.1
  16.3 0.9 %copy-done.1 = bf16[1024,128]{1,0:T(8,128)(2,1)S(1)} copy-done((bf16[1024,128]{1,0:T(8,128)(2,1)S(1)}, bf16[1024,128]{1,0:T(8,128)(2,1)}, u32[]{:S(2)}) %copy-start.1) | copy-done | bytes 262168
  17.3 0.0 copy-start.3
  17.3 0.9 %copy-done.3 = bf16[1024,128]{1,0:T(8,128)(2,1)S(1)} copy-done((bf16[1024,128]{1,0:T(8,128)(2,1)S(1)}, bf16[1024,128]{1,0:T(8,128)(2,1)}, u32[]{:S(2)}) %copy-start.3) | copy-done | bytes 262168
  18.2 1.0 %copy-done.4 = bf16[1,1,16,128,128]{4,3,2,1,0:T(8,128)(2,1)S(1)} copy-done((bf16[1,1,16,128,128]{4,3,2,1,0:T(8,128)(2,1)S(1)}, bf16[1,1,16,128,128]{4,3,2,1,0:T(8,128)(2,1)}, u32[]{:S(2)}) %copy-start.4) | copy-done | bytes 524312
  19.3 6.2 %local_tiles.1 = (f32[16,128,128]{2,1,0:T(8,128)S(1)}, f32[16,128,128]{2,1,0:T(8,128)S(1)}, f32[2,1024,128]{2,1,0:T(8,128)S(1)}, f32[2,256,128]{2,1,0:T(8,128)S(1)}, f32[16,128,128]{2,1,0:T(8,128)S(1)}) custom-call(s32[2]{0:T(128)S(1)} %pad_add_fusion.place_ref, s32[16]{0:T(128)S(1)} %bitcast.10, s32[16]{0:T(128)S(1)} %bitcast.12, s32[4]{0:T(128)S(1)} %bitcast.14, ...), custom_call_target="tpu_custom_call" | custom-call | flops 268435456 | bytes 8000000 | tf_op jit(solution)/shard_map/local_tiles/pallas_call | solution.py:33
  25.5 1.0 %copy-done = f32[16,128,128]{2,1,0:T(8,128)} copy-done((f32[16,128,128]{2,1,0:T(8,128)}, f32[16,128,128]{2,1,0:T(8,128)S(1)}, u32[]{:S(2)}) %copy-start) | copy-done | bytes 1048600
  26.4 0.0 collective-permute-done.3.refs_3_
  26.4 0.0 collective-permute-done.4.refs_4_
  26.5 0.0 collective-permute-done.5.refs_5_
  26.5 0.0 copy-done.2
  26.5 4.7 %remote_tiles.1 = (bf16[512,128]{1,0:T(8,128)(2,1)S(1)}, bf16[512,128]{1,0:T(8,128)(2,1)S(1)}, bf16[512,128]{1,0:T(8,128)(2,1)S(1)}, f32[512,128]{1,0:T(8,128)S(...) custom-call(s32[2]{0:T(128)S(1)} %pad_add_fusion.place_ref, s32[16]{0:T(128)S(1)} %bitcast.11, ...), custom_call_target="tpu_custom_call" | custom-call | flops 301989888 | bytes 8000000 | tf_op jit(solution)/shard_map/remote_tiles/pallas_call | solution.py:33
  31.1 0.6 %collective-permute-start.6 = (bf16[1024,128]{1,0:T(8,128)(2,1)S(1)}, bf16[1024,128]{1,0:T(8,128)(2,1)S(1)}, u32[]{:S(2)}, u32[]{:S(2)}) collective-permute-start(bf16[1024,128]{1,0:T(8,128)(2,1)S(1)} %get-tuple-element.38), channel_id=1, source_target_pairs={{0,4},{4,0},{8,12},{12,8},{16,20},{20,16},{24,28},{28,24},{1,5},{5... | collective-permute-start | bytes 786440 | tf_op jit(solution)/shard_map/ppermute | solution.py:95
  31.7 1.2 %collective-permute-done.6.recv_ref = bf16[1024,128]{1,0:T(8,128)(2,1)S(1)} collective-permute-done((bf16[1024,128]{1,0:T(8,128)(2,1)S(1)}, bf16[1024,128]{1,0:T(8,128)(2,1)S(1)}, u32[]{:S(2)}, u32[]{:S(2)}) %collective-permute-start.6) | collective-permute-done | bytes 262176 | tf_op jit(solution)/shard_map/ppermute | solution.py:95
  32.9 0.6 %fold_core.1 = (f32[256,128]{1,0:T(8,128)S(1)}, bf16[256,128]{1,0:T(8,128)(2,1)S(1)}, bf16[256,128]{1,0:T(8,128)(2,1)S(1)}, bf16[256,128]{1,0:T(8,128)(2,1)S(1)}) custom-call(s32[2]{0:T(128)S(1)} %pad_add_fusion.place_ref, f32[1024,128]{1,0:T(8,128)S(1)} %get-tuple-element.37.keep_ref, bf16[1024,128]{1,0:T(8,128)(2,1)S(1)} %collective-permute-done.6.recv_ref), custom_call_target="tpu_custom_call" | custom-call | bytes 1000000 | tf_op jit(solution)/shard_map/fold_core/pallas_call | solution.py:33
  33.5 1.6 %collective-permute-start.7 = (bf16[256,128]{1,0:T(8,128)(2,1)S(1)}, bf16[256,128]{1,0:T(8,128)(2,1)S(1)}, u32[]{:S(2)}, u32[]{:S(2)}) collective-permute-start(bf16[256,128]{1,0:T(8,128)(2,1)S(1)} %get-tuple-element.40), channel_id=1, source_target_pairs={{0,8},{4,12},{8,0},{12,4},{16,24},{20,28},{24,16},{28,20},{1,9},{5... | collective-permute-start | bytes 196616 | tf_op jit(solution)/shard_map/ppermute | solution.py:98
  35.0 0.8 %collective-permute-start.10 = (bf16[512,128]{1,0:T(8,128)(2,1)S(1)}, bf16[512,128]{1,0:T(8,128)(2,1)S(1)}, u32[]{:S(2)}, u32[]{:S(2)}) collective-permute-start(bf16[512,128]{1,0:T(8,128)(2,1)S(1)} %get-tuple-element.44), channel_id=1, source_target_pairs={{0,1},{1,0},{2,3},{3,2},{4,5},{5,4},{6,7},{7,6},{8,9},{9,8},{10,11... | collective-permute-start | bytes 393224 | tf_op jit(solution)/shard_map/ppermute | solution.py:92
  35.8 2.1 %collective-permute-start.11 = (bf16[512,128]{1,0:T(8,128)(2,1)S(1)}, bf16[512,128]{1,0:T(8,128)(2,1)S(1)}, u32[]{:S(2)}, u32[]{:S(2)}) collective-permute-start(bf16[512,128]{1,0:T(8,128)(2,1)S(1)} %get-tuple-element.45), channel_id=1, source_target_pairs={{0,2},{1,3},{2,0},{3,1},{4,6},{5,7},{6,4},{7,5},{8,10},{9,11},{10,... | collective-permute-start | bytes 393224 | tf_op jit(solution)/shard_map/ppermute | solution.py:92
  37.9 1.5 %collective-permute-start.12 = (bf16[512,128]{1,0:T(8,128)(2,1)S(1)}, bf16[512,128]{1,0:T(8,128)(2,1)S(1)}, u32[]{:S(2)}, u32[]{:S(2)}) collective-permute-start(bf16[512,128]{1,0:T(8,128)(2,1)S(1)} %get-tuple-element.46), channel_id=1, source_target_pairs={{0,3},{1,2},{2,1},{3,0},{4,7},{5,6},{6,5},{7,4},{8,11},{9,10},{10,... | collective-permute-start | bytes 393224 | tf_op jit(solution)/shard_map/ppermute | solution.py:92
  39.4 1.5 %collective-permute-start.8 = (bf16[256,128]{1,0:T(8,128)(2,1)S(1)}, bf16[256,128]{1,0:T(8,128)(2,1)S(1)}, u32[]{:S(2)}, u32[]{:S(2)}) collective-permute-start(bf16[256,128]{1,0:T(8,128)(2,1)S(1)} %get-tuple-element.41), channel_id=1, source_target_pairs={{0,16},{4,20},{8,24},{12,28},{16,0},{20,4},{24,8},{28,12},{1,17},{... | collective-permute-start | bytes 196616 | tf_op jit(solution)/shard_map/ppermute | solution.py:98
  41.0 0.0 collective-permute-done.7.refs_0_
  41.0 0.5 collective-permute-start.9
  41.4 3.0 %collective-permute-done.8.refs_1_ = bf16[256,128]{1,0:T(8,128)(2,1)S(1)} collective-permute-done((bf16[256,128]{1,0:T(8,128)(2,1)S(1)}, bf16[256,128]{1,0:T(8,128)(2,1)S(1)}, u32[]{:S(2)}, u32[]{:S(2)}) %collective-permute-start.8) | collective-permute-done | bytes 65568 | tf_op jit(solution)/shard_map/ppermute | solution.py:98
  44.4 1.7 %collective-permute-done.9.refs_2_ = bf16[256,128]{1,0:T(8,128)(2,1)S(1)} collective-permute-done((bf16[256,128]{1,0:T(8,128)(2,1)S(1)}, bf16[256,128]{1,0:T(8,128)(2,1)S(1)}, u32[]{:S(2)}, u32[]{:S(2)}) %collective-permute-start.9) | collective-permute-done | bytes 65568 | tf_op jit(solution)/shard_map/ppermute | solution.py:98
  46.1 0.6 %fold_chips.1 = (f32[64,128]{1,0:T(8,128)S(1)}, f32[64,128]{1,0:T(8,128)S(1)}, f32[64,128]{1,0:T(8,128)S(1)}, f32[64,128]{1,0:T(8,128)S(1)}) custom-call(s32[2]{0:T(128)S(1)} %pad_add_fusion.place_ref, f32[256,128]{1,0:T(8,128)S(1)} %get-tuple-element.39.own_ref, bf16[256,128]{1,0:T(8,128)(2,1)S(1)} %collective-permute-done.7.refs_0_, ...), custom_call_target="tpu_custom_call" | custom-call | bytes 300000 | tf_op jit(solution)/shard_map/fold_chips/pallas_call | solution.py:33
  46.7 0.1 collective-permute-start.13
  46.8 2.9 %collective-permute-start.14 = (f32[64,128]{1,0:T(8,128)S(1)}, f32[64,128]{1,0:T(8,128)S(1)}, u32[]{:S(2)}, u32[]{:S(2)}) collective-permute-start(f32[64,128]{1,0:T(8,128)S(1)} %get-tuple-element.48), channel_id=1, source_target_pairs={{0,2},{1,3},{2,0},{3,1},{4,6},{5,7},{6,4},{7,5},{8,10},{9,11},{10,... | collective-permute-start | bytes 98312 | tf_op jit(solution)/shard_map/ppermute | solution.py:92
  49.6 0.0 collective-permute-done.10.refs_0_
  49.6 1.5 %collective-permute-start.15 = (f32[64,128]{1,0:T(8,128)S(1)}, f32[64,128]{1,0:T(8,128)S(1)}, u32[]{:S(2)}, u32[]{:S(2)}) collective-permute-start(f32[64,128]{1,0:T(8,128)S(1)} %get-tuple-element.49), channel_id=1, source_target_pairs={{0,3},{1,2},{2,1},{3,0},{4,7},{5,6},{6,5},{7,4},{8,11},{9,10},{10,... | collective-permute-start | bytes 98312 | tf_op jit(solution)/shard_map/ppermute | solution.py:92
  51.2 0.0 collective-permute-done.11.refs_1_
  51.2 0.0 collective-permute-done.12.refs_2_
  51.2 0.0 collective-permute-done.13.refs_3_
  51.2 1.0 %collective-permute-done.14.refs_4_ = f32[64,128]{1,0:T(8,128)S(1)} collective-permute-done((f32[64,128]{1,0:T(8,128)S(1)}, f32[64,128]{1,0:T(8,128)S(1)}, u32[]{:S(2)}, u32[]{:S(2)}) %collective-permute-start.14) | collective-permute-done | bytes 32800 | tf_op jit(solution)/shard_map/ppermute | solution.py:92
  52.2 3.2 %collective-permute-done.15.refs_5_ = f32[64,128]{1,0:T(8,128)S(1)} collective-permute-done((f32[64,128]{1,0:T(8,128)S(1)}, f32[64,128]{1,0:T(8,128)S(1)}, u32[]{:S(2)}, u32[]{:S(2)}) %collective-permute-start.15) | collective-permute-done | bytes 32800 | tf_op jit(solution)/shard_map/ppermute | solution.py:92
  55.4 0.7 %finish.1 = (f32[256,128]{1,0:T(8,128)}, f32[256,128]{1,0:T(8,128)}, f32[32,128]{1,0:T(8,128)}, f32[32,128]{1,0:T(8,128)}) custom-call(f32[512,128]{1,0:T(8,128)S(1)} %get-tuple-element.36.user_ref, f32[64,128]{1,0:T(8,128)S(1)} %get-tuple-element.43.item_ref, bf16[512,128]{1,0:T(8,128)(2,1)S(1)} %collective-permute-done.10.refs_0_, ...), custom_call_target="tpu_custom_call" | custom-call | bytes 1000000 | tf_op jit(solution)/shard_map/finish/pallas_call | solution.py:33
  (3 shorter events, 0.0 us)
Async XLA Ops:
  0.7 0.7 %copy-start.12 = (s32[1,1,64]{2,1,0:T(1,128)S(1)}, s32[1,1,64]{2,1,0:T(1,128)}, u32[]{:S(2)}) copy-start(s32[1,1,64]{2,1,0:T(1,128)} %param.15) | copy-start | bytes 772
  0.7 0.7 %copy-start.13 = (s32[1,1,64]{2,1,0:T(1,128)S(1)}, s32[1,1,64]{2,1,0:T(1,128)}, u32[]{:S(2)}) copy-start(s32[1,1,64]{2,1,0:T(1,128)} %param.16) | copy-start | bytes 772
  1.4 0.8 %copy-start.5 = (bf16[256,128]{1,0:T(8,128)(2,1)S(1)}, bf16[256,128]{1,0:T(8,128)(2,1)}, u32[]{:S(2)}) copy-start(bf16[256,128]{1,0:T(8,128)(2,1)} %vp_ref.3) | copy-start | bytes 196612
  2.2 0.8 %copy-start.7 = (bf16[256,128]{1,0:T(8,128)(2,1)S(1)}, bf16[256,128]{1,0:T(8,128)(2,1)}, u32[]{:S(2)}) copy-start(bf16[256,128]{1,0:T(8,128)(2,1)} %vi_ref.3) | copy-start | bytes 196612
  3.1 12.6 %copy-start.6 = (bf16[256,128]{1,0:T(8,128)(2,1)S(1)}, bf16[256,128]{1,0:T(8,128)(2,1)}, u32[]{:S(2)}) copy-start(bf16[256,128]{1,0:T(8,128)(2,1)} %vp_ref.3) | copy-start | bytes 196612
  3.1 12.6 %copy-start.8 = (bf16[256,128]{1,0:T(8,128)(2,1)S(1)}, bf16[256,128]{1,0:T(8,128)(2,1)}, u32[]{:S(2)}) copy-start(bf16[256,128]{1,0:T(8,128)(2,1)} %vi_ref.3) | copy-start | bytes 196612
  3.7 5.7 %collective-permute-start = (bf16[272,128]{1,0:T(8,128)(2,1)S(1)}, bf16[272,128]{1,0:T(8,128)(2,1)S(1)}, u32[]{:S(2)}, u32[]{:S(2)}) collective-permute-start(bf16[272,128]{1,0:T(8,128)(2,1)S(1)} %get-tuple-element.33), channel_id=1, source_target_pairs={{0,1},{1,0},{2,3},{3,2},{4,5},{5,4},{6,7},{7,6},{8,9},{9,8},{10,11... | collective-permute-start | bytes 208904 | tf_op jit(solution)/shard_map/ppermute | solution.py:92
  6.8 7.5 %collective-permute-start.1 = (bf16[272,128]{1,0:T(8,128)(2,1)S(1)}, bf16[272,128]{1,0:T(8,128)(2,1)S(1)}, u32[]{:S(2)}, u32[]{:S(2)}) collective-permute-start(bf16[272,128]{1,0:T(8,128)(2,1)S(1)} %get-tuple-element.34), channel_id=1, source_target_pairs={{0,2},{1,3},{2,0},{3,1},{4,6},{5,7},{6,4},{7,5},{8,10},{9,11},{10,... | collective-permute-start | bytes 208904 | tf_op jit(solution)/shard_map/ppermute | solution.py:92
  9.4 6.2 %collective-permute-start.2 = (bf16[272,128]{1,0:T(8,128)(2,1)S(1)}, bf16[272,128]{1,0:T(8,128)(2,1)S(1)}, u32[]{:S(2)}, u32[]{:S(2)}) collective-permute-start(bf16[272,128]{1,0:T(8,128)(2,1)S(1)} %get-tuple-element.35), channel_id=1, source_target_pairs={{0,3},{1,2},{2,1},{3,0},{4,7},{5,6},{6,5},{7,4},{8,11},{9,10},{10,... | collective-permute-start | bytes 208904 | tf_op jit(solution)/shard_map/ppermute | solution.py:92
  9.4 17.0 %collective-permute-start.3 = (bf16[272,128]{1,0:T(8,128)(2,1)S(1)}, bf16[272,128]{1,0:T(8,128)(2,1)S(1)}, u32[]{:S(2)}, u32[]{:S(2)}) collective-permute-start(bf16[272,128]{1,0:T(8,128)(2,1)S(1)} %collective-permute-done.refs_0_), channel_id=1, source_target_pairs={{0,4},{4,0},{8,12},{12,8},{16,20},{20,16},{24,28},{28,24},{1,5},{5... | collective-permute-start | bytes 208904 | tf_op jit(solution)/shard_map/ppermute | solution.py:95
  14.4 12.1 %collective-permute-start.4 = (bf16[272,128]{1,0:T(8,128)(2,1)S(1)}, bf16[272,128]{1,0:T(8,128)(2,1)S(1)}, u32[]{:S(2)}, u32[]{:S(2)}) collective-permute-start(bf16[272,128]{1,0:T(8,128)(2,1)S(1)} %collective-permute-done.1.refs_1_), channel_id=1, source_target_pairs={{0,4},{4,0},{8,12},{12,8},{16,20},{20,16},{24,28},{28,24},{1,5},{5... | collective-permute-start | bytes 208904 | tf_op jit(solution)/shard_map/ppermute | solution.py:95
  15.6 10.8 %collective-permute-start.5 = (bf16[272,128]{1,0:T(8,128)(2,1)S(1)}, bf16[272,128]{1,0:T(8,128)(2,1)S(1)}, u32[]{:S(2)}, u32[]{:S(2)}) collective-permute-start(bf16[272,128]{1,0:T(8,128)(2,1)S(1)} %collective-permute-done.2.refs_2_), channel_id=1, source_target_pairs={{0,4},{4,0},{8,12},{12,8},{16,20},{20,16},{24,28},{28,24},{1,5},{5... | collective-permute-start | bytes 208904 | tf_op jit(solution)/shard_map/ppermute | solution.py:95
  15.6 0.7 %copy-start.9 = (s32[1,1,16]{2,1,0:T(1,128)S(1)}, s32[1,1,16]{2,1,0:T(1,128)}, u32[]{:S(2)}) copy-start(s32[1,1,16]{2,1,0:T(1,128)} %param.17) | copy-start | bytes 196
  15.6 0.7 %copy-start.10 = (s32[1,1,16]{2,1,0:T(1,128)S(1)}, s32[1,1,16]{2,1,0:T(1,128)}, u32[]{:S(2)}) copy-start(s32[1,1,16]{2,1,0:T(1,128)} %param.18) | copy-start | bytes 196
  15.6 0.7 %copy-start.11 = (s32[1,1,4]{2,1,0:T(1,128)S(1)}, s32[1,1,4]{2,1,0:T(1,128)}, u32[]{:S(2)}) copy-start(s32[1,1,4]{2,1,0:T(1,128)} %param.19) | copy-start | bytes 52
  16.3 0.9 %copy-start.1 = (bf16[1024,128]{1,0:T(8,128)(2,1)S(1)}, bf16[1024,128]{1,0:T(8,128)(2,1)}, u32[]{:S(2)}) copy-start(bf16[1024,128]{1,0:T(8,128)(2,1)} %up_ref.3) | copy-start | bytes 786436
  17.3 0.9 %copy-start.3 = (bf16[1024,128]{1,0:T(8,128)(2,1)S(1)}, bf16[1024,128]{1,0:T(8,128)(2,1)}, u32[]{:S(2)}) copy-start(bf16[1024,128]{1,0:T(8,128)(2,1)} %ux_ref.3) | copy-start | bytes 786436
  18.2 1.0 %copy-start.4 = (bf16[1,1,16,128,128]{4,3,2,1,0:T(8,128)(2,1)S(1)}, bf16[1,1,16,128,128]{4,3,2,1,0:T(8,128)(2,1)}, u32[]{:S(2)}) copy-start(bf16[1,1,16,128,128]{4,3,2,1,0:T(8,128)(2,1)} %param.21) | copy-start | bytes 1572868
  19.3 7.2 %copy-start.2 = (bf16[1024,128]{1,0:T(8,128)(2,1)S(1)}, bf16[1024,128]{1,0:T(8,128)(2,1)}, u32[]{:S(2)}) copy-start(bf16[1024,128]{1,0:T(8,128)(2,1)} %up_ref.3) | copy-start | bytes 786436
  25.5 1.0 %copy-start = (f32[16,128,128]{2,1,0:T(8,128)}, f32[16,128,128]{2,1,0:T(8,128)S(1)}, u32[]{:S(2)}) copy-start(f32[16,128,128]{2,1,0:T(8,128)S(1)} %get-tuple-element.32.w_ref) | copy-start | bytes 3145732
  31.1 1.7 %collective-permute-start.6 = (bf16[1024,128]{1,0:T(8,128)(2,1)S(1)}, bf16[1024,128]{1,0:T(8,128)(2,1)S(1)}, u32[]{:S(2)}, u32[]{:S(2)}) collective-permute-start(bf16[1024,128]{1,0:T(8,128)(2,1)S(1)} %get-tuple-element.38), channel_id=1, source_target_pairs={{0,4},{4,0},{8,12},{12,8},{16,20},{20,16},{24,28},{28,24},{1,5},{5... | collective-permute-start | bytes 786440 | tf_op jit(solution)/shard_map/ppermute | solution.py:95
  33.5 7.5 %collective-permute-start.7 = (bf16[256,128]{1,0:T(8,128)(2,1)S(1)}, bf16[256,128]{1,0:T(8,128)(2,1)S(1)}, u32[]{:S(2)}, u32[]{:S(2)}) collective-permute-start(bf16[256,128]{1,0:T(8,128)(2,1)S(1)} %get-tuple-element.40), channel_id=1, source_target_pairs={{0,8},{4,12},{8,0},{12,4},{16,24},{20,28},{24,16},{28,20},{1,9},{5... | collective-permute-start | bytes 196616 | tf_op jit(solution)/shard_map/ppermute | solution.py:98
  35.0 14.6 %collective-permute-start.10 = (bf16[512,128]{1,0:T(8,128)(2,1)S(1)}, bf16[512,128]{1,0:T(8,128)(2,1)S(1)}, u32[]{:S(2)}, u32[]{:S(2)}) collective-permute-start(bf16[512,128]{1,0:T(8,128)(2,1)S(1)} %get-tuple-element.44), channel_id=1, source_target_pairs={{0,1},{1,0},{2,3},{3,2},{4,5},{5,4},{6,7},{7,6},{8,9},{9,8},{10,11... | collective-permute-start | bytes 393224 | tf_op jit(solution)/shard_map/ppermute | solution.py:92
  35.8 15.3 %collective-permute-start.11 = (bf16[512,128]{1,0:T(8,128)(2,1)S(1)}, bf16[512,128]{1,0:T(8,128)(2,1)S(1)}, u32[]{:S(2)}, u32[]{:S(2)}) collective-permute-start(bf16[512,128]{1,0:T(8,128)(2,1)S(1)} %get-tuple-element.45), channel_id=1, source_target_pairs={{0,2},{1,3},{2,0},{3,1},{4,6},{5,7},{6,4},{7,5},{8,10},{9,11},{10,... | collective-permute-start | bytes 393224 | tf_op jit(solution)/shard_map/ppermute | solution.py:92
  37.9 13.2 %collective-permute-start.12 = (bf16[512,128]{1,0:T(8,128)(2,1)S(1)}, bf16[512,128]{1,0:T(8,128)(2,1)S(1)}, u32[]{:S(2)}, u32[]{:S(2)}) collective-permute-start(bf16[512,128]{1,0:T(8,128)(2,1)S(1)} %get-tuple-element.46), channel_id=1, source_target_pairs={{0,3},{1,2},{2,1},{3,0},{4,7},{5,6},{6,5},{7,4},{8,11},{9,10},{10,... | collective-permute-start | bytes 393224 | tf_op jit(solution)/shard_map/ppermute | solution.py:92
  39.4 5.0 %collective-permute-start.8 = (bf16[256,128]{1,0:T(8,128)(2,1)S(1)}, bf16[256,128]{1,0:T(8,128)(2,1)S(1)}, u32[]{:S(2)}, u32[]{:S(2)}) collective-permute-start(bf16[256,128]{1,0:T(8,128)(2,1)S(1)} %get-tuple-element.41), channel_id=1, source_target_pairs={{0,16},{4,20},{8,24},{12,28},{16,0},{20,4},{24,8},{28,12},{1,17},{... | collective-permute-start | bytes 196616 | tf_op jit(solution)/shard_map/ppermute | solution.py:98
  41.0 5.2 %collective-permute-start.9 = (bf16[256,128]{1,0:T(8,128)(2,1)S(1)}, bf16[256,128]{1,0:T(8,128)(2,1)S(1)}, u32[]{:S(2)}, u32[]{:S(2)}) collective-permute-start(bf16[256,128]{1,0:T(8,128)(2,1)S(1)} %get-tuple-element.42), channel_id=1, source_target_pairs={{0,24},{4,28},{8,16},{12,20},{16,8},{20,12},{24,0},{28,4},{1,25},{... | collective-permute-start | bytes 196616 | tf_op jit(solution)/shard_map/ppermute | solution.py:98
  46.7 4.5 %collective-permute-start.13 = (f32[64,128]{1,0:T(8,128)S(1)}, f32[64,128]{1,0:T(8,128)S(1)}, u32[]{:S(2)}, u32[]{:S(2)}) collective-permute-start(f32[64,128]{1,0:T(8,128)S(1)} %get-tuple-element.47), channel_id=1, source_target_pairs={{0,1},{1,0},{2,3},{3,2},{4,5},{5,4},{6,7},{7,6},{8,9},{9,8},{10,11... | collective-permute-start | bytes 98312 | tf_op jit(solution)/shard_map/ppermute | solution.py:92
  46.8 5.4 %collective-permute-start.14 = (f32[64,128]{1,0:T(8,128)S(1)}, f32[64,128]{1,0:T(8,128)S(1)}, u32[]{:S(2)}, u32[]{:S(2)}) collective-permute-start(f32[64,128]{1,0:T(8,128)S(1)} %get-tuple-element.48), channel_id=1, source_target_pairs={{0,2},{1,3},{2,0},{3,1},{4,6},{5,7},{6,4},{7,5},{8,10},{9,11},{10,... | collective-permute-start | bytes 98312 | tf_op jit(solution)/shard_map/ppermute | solution.py:92
  49.6 5.7 %collective-permute-start.15 = (f32[64,128]{1,0:T(8,128)S(1)}, f32[64,128]{1,0:T(8,128)S(1)}, u32[]{:S(2)}, u32[]{:S(2)}) collective-permute-start(f32[64,128]{1,0:T(8,128)S(1)} %get-tuple-element.49), channel_id=1, source_target_pairs={{0,3},{1,2},{2,1},{3,0},{4,7},{5,6},{6,5},{7,4},{8,11},{9,10},{10,... | collective-permute-start | bytes 98312 | tf_op jit(solution)/shard_map/ppermute | solution.py:92

commit v2 on v1

--- a/solution.py
+++ b/solution.py
@@ -7,10 +7,11 @@
 
 loss_weight = 0.015625
 cores = 2
-vmem_bytes = 48 * 1024 * 1024
+vmem_bytes = 16 * 1024 * 1024
 
 VM = pl.BlockSpec(memory_space=pltpu.VMEM)
 SM = pl.BlockSpec(memory_space=pltpu.SMEM)
+HBM = pl.BlockSpec(memory_space=pltpu.HBM)
 
 
 def dot(first, second, dims):
@@ -40,6 +41,10 @@
         cost_estimate=pl.CostEstimate(flops=cost[0], bytes_accessed=cost[1], transcendentals=cost[2]),
         name=name,
     )(*args)
+
+
+def in_hbm(arrays):
+    return tuple(pltpu.with_memory_space_constraint(x, pltpu.HBM) for x in arrays)
 
 
 def shape(dims, kind):
@@ -79,7 +84,6 @@
     f32 = jnp.float32
     bf16 = jnp.bfloat16
 
-    place = jnp.stack([lax.axis_index("item"), lax.axis_index("user")]).astype(jnp.int32)
     uno_user = uno_user.reshape(-1)
     uno_item = uno_item.reshape(-1)
     obs_user = obs_user.reshape(-1)
@@ -97,10 +101,30 @@
     def chip_peer(x, k):
         return lax.ppermute(x, "user", [(i, i ^ (cores * k)) for i in range(user_ways)])
 
-    def pack(place_ref, uu_ref, ui_ref, vp_ref, vi_ref, *outs):
-        pos = place_ref[0]
-        core = lax.rem(place_ref[1], cores)
+    def pack(uu_hbm, ui_hbm, vp_hbm, vi_hbm, *refs):
+        outs = refs[: peers + 1]
+        uu_ref, ui_ref, sems, ssem = refs[peers + 1 :]
+        pos = lax.axis_index("item")
+        core = lax.rem(lax.axis_index("user"), cores)
         start = pl.multiple_of(core * half, half)
+        lists = [
+            pltpu.make_async_copy(uu_hbm, uu_ref, ssem.at[0]),
+            pltpu.make_async_copy(ui_hbm, ui_ref, ssem.at[1]),
+        ]
+        for c in lists:
+            c.start()
+        copies = []
+        for k in range(peers):
+            for m, ref in enumerate((vp_hbm, vi_hbm)):
+                copies.append(
+                    pltpu.make_async_copy(
+                        ref.at[pl.ds(start, half)], outs[k].at[pl.ds(m * half, half)], sems.at[k, m]
+                    )
+                )
+        for c in copies:
+            c.start()
+        for c in lists:
+            c.wait()
         row = lax.broadcasted_iota(jnp.int32, (pairs, rank), 0)
         for k in range(item_ways):
             group = lax.bitwise_xor(pos, k)
@@ -112,22 +136,26 @@
             if k == 0:
                 outs[peers][...] = count
             else:
-                out = outs[k - 1]
-                out[0:half] = vp_ref[pl.ds(start, half)]
-                out[half : 2 * half] = vi_ref[pl.ds(start, half)]
-                out[2 * half :] = count.astype(bf16)
+                outs[k - 1][2 * half :] = count.astype(bf16)
+        for c in copies:
+            c.wait()
 
     packed = call(
         pack,
         "pack",
         tuple(shape((2 * half + pairs, rank), bf16) for _ in range(peers)) + (shape((pairs, rank), f32),),
-        [SM, SM, SM, VM, VM],
-        (place, uno_user, uno_item, item_pred, item_imp),
+        [HBM, HBM, HBM, HBM],
+        in_hbm((uno_user, uno_item, item_pred, item_imp)),
         (0, 400000, 0),
+        (
+            pltpu.SMEM(uno_user.shape, jnp.int32),
+            pltpu.SMEM(uno_item.shape, jnp.int32),
+            pltpu.SemaphoreType.DMA((peers, 2)),
+            pltpu.SemaphoreType.DMA((2,)),
+        ),
     )
     own_count = packed[peers]
     received = [item_peer(packed[k], k + 1) for k in range(peers)]
-    swapped = [core_peer(x) for x in received]
 
     def observed(logits, imputed, weight, used):
         p = jax.nn.sigmoid(logits)
@@ -138,15 +166,21 @@
         h = (2.0 * term * logits * logits * q * (1.0 - q) * (used * loss_weight)).astype(bf16)
         return g, h
 
-    def local(
-        place_ref, ou_ref, oi_ref, oc_ref, up_ref, ux_ref, vp_ref, vi_ref, lab_ref, prop_ref,
-        utile_ref, itile_ref, uacc_ref, iacc_ref, w_ref,
-    ):
-        pos = place_ref[0]
-        for t in range(obs_all):
-            state = lab_ref[t]
-            inverse = 1.0 / prop_ref[t].astype(f32)
-            w_ref[t] = jnp.where(state == 0, 0.0, jnp.where(state == 2, -inverse, inverse))
+    def local(ou_hbm, oi_hbm, oc_hbm, up_hbm, ux_hbm, vp_hbm, vi_hbm, lab_hbm, prop_hbm, *refs):
+        utile_ref, itile_ref, uacc_ref, iacc_ref, w_ref, one_ref = refs[:6]
+        bufs = refs[6:15]
+        sems = refs[15]
+        ou_ref, oi_ref, oc_ref, up_ref, ux_ref, vp_ref, vi_ref, lab_ref, prop_ref = bufs
+        sources = (ou_hbm, oi_hbm, oc_hbm, up_hbm, ux_hbm, vp_hbm, vi_hbm, lab_hbm, prop_hbm)
+        copies = [pltpu.make_async_copy(a, b, sems.at[n]) for n, (a, b) in enumerate(zip(sources, bufs))]
+        for n in (5, 6, 3, 4, 0, 1, 2, 7, 8):
+            copies[n].start()
+        pos = lax.axis_index("item")
+        one_ref[...] = jnp.ones_like(one_ref)
+        uacc_ref[...] = jnp.zeros_like(uacc_ref)
+        iacc_ref[...] = jnp.zeros_like(iacc_ref)
+        for n in (5, 6, 3, 4):
+            copies[n].wait()
         for u in range(user_blocks):
             urows = pl.ds(u * tile, tile)
             for b in range(item_blocks):
@@ -156,8 +190,12 @@
                 g = ((jax.nn.sigmoid(logits) - jax.nn.sigmoid(imputed)) * loss_weight).astype(bf16)
                 utile_ref[u * item_blocks + b] = plain(g, vp_ref[irows])
                 itile_ref[u * item_blocks + b] = over_rows(g, up_ref[urows])
-        uacc_ref[...] = jnp.zeros_like(uacc_ref)
-        iacc_ref[...] = jnp.zeros_like(iacc_ref)
+        for n in (0, 1, 2, 7, 8):
+            copies[n].wait()
+        for t in range(obs_all):
+            state = lab_ref[t]
+            inverse = 1.0 / prop_ref[t].astype(f32)
+            w_ref[t] = jnp.where(state == 0, 0.0, jnp.where(state == 2, -inverse, inverse))
         for s in range(obs_slots):
             at = pos * obs_slots + s
             urows = pl.ds(pl.multiple_of(ou_ref[at] * tile, tile), tile)
@@ -171,7 +209,8 @@
             iacc_ref[0, irows] += over_rows(g, up_ref[urows])
             iacc_ref[1, irows] += over_rows(h, ux_ref[urows])
 
-    utile, itile, uacc, iacc, weights = call(
+    local_args = (obs_user, obs_item, obs_count, user_pred, user_imp, item_pred, item_imp, labels, propens)
+    utile, itile, uacc, iacc, weights, one = call(
         local,
         "local_tiles",
         (
@@ -180,22 +219,28 @@
             shape((2, user_rows, rank), f32),
             shape((2, shard_rows, rank), f32),
             shape((obs_all, tile, tile), f32),
+            shape((16, rank), bf16),
         ),
-        [SM, SM, SM, SM, VM, VM, VM, VM, VM, VM],
-        (place, obs_user, obs_item, obs_count, user_pred, user_imp, item_pred, item_imp, labels, propens),
+        [HBM] * 9,
+        in_hbm(local_args),
         (4 * pairs * 2 * tile**3, 8000000, 2 * pairs * tile * tile),
-    )
+        tuple(pltpu.SMEM(x.shape, x.dtype) for x in local_args[:3])
+        + tuple(pltpu.VMEM(x.shape, x.dtype) for x in local_args[3:])
+        + (pltpu.SemaphoreType.DMA((9,)),),
+    )
+    swapped = [core_peer(x[: 2 * half] * one[:1]) for x in received]
 
     def remote(
-        place_ref, ou_ref, oi_ref, oc_ref, up_ref, ux_ref, count_ref, utile_ref, itile_ref, uacc_in, iacc_in, w_ref,
-        *refs,
+        ou_ref, oi_ref, oc_ref, up_ref, ux_ref, count_ref, utile_ref, itile_ref, uacc_in, iacc_in, w_ref, *refs
     ):
         recv = refs[:peers]
         swap = refs[peers : 2 * peers]
         outs = refs[2 * peers : 2 * peers + peers + 3]
         vbuf, uacc, iacc = refs[2 * peers + peers + 3 :]
-        pos = place_ref[0]
-        core = lax.rem(place_ref[1], cores)
+        pos = lax.axis_index("item")
+        user = lax.axis_index("user")
+        core = lax.rem(user, cores)
+        chip = lax.div(user, cores)
         mine = pl.multiple_of(core * half, half)
         other = pl.multiple_of((1 - core) * half, half)
         count = count_ref[...]
@@ -244,11 +289,11 @@
                 else:
                     outs[k - 1][m * share : (m + 1) * share] = part.astype(bf16)
         send, keep = outs[peers + 1], outs[peers + 2]
-        for m in range(2):
-            for j in range(item_ways):
-                for q in range(chips):
-                    at = ((m * item_ways + j) * chips + q) * item_share
-                    base = j * shard_rows + q * cores * item_share
+        for q in range(chips):
+            for r in range(item_ways):
+                for m in range(2):
+                    at = ((q * item_ways + r) * 2 + m) * item_share
+                    base = lax.bitwise_xor(pos, r) * shard_rows + lax.bitwise_xor(chip, q) * cores * item_share
                     to_keep = pl.ds(pl.multiple_of(base + core * item_share, item_share), item_share)
                     to_send = pl.ds(pl.multiple_of(base + (1 - core) * item_share, item_share), item_share)
                     keep[at : at + item_share] = iacc[m, to_keep]
@@ -260,9 +305,9 @@
         "remote_tiles",
         tuple(shape((2 * share, rank), bf16) for _ in range(peers))
         + (shape((2 * share, rank), f32), shape((core_rows, rank), bf16), shape((core_rows, rank), f32)),
-        [SM, SM, SM, SM] + [VM] * (8 + 2 * peers),
+        [SM, SM, SM] + [VM] * (8 + 2 * peers),
         (
-            place, obs_user, obs_item, obs_count, user_pred, user_imp, own_count, utile, itile, uacc, iacc, weights,
+            obs_user, obs_item, obs_count, user_pred, user_imp, own_count, utile, itile, uacc, iacc, weights,
             *received, *swapped,
         ),
         (6 * (obs_all - obs_slots) * 2 * tile**3, 8000000, 2 * (obs_all - obs_slots) * tile * tile),
@@ -278,45 +323,38 @@
 
     chip_rows = 2 * item_ways * item_share
 
-    def fold_core(place_ref, keep_ref, recv_ref, *outs):
-        chip = lax.div(place_ref[1], cores)
+    def fold_core(keep_ref, recv_ref, *outs):
         for k in range(chips):
-            peer = lax.bitwise_xor(chip, k)
-            for g in range(2 * item_ways):
-                rows = pl.ds(pl.multiple_of((g * chips + peer) * item_share, item_share), item_share)
-                part = keep_ref[rows] + recv_ref[rows].astype(f32)
-                outs[k][g * item_share : (g + 1) * item_share] = part.astype(outs[k].dtype)
+            rows = pl.ds(k * chip_rows, chip_rows)
+            outs[k][...] = (keep_ref[rows] + recv_ref[rows].astype(f32)).astype(outs[k].dtype)
 
     folded = call(
         fold_core,
         "fold_core",
         (shape((chip_rows, rank), f32),) + tuple(shape((chip_rows, rank), bf16) for _ in range(chips - 1)),
-        [SM, VM, VM],
-        (place, core_keep, core_recv),
-        (0, 1000000, 0),
+        [VM, VM],
+        (core_keep, core_recv),
+        (0, 1000, 0),
     )
     chip_recv = [chip_peer(folded[k], k) for k in range(1, chips)]
 
-    def fold_chips(place_ref, own_ref, *refs):
+    def fold_chips(own_ref, *refs):
         recv = refs[: chips - 1]
         outs = refs[chips - 1 :]
-        pos = place_ref[0]
         for k in range(item_ways):
-            peer = lax.bitwise_xor(pos, k)
-            for m in range(2):
-                rows = pl.ds(pl.multiple_of((m * item_ways + peer) * item_share, item_share), item_share)
-                part = own_ref[rows]
-                for r in recv:
-                    part = part + r[rows].astype(f32)
-                outs[k][m * item_share : (m + 1) * item_share] = part
+            rows = pl.ds(k * 2 * item_share, 2 * item_share)
+            part = own_ref[rows]
+            for r in recv:
+                part = part + r[rows].astype(f32)
+            outs[k][...] = part
 
     shares = call(
         fold_chips,
         "fold_chips",
         tuple(shape((2 * item_share, rank), f32) for _ in range(item_ways)),
-        [SM, VM] + [VM] * (chips - 1),
-        (place, folded[0], *chip_recv),
-        (0, 300000, 0),
+        [VM] * chips,
+        (folded[0], *chip_recv),
+        (0, 1000, 0),
     )
     item_recv = [item_peer(shares[k], k) for k in range(1, item_ways)]
 

time: 56.5 us -> 45.4 us (0.80)
  local copies, waits for them, and re-layouts: 6.94 us -> 0.68 us
  waiting for transfers between devices: 16.3 us -> 13 us
  Pallas kernels: 13.4 us -> 11.8 us
    unnamed x28 -> x10, local copies, waits for them, and re-layouts: 6.94 us -> 0.68 us
    ppermute x9, waiting for transfers between devices: 10.4 us -> 5.6 us  [item_peer(): return lax.ppermute(x, 'item', [(i, i ^ k) for i in range(item_ways)])]
    pallas_call x6, Pallas kernels: 13.4 us -> 11.8 us  [call(): pl.pallas_call(body, out_shape=out_shapes, in_specs=specs, out_specs=tupl...]
    ppermute x4, waiting for transfers between devices: 1.17 us -> 2.55 us  [core_peer(): return lax.ppermute(x, 'user', [(i, i ^ 1) for i in range(user_ways)])]
  transfers between devices with their start and end apart: 16 -> 16, of which waited for: 7 -> 9; matrix products, arithmetic and copies ran while one was open for 0% -> 0% of each run, Pallas kernels for 12% -> 13%
where the time goes in v2:
time: 45.4 us; the launch traced here: 45.2 us
  starting transfers between devices  18.9 us (42%)
  waiting for transfers between devices  13 us (29%)
  Pallas kernels  11.8 us (26%)
  between operations  0.74 us (2%)
  local copies, waits for them, and re-layouts  0.68 us (1%)
    ppermute x9, starting transfers between devices, item_peer(): return lax.ppermute(x, 'item', [(i, i ^ k) for i in range(item_ways)])  14.5 us
    pallas_call x6, Pallas kernels, call(): pl.pallas_call(body, out_shape=out_shapes, in_specs=specs, out_specs=tupl...  11.8 us
    ppermute x9, waiting for transfers between devices, item_peer(): return lax.ppermute(x, 'item', [(i, i ^ k) for i in range(item_ways)])  5.6 us
    ppermute x3, waiting for transfers between devices, chip_peer(): lax.ppermute(x, 'user', [(i, i ^ cores * k) for i in range(user_ways)])  4.82 us
    ppermute x3, starting transfers between devices, chip_peer(): lax.ppermute(x, 'user', [(i, i ^ cores * k) for i in range(user_ways)])  3.55 us
    ppermute x4, waiting for transfers between devices, core_peer(): return lax.ppermute(x, 'user', [(i, i ^ 1) for i in range(user_ways)])  2.55 us
  transfers between devices with their start and end apart: 16, of which 9 were waited for; matrix products, arithmetic and copies ran while one was open for 0% of the time, Pallas kernels for 13%

profile of v2, /device:TPU:0, one launch (start us, length us, event | category | flops | bytes accessed | tf_op | source)
XLA Modules:
  0.0 45.2 jit_solution(15797483343785547529)
XLA Ops:
  0.6 1.0 %pack.1 = (bf16[272,128]{1,0:T(8,128)(2,1)S(1)}, bf16[272,128]{1,0:T(8,128)(2,1)S(1)}, bf16[272,128]{1,0:T(8,128)(2,1)S(1)}, f32[16,128]{1,0:T(8,128)S(1)}) custom-call(s32[64]{0:T(128)} %bitcast.17, s32[64]{0:T(128)} %bitcast.18, bf16[256,128]{1,0:T(8,128)(2,1)} %vp_hbm.3, bf16[256,128]{1,0:T(8,128)(2,1)} %vi_hbm.3), custom_call_target="tpu_custom_call" | custom-call | bytes 400000 | tf_op jit(solution)/shard_map/pack/pallas_call | solution.py:34
  1.6 3.1 %collective-permute-start = (bf16[272,128]{1,0:T(8,128)(2,1)S(1)}, bf16[272,128]{1,0:T(8,128)(2,1)S(1)}, u32[]{:S(2)}, u32[]{:S(2)}) collective-permute-start(bf16[272,128]{1,0:T(8,128)(2,1)S(1)} %get-tuple-element.34), channel_id=1, source_target_pairs={{0,1},{1,0},{2,3},{3,2},{4,5},{5,4},{6,7},{7,6},{8,9},{9,8},{10,11... | collective-permute-start | bytes 208904 | tf_op jit(solution)/shard_map/ppermute | solution.py:96
  4.7 2.6 %collective-permute-start.1 = (bf16[272,128]{1,0:T(8,128)(2,1)S(1)}, bf16[272,128]{1,0:T(8,128)(2,1)S(1)}, u32[]{:S(2)}, u32[]{:S(2)}) collective-permute-start(bf16[272,128]{1,0:T(8,128)(2,1)S(1)} %get-tuple-element.35), channel_id=1, source_target_pairs={{0,2},{1,3},{2,0},{3,1},{4,6},{5,7},{6,4},{7,5},{8,10},{9,11},{10,... | collective-permute-start | bytes 208904 | tf_op jit(solution)/shard_map/ppermute | solution.py:96
  7.3 0.0 collective-permute-start.2
  7.3 0.0 copy-start.1
  7.3 6.1 %local_tiles.1 = (f32[16,128,128]{2,1,0:T(8,128)S(1)}, f32[16,128,128]{2,1,0:T(8,128)S(1)}, f32[2,1024,128]{2,1,0:T(8,128)S(1)}, f32[2,256,128]{2,1,0:T(8,128)S(...) custom-call(s32[16]{0:T(128)} %bitcast.9, s32[16]{0:T(128)} %bitcast.11, s32[4]{0:T(128)} %bitcast.13, ...), custom_call_target="tpu_custom_call" | custom-call | flops 268435456 | bytes 8000000 | tf_op jit(solution)/shard_map/local_tiles/pallas_call | solution.py:34
  13.3 0.0 copy-start
  13.4 0.0 collective-permute-done.refs_0_
  13.4 0.0 collective-permute-done.1.refs_1_
  13.4 0.1 collective-permute-done.2.refs_2_
  13.5 0.1 collective-permute-start.5
  13.6 0.5 %collective-permute-start.4 = (bf16[256,128]{1,0:T(8,128)(2,1)S(1)}, bf16[256,128]{1,0:T(8,128)(2,1)S(1)}, u32[]{:S(2)}, u32[]{:S(2)}) collective-permute-start(bf16[256,128]{1,0:T(8,128)(2,1)S(1)} %get-tuple-element.53), channel_id=1, source_target_pairs={{0,4},{4,0},{8,12},{12,8},{16,20},{20,16},{24,28},{28,24},{1,5},{5... | collective-permute-start | bytes 196616 | tf_op jit(solution)/shard_map/ppermute | solution.py:99
  14.1 0.1 collective-permute-start.3
  14.2 0.7 %collective-permute-done.5.refs_5_ = bf16[256,128]{1,0:T(8,128)(2,1)S(1)} collective-permute-done((bf16[256,128]{1,0:T(8,128)(2,1)S(1)}, bf16[256,128]{1,0:T(8,128)(2,1)S(1)}, u32[]{:S(2)}, u32[]{:S(2)}) %collective-permute-start.5) | collective-permute-done | bytes 65568 | tf_op jit(solution)/shard_map/ppermute | solution.py:99
  14.8 0.2 collective-permute-done.4.refs_4_
  15.0 0.4 collective-permute-done.3.refs_3_
  15.3 0.0 copy-start.2
  15.3 0.0 copy-start.3
  15.3 0.0 copy-start.4
  15.3 0.0 copy-done.1
  15.4 0.0 copy-done
  15.4 0.6 %copy-done.2 = s32[1,1,16]{2,1,0:T(1,128)S(1)} copy-done((s32[1,1,16]{2,1,0:T(1,128)S(1)}, s32[1,1,16]{2,1,0:T(1,128)}, u32[]{:S(2)}) %copy-start.2) | copy-done | bytes 88
  16.0 0.0 copy-done.3
  16.0 0.0 copy-done.4
  16.0 4.0 %remote_tiles.1 = (bf16[512,128]{1,0:T(8,128)(2,1)S(1)}, bf16[512,128]{1,0:T(8,128)(2,1)S(1)}, bf16[512,128]{1,0:T(8,128)(2,1)S(1)}, f32[512,128]{1,0:T(8,128)S(...) custom-call(s32[16]{0:T(128)S(1)} %bitcast.10, s32[16]{0:T(128)S(1)} %bitcast.12, s32[4]{0:T(128)S(1)} %bitcast.14, ...), custom_call_target="tpu_custom_call" | custom-call | flops 301989888 | bytes 8000000 | tf_op jit(solution)/shard_map/remote_tiles/pallas_call | solution.py:34
  20.0 0.2 collective-permute-start.6
  20.2 1.4 %collective-permute-done.6.recv_ref = bf16[1024,128]{1,0:T(8,128)(2,1)S(1)} collective-permute-done((bf16[1024,128]{1,0:T(8,128)(2,1)S(1)}, bf16[1024,128]{1,0:T(8,128)(2,1)S(1)}, u32[]{:S(2)}, u32[]{:S(2)}) %collective-permute-start.6) | collective-permute-done | bytes 262176 | tf_op jit(solution)/shard_map/ppermute | solution.py:99
  21.7 1.7 %collective-permute-start.7 = (bf16[256,128]{1,0:T(8,128)(2,1)S(1)}, bf16[256,128]{1,0:T(8,128)(2,1)S(1)}, u32[]{:S(2)}, u32[]{:S(2)}) collective-permute-start(bf16[256,128]{1,0:T(8,128)(2,1)S(1)} %get-tuple-element.42), channel_id=1, source_target_pairs={{0,8},{4,12},{8,0},{12,4},{16,24},{20,28},{24,16},{28,20},{1,9},{5... | collective-permute-start | bytes 196616 | tf_op jit(solution)/shard_map/ppermute | solution.py:102
  23.4 0.7 %collective-permute-start.10 = (bf16[512,128]{1,0:T(8,128)(2,1)S(1)}, bf16[512,128]{1,0:T(8,128)(2,1)S(1)}, u32[]{:S(2)}, u32[]{:S(2)}) collective-permute-start(bf16[512,128]{1,0:T(8,128)(2,1)S(1)} %get-tuple-element.46), channel_id=1, source_target_pairs={{0,1},{1,0},{2,3},{3,2},{4,5},{5,4},{6,7},{7,6},{8,9},{9,8},{10,11... | collective-permute-start | bytes 393224 | tf_op jit(solution)/shard_map/ppermute | solution.py:96
  24.0 3.5 %collective-permute-start.11 = (bf16[512,128]{1,0:T(8,128)(2,1)S(1)}, bf16[512,128]{1,0:T(8,128)(2,1)S(1)}, u32[]{:S(2)}, u32[]{:S(2)}) collective-permute-start(bf16[512,128]{1,0:T(8,128)(2,1)S(1)} %get-tuple-element.47), channel_id=1, source_target_pairs={{0,2},{1,3},{2,0},{3,1},{4,6},{5,7},{6,4},{7,5},{8,10},{9,11},{10,... | collective-permute-start | bytes 393224 | tf_op jit(solution)/shard_map/ppermute | solution.py:96
  27.5 0.2 collective-permute-start.12
  27.7 1.5 %collective-permute-start.8 = (bf16[256,128]{1,0:T(8,128)(2,1)S(1)}, bf16[256,128]{1,0:T(8,128)(2,1)S(1)}, u32[]{:S(2)}, u32[]{:S(2)}) collective-permute-start(bf16[256,128]{1,0:T(8,128)(2,1)S(1)} %get-tuple-element.43), channel_id=1, source_target_pairs={{0,16},{4,20},{8,24},{12,28},{16,0},{20,4},{24,8},{28,12},{1,17},{... | collective-permute-start | bytes 196616 | tf_op jit(solution)/shard_map/ppermute | solution.py:102
  29.3 0.0 collective-permute-done.7.refs_0_
  29.3 0.3 collective-permute-start.9
  29.6 3.1 %collective-permute-done.8.refs_1_ = bf16[256,128]{1,0:T(8,128)(2,1)S(1)} collective-permute-done((bf16[256,128]{1,0:T(8,128)(2,1)S(1)}, bf16[256,128]{1,0:T(8,128)(2,1)S(1)}, u32[]{:S(2)}, u32[]{:S(2)}) %collective-permute-start.8) | collective-permute-done | bytes 65568 | tf_op jit(solution)/shard_map/ppermute | solution.py:102
  32.7 1.7 %collective-permute-done.9.refs_2_ = bf16[256,128]{1,0:T(8,128)(2,1)S(1)} collective-permute-done((bf16[256,128]{1,0:T(8,128)(2,1)S(1)}, bf16[256,128]{1,0:T(8,128)(2,1)S(1)}, u32[]{:S(2)}, u32[]{:S(2)}) %collective-permute-start.9) | collective-permute-done | bytes 65568 | tf_op jit(solution)/shard_map/ppermute | solution.py:102
  34.5 0.4 collective-permute-start.13
  34.9 3.8 %collective-permute-start.14 = (f32[64,128]{1,0:T(8,128)S(1)}, f32[64,128]{1,0:T(8,128)S(1)}, u32[]{:S(2)}, u32[]{:S(2)}) collective-permute-start(f32[64,128]{1,0:T(8,128)S(1)} %get-tuple-element.50), channel_id=1, source_target_pairs={{0,2},{1,3},{2,0},{3,1},{4,6},{5,7},{6,4},{7,5},{8,10},{9,11},{10,... | collective-permute-start | bytes 98312 | tf_op jit(solution)/shard_map/ppermute | solution.py:96
  38.7 0.0 collective-permute-done.10.refs_0_
  38.7 0.2 collective-permute-start.15
  38.9 0.0 collective-permute-done.11.refs_1_
  38.9 0.0 collective-permute-done.12.refs_2_
  38.9 0.0 collective-permute-done.13.refs_3_
  38.9 2.4 %collective-permute-done.14.refs_4_ = f32[64,128]{1,0:T(8,128)S(1)} collective-permute-done((f32[64,128]{1,0:T(8,128)S(1)}, f32[64,128]{1,0:T(8,128)S(1)}, u32[]{:S(2)}, u32[]{:S(2)}) %collective-permute-start.14) | collective-permute-done | bytes 32800 | tf_op jit(solution)/shard_map/ppermute | solution.py:96
  41.4 3.0 %collective-permute-done.15.refs_5_ = f32[64,128]{1,0:T(8,128)S(1)} collective-permute-done((f32[64,128]{1,0:T(8,128)S(1)}, f32[64,128]{1,0:T(8,128)S(1)}, u32[]{:S(2)}, u32[]{:S(2)}) %collective-permute-start.15) | collective-permute-done | bytes 32800 | tf_op jit(solution)/shard_map/ppermute | solution.py:96
  44.4 0.7 %finish.1 = (f32[256,128]{1,0:T(8,128)}, f32[256,128]{1,0:T(8,128)}, f32[32,128]{1,0:T(8,128)}, f32[32,128]{1,0:T(8,128)}) custom-call(f32[512,128]{1,0:T(8,128)S(1)} %get-tuple-element.38.user_ref, f32[64,128]{1,0:T(8,128)S(1)} %get-tuple-element.45.item_ref, bf16[512,128]{1,0:T(8,128)(2,1)S(1)} %collective-permute-done.10.refs_0_, ...), custom_call_target="tpu_custom_call" | custom-call | bytes 1000000 | tf_op jit(solution)/shard_map/finish/pallas_call | solution.py:34
  (4 shorter events, 0.1 us)
Async XLA Ops:
  1.6 11.8 %collective-permute-start = (bf16[272,128]{1,0:T(8,128)(2,1)S(1)}, bf16[272,128]{1,0:T(8,128)(2,1)S(1)}, u32[]{:S(2)}, u32[]{:S(2)}) collective-permute-start(bf16[272,128]{1,0:T(8,128)(2,1)S(1)} %get-tuple-element.34), channel_id=1, source_target_pairs={{0,1},{1,0},{2,3},{3,2},{4,5},{5,4},{6,7},{7,6},{8,9},{9,8},{10,11... | collective-permute-start | bytes 208904 | tf_op jit(solution)/shard_map/ppermute | solution.py:96
  4.7 8.7 %collective-permute-start.1 = (bf16[272,128]{1,0:T(8,128)(2,1)S(1)}, bf16[272,128]{1,0:T(8,128)(2,1)S(1)}, u32[]{:S(2)}, u32[]{:S(2)}) collective-permute-start(bf16[272,128]{1,0:T(8,128)(2,1)S(1)} %get-tuple-element.35), channel_id=1, source_target_pairs={{0,2},{1,3},{2,0},{3,1},{4,6},{5,7},{6,4},{7,5},{8,10},{9,11},{10,... | collective-permute-start | bytes 208904 | tf_op jit(solution)/shard_map/ppermute | solution.py:96
  7.3 6.2 %collective-permute-start.2 = (bf16[272,128]{1,0:T(8,128)(2,1)S(1)}, bf16[272,128]{1,0:T(8,128)(2,1)S(1)}, u32[]{:S(2)}, u32[]{:S(2)}) collective-permute-start(bf16[272,128]{1,0:T(8,128)(2,1)S(1)} %get-tuple-element.36), channel_id=1, source_target_pairs={{0,3},{1,2},{2,1},{3,0},{4,7},{5,6},{6,5},{7,4},{8,11},{9,10},{10,... | collective-permute-start | bytes 208904 | tf_op jit(solution)/shard_map/ppermute | solution.py:96
  7.3 8.1 %copy-start.1 = (bf16[1024,128]{1,0:T(8,128)(2,1)S(1)}, bf16[1024,128]{1,0:T(8,128)(2,1)}, u32[]{:S(2)}) copy-start(bf16[1024,128]{1,0:T(8,128)(2,1)} %ux_ref.1) | copy-start | bytes 786436
  13.3 2.0 %copy-start = (bf16[1024,128]{1,0:T(8,128)(2,1)S(1)}, bf16[1024,128]{1,0:T(8,128)(2,1)}, u32[]{:S(2)}) copy-start(bf16[1024,128]{1,0:T(8,128)(2,1)} %up_ref.1) | copy-start | bytes 786436
  13.5 1.3 %collective-permute-start.5 = (bf16[256,128]{1,0:T(8,128)(2,1)S(1)}, bf16[256,128]{1,0:T(8,128)(2,1)S(1)}, u32[]{:S(2)}, u32[]{:S(2)}) collective-permute-start(bf16[256,128]{1,0:T(8,128)(2,1)S(1)} %get-tuple-element.52), channel_id=1, source_target_pairs={{0,4},{4,0},{8,12},{12,8},{16,20},{20,16},{24,28},{28,24},{1,5},{5... | collective-permute-start | bytes 196616 | tf_op jit(solution)/shard_map/ppermute | solution.py:99
  13.6 1.4 %collective-permute-start.4 = (bf16[256,128]{1,0:T(8,128)(2,1)S(1)}, bf16[256,128]{1,0:T(8,128)(2,1)S(1)}, u32[]{:S(2)}, u32[]{:S(2)}) collective-permute-start(bf16[256,128]{1,0:T(8,128)(2,1)S(1)} %get-tuple-element.53), channel_id=1, source_target_pairs={{0,4},{4,0},{8,12},{12,8},{16,20},{20,16},{24,28},{28,24},{1,5},{5... | collective-permute-start | bytes 196616 | tf_op jit(solution)/shard_map/ppermute | solution.py:99
  14.1 1.3 %collective-permute-start.3 = (bf16[256,128]{1,0:T(8,128)(2,1)S(1)}, bf16[256,128]{1,0:T(8,128)(2,1)S(1)}, u32[]{:S(2)}, u32[]{:S(2)}) collective-permute-start(bf16[256,128]{1,0:T(8,128)(2,1)S(1)} %get-tuple-element.54), channel_id=1, source_target_pairs={{0,4},{4,0},{8,12},{12,8},{16,20},{20,16},{24,28},{28,24},{1,5},{5... | collective-permute-start | bytes 196616 | tf_op jit(solution)/shard_map/ppermute | solution.py:99
  15.3 0.7 %copy-start.2 = (s32[1,1,16]{2,1,0:T(1,128)S(1)}, s32[1,1,16]{2,1,0:T(1,128)}, u32[]{:S(2)}) copy-start(s32[1,1,16]{2,1,0:T(1,128)} %param.17) | copy-start | bytes 196
  15.3 0.7 %copy-start.3 = (s32[1,1,16]{2,1,0:T(1,128)S(1)}, s32[1,1,16]{2,1,0:T(1,128)}, u32[]{:S(2)}) copy-start(s32[1,1,16]{2,1,0:T(1,128)} %param.18) | copy-start | bytes 196
  15.3 0.7 %copy-start.4 = (s32[1,1,4]{2,1,0:T(1,128)S(1)}, s32[1,1,4]{2,1,0:T(1,128)}, u32[]{:S(2)}) copy-start(s32[1,1,4]{2,1,0:T(1,128)} %param.19) | copy-start | bytes 52
  20.0 1.6 %collective-permute-start.6 = (bf16[1024,128]{1,0:T(8,128)(2,1)S(1)}, bf16[1024,128]{1,0:T(8,128)(2,1)S(1)}, u32[]{:S(2)}, u32[]{:S(2)}) collective-permute-start(bf16[1024,128]{1,0:T(8,128)(2,1)S(1)} %get-tuple-element.40), channel_id=1, source_target_pairs={{0,4},{4,0},{8,12},{12,8},{16,20},{20,16},{24,28},{28,24},{1,5},{5... | collective-permute-start | bytes 786440 | tf_op jit(solution)/shard_map/ppermute | solution.py:99
  21.7 7.6 %collective-permute-start.7 = (bf16[256,128]{1,0:T(8,128)(2,1)S(1)}, bf16[256,128]{1,0:T(8,128)(2,1)S(1)}, u32[]{:S(2)}, u32[]{:S(2)}) collective-permute-start(bf16[256,128]{1,0:T(8,128)(2,1)S(1)} %get-tuple-element.42), channel_id=1, source_target_pairs={{0,8},{4,12},{8,0},{12,4},{16,24},{20,28},{24,16},{28,20},{1,9},{5... | collective-permute-start | bytes 196616 | tf_op jit(solution)/shard_map/ppermute | solution.py:102
  23.4 15.3 %collective-permute-start.10 = (bf16[512,128]{1,0:T(8,128)(2,1)S(1)}, bf16[512,128]{1,0:T(8,128)(2,1)S(1)}, u32[]{:S(2)}, u32[]{:S(2)}) collective-permute-start(bf16[512,128]{1,0:T(8,128)(2,1)S(1)} %get-tuple-element.46), channel_id=1, source_target_pairs={{0,1},{1,0},{2,3},{3,2},{4,5},{5,4},{6,7},{7,6},{8,9},{9,8},{10,11... | collective-permute-start | bytes 393224 | tf_op jit(solution)/shard_map/ppermute | solution.py:96
  24.0 14.9 %collective-permute-start.11 = (bf16[512,128]{1,0:T(8,128)(2,1)S(1)}, bf16[512,128]{1,0:T(8,128)(2,1)S(1)}, u32[]{:S(2)}, u32[]{:S(2)}) collective-permute-start(bf16[512,128]{1,0:T(8,128)(2,1)S(1)} %get-tuple-element.47), channel_id=1, source_target_pairs={{0,2},{1,3},{2,0},{3,1},{4,6},{5,7},{6,4},{7,5},{8,10},{9,11},{10,... | collective-permute-start | bytes 393224 | tf_op jit(solution)/shard_map/ppermute | solution.py:96
  27.5 11.4 %collective-permute-start.12 = (bf16[512,128]{1,0:T(8,128)(2,1)S(1)}, bf16[512,128]{1,0:T(8,128)(2,1)S(1)}, u32[]{:S(2)}, u32[]{:S(2)}) collective-permute-start(bf16[512,128]{1,0:T(8,128)(2,1)S(1)} %get-tuple-element.48), channel_id=1, source_target_pairs={{0,3},{1,2},{2,1},{3,0},{4,7},{5,6},{6,5},{7,4},{8,11},{9,10},{10,... | collective-permute-start | bytes 393224 | tf_op jit(solution)/shard_map/ppermute | solution.py:96
  27.7 5.0 %collective-permute-start.8 = (bf16[256,128]{1,0:T(8,128)(2,1)S(1)}, bf16[256,128]{1,0:T(8,128)(2,1)S(1)}, u32[]{:S(2)}, u32[]{:S(2)}) collective-permute-start(bf16[256,128]{1,0:T(8,128)(2,1)S(1)} %get-tuple-element.43), channel_id=1, source_target_pairs={{0,16},{4,20},{8,24},{12,28},{16,0},{20,4},{24,8},{28,12},{1,17},{... | collective-permute-start | bytes 196616 | tf_op jit(solution)/shard_map/ppermute | solution.py:102
  29.3 5.2 %collective-permute-start.9 = (bf16[256,128]{1,0:T(8,128)(2,1)S(1)}, bf16[256,128]{1,0:T(8,128)(2,1)S(1)}, u32[]{:S(2)}, u32[]{:S(2)}) collective-permute-start(bf16[256,128]{1,0:T(8,128)(2,1)S(1)} %get-tuple-element.44), channel_id=1, source_target_pairs={{0,24},{4,28},{8,16},{12,20},{16,8},{20,12},{24,0},{28,4},{1,25},{... | collective-permute-start | bytes 196616 | tf_op jit(solution)/shard_map/ppermute | solution.py:102
  34.5 4.5 %collective-permute-start.13 = (f32[64,128]{1,0:T(8,128)S(1)}, f32[64,128]{1,0:T(8,128)S(1)}, u32[]{:S(2)}, u32[]{:S(2)}) collective-permute-start(f32[64,128]{1,0:T(8,128)S(1)} %get-tuple-element.49), channel_id=1, source_target_pairs={{0,1},{1,0},{2,3},{3,2},{4,5},{5,4},{6,7},{7,6},{8,9},{9,8},{10,11... | collective-permute-start | bytes 98312 | tf_op jit(solution)/shard_map/ppermute | solution.py:96
  34.9 6.5 %collective-permute-start.14 = (f32[64,128]{1,0:T(8,128)S(1)}, f32[64,128]{1,0:T(8,128)S(1)}, u32[]{:S(2)}, u32[]{:S(2)}) collective-permute-start(f32[64,128]{1,0:T(8,128)S(1)} %get-tuple-element.50), channel_id=1, source_target_pairs={{0,2},{1,3},{2,0},{3,1},{4,6},{5,7},{6,4},{7,5},{8,10},{9,11},{10,... | collective-permute-start | bytes 98312 | tf_op jit(solution)/shard_map/ppermute | solution.py:96
  38.7 5.7 %collective-permute-start.15 = (f32[64,128]{1,0:T(8,128)S(1)}, f32[64,128]{1,0:T(8,128)S(1)}, u32[]{:S(2)}, u32[]{:S(2)}) collective-permute-start(f32[64,128]{1,0:T(8,128)S(1)} %get-tuple-element.51), channel_id=1, source_target_pairs={{0,3},{1,2},{2,1},{3,0},{4,7},{5,6},{6,5},{7,4},{8,11},{9,10},{10,... | collective-permute-start | bytes 98312 | tf_op jit(solution)/shard_map/ppermute | solution.py:96

commit v3 on v2

--- a/solution.py
+++ b/solution.py
@@ -167,16 +167,18 @@
         return g, h
 
     def local(ou_hbm, oi_hbm, oc_hbm, up_hbm, ux_hbm, vp_hbm, vi_hbm, lab_hbm, prop_hbm, *refs):
-        utile_ref, itile_ref, uacc_ref, iacc_ref, w_ref, one_ref = refs[:6]
-        bufs = refs[6:15]
-        sems = refs[15]
+        utile_ref, itile_ref, uacc_ref, iacc_ref, w_ref = refs[:5]
+        ones = refs[5 : 5 + peers]
+        bufs = refs[5 + peers : 14 + peers]
+        sems, gbuf, hbuf = refs[14 + peers :]
         ou_ref, oi_ref, oc_ref, up_ref, ux_ref, vp_ref, vi_ref, lab_ref, prop_ref = bufs
         sources = (ou_hbm, oi_hbm, oc_hbm, up_hbm, ux_hbm, vp_hbm, vi_hbm, lab_hbm, prop_hbm)
         copies = [pltpu.make_async_copy(a, b, sems.at[n]) for n, (a, b) in enumerate(zip(sources, bufs))]
         for n in (5, 6, 3, 4, 0, 1, 2, 7, 8):
             copies[n].start()
         pos = lax.axis_index("item")
-        one_ref[...] = jnp.ones_like(one_ref)
+        for ref in ones:
+            ref[...] = jnp.ones_like(ref)
         uacc_ref[...] = jnp.zeros_like(uacc_ref)
         iacc_ref[...] = jnp.zeros_like(iacc_ref)
         for n in (5, 6, 3, 4):
@@ -187,30 +189,39 @@
                 irows = pl.ds(b * tile, tile)
                 logits = rows_by_cols(up_ref[urows], vp_ref[irows])
                 imputed = rows_by_cols(ux_ref[urows], vi_ref[irows])
-                g = ((jax.nn.sigmoid(logits) - jax.nn.sigmoid(imputed)) * loss_weight).astype(bf16)
-                utile_ref[u * item_blocks + b] = plain(g, vp_ref[irows])
-                itile_ref[u * item_blocks + b] = over_rows(g, up_ref[urows])
+                gbuf[u * item_blocks + b] = (
+                    (jax.nn.sigmoid(logits) - jax.nn.sigmoid(imputed)) * loss_weight
+                ).astype(bf16)
         for n in (0, 1, 2, 7, 8):
             copies[n].wait()
         for t in range(obs_all):
             state = lab_ref[t]
             inverse = 1.0 / prop_ref[t].astype(f32)
             w_ref[t] = jnp.where(state == 0, 0.0, jnp.where(state == 2, -inverse, inverse))
+        places = []
         for s in range(obs_slots):
             at = pos * obs_slots + s
             urows = pl.ds(pl.multiple_of(ou_ref[at] * tile, tile), tile)
             irows = pl.ds(pl.multiple_of(oi_ref[at] * tile, tile), tile)
+            places.append((urows, irows))
             used = jnp.where(s < oc_ref[pos], 1.0, 0.0)
             logits = rows_by_cols(up_ref[urows], vp_ref[irows])
             imputed = rows_by_cols(ux_ref[urows], vi_ref[irows])
-            g, h = observed(logits, imputed, w_ref[at], used)
-            uacc_ref[0, urows] += plain(g, vp_ref[irows])
-            uacc_ref[1, urows] += plain(h, vi_ref[irows])
-            iacc_ref[0, irows] += over_rows(g, up_ref[urows])
-            iacc_ref[1, irows] += over_rows(h, ux_ref[urows])
+            gbuf[pairs + s], hbuf[s] = observed(logits, imputed, w_ref[at], used)
+        for u in range(user_blocks):
+            urows = pl.ds(u * tile, tile)
+            for b in range(item_blocks):
+                t = u * item_blocks + b
+                utile_ref[t] = plain(gbuf[t], vp_ref[b * tile : (b + 1) * tile])
+                itile_ref[t] = over_rows(gbuf[t], up_ref[urows])
+        for s, (urows, irows) in enumerate(places):
+            uacc_ref[0, urows] += plain(gbuf[pairs + s], vp_ref[irows])
+            uacc_ref[1, urows] += plain(hbuf[s], vi_ref[irows])
+            iacc_ref[0, irows] += over_rows(gbuf[pairs + s], up_ref[urows])
+            iacc_ref[1, irows] += over_rows(hbuf[s], ux_ref[urows])
 
     local_args = (obs_user, obs_item, obs_count, user_pred, user_imp, item_pred, item_imp, labels, propens)
-    utile, itile, uacc, iacc, weights, one = call(
+    utile, itile, uacc, iacc, weights, *ones = call(
         local,
         "local_tiles",
         (
@@ -219,24 +230,35 @@
             shape((2, user_rows, rank), f32),
             shape((2, shard_rows, rank), f32),
             shape((obs_all, tile, tile), f32),
-            shape((16, rank), bf16),
+            *(shape((16, rank), bf16) for _ in range(peers)),
         ),
         [HBM] * 9,
         in_hbm(local_args),
         (4 * pairs * 2 * tile**3, 8000000, 2 * pairs * tile * tile),
         tuple(pltpu.SMEM(x.shape, x.dtype) for x in local_args[:3])
         + tuple(pltpu.VMEM(x.shape, x.dtype) for x in local_args[3:])
-        + (pltpu.SemaphoreType.DMA((9,)),),
-    )
-    swapped = [core_peer(x[: 2 * half] * one[:1]) for x in received]
-
-    def remote(
-        ou_ref, oi_ref, oc_ref, up_ref, ux_ref, count_ref, utile_ref, itile_ref, uacc_in, iacc_in, w_ref, *refs
-    ):
+        + (
+            pltpu.SemaphoreType.DMA((9,)),
+            pltpu.VMEM((pairs + obs_slots, tile, tile), bf16),
+            pltpu.VMEM((obs_slots, tile, tile), bf16),
+        ),
+    )
+    swapped = [core_peer(x[: 2 * half] * one[:1]) for x, one in zip(received, ones)]
+
+    slots = peers * obs_slots
+
+    def items(ou_hbm, oi_hbm, oc_hbm, up_ref, ux_ref, count_ref, itile_ref, iacc_in, w_ref, *refs):
         recv = refs[:peers]
         swap = refs[peers : 2 * peers]
-        outs = refs[2 * peers : 2 * peers + peers + 3]
-        vbuf, uacc, iacc = refs[2 * peers + peers + 3 :]
+        send, keep, vbuf, gbuf, hbuf, total_ref = refs[2 * peers : 2 * peers + 6]
+        ou_ref, oi_ref, oc_ref, sems, iacc = refs[2 * peers + 6 :]
+        copies = [
+            pltpu.make_async_copy(ou_hbm, ou_ref, sems.at[0]),
+            pltpu.make_async_copy(oi_hbm, oi_ref, sems.at[1]),
+            pltpu.make_async_copy(oc_hbm, oc_ref, sems.at[2]),
+        ]
+        for c in copies:
+            c.start()
         pos = lax.axis_index("item")
         user = lax.axis_index("user")
         core = lax.rem(user, cores)
@@ -249,6 +271,7 @@
             for m in range(2):
                 vbuf[k, m, pl.ds(mine, half)] = recv[k][m * half : (m + 1) * half]
                 vbuf[k, m, pl.ds(other, half)] = swap[k][m * half : (m + 1) * half]
+        total_ref[...] = count
         own = pl.ds(pl.multiple_of(pos * shard_rows, shard_rows), shard_rows)
         iacc[...] = jnp.zeros_like(iacc)
         iacc[1, own] = iacc_in[1]
@@ -258,13 +281,9 @@
                 t = u * item_blocks + b
                 total = total + itile_ref[t] * count[t : t + 1]
             iacc[0, pl.ds(pl.multiple_of(pos * shard_rows + b * tile, tile), tile)] = total
-        for u in range(user_blocks):
-            total = uacc_in[0, u * tile : (u + 1) * tile]
-            for b in range(item_blocks):
-                t = u * item_blocks + b
-                total = total + utile_ref[t] * count[t : t + 1]
-            uacc[0, u * tile : (u + 1) * tile] = total
-        uacc[1] = uacc_in[1]
+        for c in copies:
+            c.wait()
+        places = []
         for k in range(peers):
             group = lax.bitwise_xor(pos, k + 1)
             for s in range(obs_slots):
@@ -272,23 +291,15 @@
                 urows = pl.ds(pl.multiple_of(ou_ref[at] * tile, tile), tile)
                 brows = pl.ds(pl.multiple_of(oi_ref[at] * tile, tile), tile)
                 irows = pl.ds(pl.multiple_of(group * shard_rows + oi_ref[at] * tile, tile), tile)
+                places.append((urows, irows))
                 used = jnp.where(s < oc_ref[group], 1.0, 0.0)
                 logits = rows_by_cols(up_ref[urows], vbuf[k, 0, brows])
                 imputed = rows_by_cols(ux_ref[urows], vbuf[k, 1, brows])
-                g, h = observed(logits, imputed, w_ref[at], used)
-                uacc[0, urows] += plain(g, vbuf[k, 0, brows])
-                uacc[1, urows] += plain(h, vbuf[k, 1, brows])
-                iacc[0, irows] += over_rows(g, up_ref[urows])
-                iacc[1, irows] += over_rows(h, ux_ref[urows])
-        for k in range(item_ways):
-            rows = pl.ds(pl.multiple_of(lax.bitwise_xor(pos, k) * share, share), share)
-            for m in range(2):
-                part = uacc[m, rows]
-                if k == 0:
-                    outs[peers][m * share : (m + 1) * share] = part
-                else:
-                    outs[k - 1][m * share : (m + 1) * share] = part.astype(bf16)
-        send, keep = outs[peers + 1], outs[peers + 2]
+                t = k * obs_slots + s
+                gbuf[t], hbuf[t] = observed(logits, imputed, w_ref[at], used)
+        for t, (urows, irows) in enumerate(places):
+            iacc[0, irows] += over_rows(gbuf[t], up_ref[urows])
+            iacc[1, irows] += over_rows(hbuf[t], ux_ref[urows])
         for q in range(chips):
             for r in range(item_ways):
                 for m in range(2):
@@ -300,60 +311,110 @@
                     send[at : at + item_share] = iacc[m, to_send].astype(bf16)
 
     core_rows = 2 * item_ways * chips * item_share
+    id_args = (obs_user, obs_item, obs_count)
+    core_send, core_keep, vbuf, gbuf, hbuf, count = call(
+        items,
+        "item_tiles",
+        (
+            shape((core_rows, rank), bf16),
+            shape((core_rows, rank), f32),
+            shape((peers, 2, shard_rows, rank), bf16),
+            shape((slots, tile, tile), bf16),
+            shape((slots, tile, tile), bf16),
+            shape((pairs, rank), f32),
+        ),
+        [HBM, HBM, HBM] + [VM] * (6 + 2 * peers),
+        (*in_hbm(id_args), user_pred, user_imp, own_count, itile, iacc, weights, *received, *swapped),
+        (4 * slots * 2 * tile**3, 4000000, 2 * slots * tile * tile),
+        tuple(pltpu.SMEM(x.shape, x.dtype) for x in id_args)
+        + (pltpu.SemaphoreType.DMA((3,)), pltpu.VMEM((2, item_ways * shard_rows, rank), f32)),
+    )
+
+    def users(ou_hbm, oi_hbm, utile_ref, uacc_in, count_ref, vbuf, gbuf, hbuf, *refs):
+        outs = refs[: peers + 1]
+        ou_ref, oi_ref, sems, uacc = refs[peers + 1 :]
+        copies = [
+            pltpu.make_async_copy(ou_hbm, ou_ref, sems.at[0]),
+            pltpu.make_async_copy(oi_hbm, oi_ref, sems.at[1]),
+        ]
+        for c in copies:
+            c.start()
+        pos = lax.axis_index("item")
+        count = count_ref[...]
+        for u in range(user_blocks):
+            total = uacc_in[0, u * tile : (u + 1) * tile]
+            for b in range(item_blocks):
+                t = u * item_blocks + b
+                total = total + utile_ref[t] * count[t : t + 1]
+            uacc[0, u * tile : (u + 1) * tile] = total
+        uacc[1] = uacc_in[1]
+        for c in copies:
+            c.wait()
+        for k in range(peers):
+            group = lax.bitwise_xor(pos, k + 1)
+            for s in range(obs_slots):
+                at = group * obs_slots + s
+                t = k * obs_slots + s
+                urows = pl.ds(pl.multiple_of(ou_ref[at] * tile, tile), tile)
+                brows = pl.ds(pl.multiple_of(oi_ref[at] * tile, tile), tile)
+                uacc[0, urows] += plain(gbuf[t], vbuf[k, 0, brows])
+                uacc[1, urows] += plain(hbuf[t], vbuf[k, 1, brows])
+        for k in range(item_ways):
+            rows = pl.ds(pl.multiple_of(lax.bitwise_xor(pos, k) * share, share), share)
+            for m in range(2):
+                part = uacc[m, rows]
+                if k == 0:
+                    outs[peers][m * share : (m + 1) * share] = part
+                else:
+                    outs[k - 1][m * share : (m + 1) * share] = part.astype(bf16)
+
     results = call(
-        remote,
-        "remote_tiles",
-        tuple(shape((2 * share, rank), bf16) for _ in range(peers))
-        + (shape((2 * share, rank), f32), shape((core_rows, rank), bf16), shape((core_rows, rank), f32)),
-        [SM, SM, SM] + [VM] * (8 + 2 * peers),
-        (
-            obs_user, obs_item, obs_count, user_pred, user_imp, own_count, utile, itile, uacc, iacc, weights,
-            *received, *swapped,
-        ),
-        (6 * (obs_all - obs_slots) * 2 * tile**3, 8000000, 2 * (obs_all - obs_slots) * tile * tile),
-        (
-            pltpu.VMEM((peers, 2, shard_rows, rank), bf16),
-            pltpu.VMEM((2, user_rows, rank), f32),
-            pltpu.VMEM((2, item_ways * shard_rows, rank), f32),
-        ),
-    )
-    user_own, core_send, core_keep = results[peers:]
+        users,
+        "user_tiles",
+        tuple(shape((2 * share, rank), bf16) for _ in range(peers)) + (shape((2 * share, rank), f32),),
+        [HBM, HBM] + [VM] * 6,
+        (*in_hbm(id_args[:2]), utile, uacc, count, vbuf, gbuf, hbuf),
+        (2 * slots * 2 * tile**3, 4000000, 0),
+        tuple(pltpu.SMEM(x.shape, x.dtype) for x in id_args[:2])
+        + (pltpu.SemaphoreType.DMA((2,)), pltpu.VMEM((2, user_rows, rank), f32)),
+    )
+    user_own = results[peers]
     core_recv = core_peer(core_send)
     user_recv = [item_peer(results[k], k + 1) for k in range(peers)]
 
     chip_rows = 2 * item_ways * item_share
 
-    def fold_core(keep_ref, recv_ref, *outs):
-        for k in range(chips):
-            rows = pl.ds(k * chip_rows, chip_rows)
-            outs[k][...] = (keep_ref[rows] + recv_ref[rows].astype(f32)).astype(outs[k].dtype)
-
-    folded = call(
-        fold_core,
-        "fold_core",
-        (shape((chip_rows, rank), f32),) + tuple(shape((chip_rows, rank), bf16) for _ in range(chips - 1)),
-        [VM, VM],
-        (core_keep, core_recv),
-        (0, 1000, 0),
-    )
-    chip_recv = [chip_peer(folded[k], k) for k in range(1, chips)]
-
-    def fold_chips(own_ref, *refs):
-        recv = refs[: chips - 1]
-        outs = refs[chips - 1 :]
+    def fold_half(keep_ref, recv_ref, *refs):
+        low_ref, high_ref = refs[-2:]
+        rows = low_ref.shape[0]
+        low_ref[...] = keep_ref[:rows] + recv_ref[:rows].astype(f32)
+        high_ref[...] = (keep_ref[rows:] + recv_ref[rows:].astype(f32)).astype(bf16)
+
+    kept, arrived, after = core_keep, core_recv, (user_own,)
+    step = chips // 2
+    while step:
+        kept, sent = call(
+            fold_half,
+            "fold_half",
+            (shape((step * chip_rows, rank), f32), shape((step * chip_rows, rank), bf16)),
+            [VM, VM] + [VM] * len(after),
+            (kept, arrived, *after),
+            (0, 1000, 0),
+        )
+        arrived, after = chip_peer(sent, step), ()
+        step //= 2
+
+    def fold_chips(own_ref, recv_ref, *outs):
         for k in range(item_ways):
             rows = pl.ds(k * 2 * item_share, 2 * item_share)
-            part = own_ref[rows]
-            for r in recv:
-                part = part + r[rows].astype(f32)
-            outs[k][...] = part
+            outs[k][...] = (own_ref[rows] + recv_ref[rows].astype(f32)).astype(outs[k].dtype)
 
     shares = call(
         fold_chips,
         "fold_chips",
-        tuple(shape((2 * item_share, rank), f32) for _ in range(item_ways)),
-        [VM] * chips,
-        (folded[0], *chip_recv),
+        (shape((2 * item_share, rank), f32),) + tuple(shape((2 * item_share, rank), bf16) for _ in range(peers)),
+        [VM, VM],
+        (kept, arrived),
         (0, 1000, 0),
     )
     item_recv = [item_peer(shares[k], k) for k in range(1, item_ways)]
@@ -369,7 +430,7 @@
             outs[m][...] = part
             part = item_ref[m * item_share : (m + 1) * item_share]
             for r in irecv:
-                part = part + r[m * item_share : (m + 1) * item_share]
+                part = part + r[m * item_share : (m + 1) * item_share].astype(f32)
             outs[2 + m][...] = part
 
     return call(

time: 45.4 us -> 38.1 us (0.84)
  Pallas kernels: 11.8 us -> 8.06 us
  waiting for transfers between devices: 13 us -> 10.9 us
  starting transfers between devices: 18.9 us -> 18.1 us
  local copies, waits for them, and re-layouts: 0.68 us -> 0.02 us
    pallas_call x6 -> x8, Pallas kernels: 11.8 us -> 8.06 us  [call(): pl.pallas_call(body, out_shape=out_shapes, in_specs=specs, out_specs=tupl...]
    ppermute x3 -> x2, waiting for transfers between devices: 4.82 us -> 2.78 us  [chip_peer(): lax.ppermute(x, 'user', [(i, i ^ cores * k) for i in range(user_ways)])]
    ppermute x4, waiting for transfers between devices: 2.55 us -> 1.48 us  [core_peer(): return lax.ppermute(x, 'user', [(i, i ^ 1) for i in range(user_ways)])]
    ppermute x9, waiting for transfers between devices: 5.6 us -> 6.65 us  [item_peer(): return lax.ppermute(x, 'item', [(i, i ^ k) for i in range(item_ways)])]
    unnamed x10 -> x4, local copies, waits for them, and re-layouts: 0.68 us -> 0.01 us
    ppermute x3 -> x2, starting transfers between devices: 3.55 us -> 3.14 us  [chip_peer(): lax.ppermute(x, 'user', [(i, i ^ cores * k) for i in range(user_ways)])]
  transfers between devices with their start and end apart: 16 -> 15, of which waited for: 9 -> 8; matrix products, arithmetic and copies ran while one was open for 0% -> 0% of each run, Pallas kernels for 13% -> 12%
where the time goes in v3:
time: 38.1 us; the launch traced here: 37.9 us
  starting transfers between devices  18.1 us (48%)
  waiting for transfers between devices  10.9 us (29%)
  Pallas kernels  8.06 us (21%)
  between operations  0.78 us (2%)
    ppermute x9, starting transfers between devices, item_peer(): return lax.ppermute(x, 'item', [(i, i ^ k) for i in range(item_ways)])  14.5 us
    pallas_call x8, Pallas kernels, call(): pl.pallas_call(body, out_shape=out_shapes, in_specs=specs, out_specs=tupl...  8.06 us
    ppermute x9, waiting for transfers between devices, item_peer(): return lax.ppermute(x, 'item', [(i, i ^ k) for i in range(item_ways)])  6.65 us
    ppermute x2, starting transfers between devices, chip_peer(): lax.ppermute(x, 'user', [(i, i ^ cores * k) for i in range(user_ways)])  3.14 us
    ppermute x2, waiting for transfers between devices, chip_peer(): lax.ppermute(x, 'user', [(i, i ^ cores * k) for i in range(user_ways)])  2.78 us
    ppermute x4, waiting for transfers between devices, core_peer(): return lax.ppermute(x, 'user', [(i, i ^ 1) for i in range(user_ways)])  1.48 us
  transfers between devices with their start and end apart: 15, of which 8 were waited for; matrix products, arithmetic and copies ran while one was open for 0% of the time, Pallas kernels for 12%

profile of v3, /device:TPU:0, one launch (start us, length us, event | category | flops | bytes accessed | tf_op | source)
XLA Modules:
  0.0 37.9 jit_solution(8948621967127945458)
XLA Ops:
  0.6 1.0 %pack.1 = (bf16[272,128]{1,0:T(8,128)(2,1)S(1)}, bf16[272,128]{1,0:T(8,128)(2,1)S(1)}, bf16[272,128]{1,0:T(8,128)(2,1)S(1)}, f32[16,128]{1,0:T(8,128)S(1)}) custom-call(s32[64]{0:T(128)} %bitcast.23, s32[64]{0:T(128)} %bitcast.24, bf16[256,128]{1,0:T(8,128)(2,1)} %vp_hbm.3, bf16[256,128]{1,0:T(8,128)(2,1)} %vi_hbm.3), custom_call_target="tpu_custom_call" | custom-call | bytes 400000 | tf_op jit(solution)/shard_map/pack/pallas_call | solution.py:34
  1.6 3.1 %collective-permute-start = (bf16[272,128]{1,0:T(8,128)(2,1)S(1)}, bf16[272,128]{1,0:T(8,128)(2,1)S(1)}, u32[]{:S(2)}, u32[]{:S(2)}) collective-permute-start(bf16[272,128]{1,0:T(8,128)(2,1)S(1)} %get-tuple-element.40), channel_id=1, source_target_pairs={{0,1},{1,0},{2,3},{3,2},{4,5},{5,4},{6,7},{7,6},{8,9},{9,8},{10,11... | collective-permute-start | bytes 208904 | tf_op jit(solution)/shard_map/ppermute | solution.py:96
  4.7 2.6 %collective-permute-start.1 = (bf16[272,128]{1,0:T(8,128)(2,1)S(1)}, bf16[272,128]{1,0:T(8,128)(2,1)S(1)}, u32[]{:S(2)}, u32[]{:S(2)}) collective-permute-start(bf16[272,128]{1,0:T(8,128)(2,1)S(1)} %get-tuple-element.41), channel_id=1, source_target_pairs={{0,2},{1,3},{2,0},{3,1},{4,6},{5,7},{6,4},{7,5},{8,10},{9,11},{10,... | collective-permute-start | bytes 208904 | tf_op jit(solution)/shard_map/ppermute | solution.py:96
  7.3 0.0 collective-permute-start.2
  7.3 0.0 copy-start.1
  7.3 3.2 %local_tiles.1 = (f32[16,128,128]{2,1,0:T(8,128)S(1)}, f32[16,128,128]{2,1,0:T(8,128)S(1)}, f32[2,1024,128]{2,1,0:T(8,128)S(1)}, f32[2,256,128]{2,1,0:T(8,128)S(...) custom-call(s32[16]{0:T(128)} %bitcast.15, ...), custom_call_target="tpu_custom_call" | custom-call | flops 268435456 | bytes 8000000 | tf_op jit(solution)/shard_map/local_tiles/pallas_call | solution.py:34
  10.5 0.0 copy-start
  10.5 0.0 collective-permute-done.refs_0_
  10.6 0.1 collective-permute-start.3
  10.6 1.6 %collective-permute-done.1.refs_1_ = bf16[272,128]{1,0:T(8,128)(2,1)S(1)} collective-permute-done((bf16[272,128]{1,0:T(8,128)(2,1)S(1)}, bf16[272,128]{1,0:T(8,128)(2,1)S(1)}, u32[]{:S(2)}, u32[]{:S(2)}) %collective-permute-start.1) | collective-permute-done | bytes 69664 | tf_op jit(solution)/shard_map/ppermute | solution.py:96
  12.2 0.1 collective-permute-start.4
  12.3 1.2 %collective-permute-done.2.refs_2_ = bf16[272,128]{1,0:T(8,128)(2,1)S(1)} collective-permute-done((bf16[272,128]{1,0:T(8,128)(2,1)S(1)}, bf16[272,128]{1,0:T(8,128)(2,1)S(1)}, u32[]{:S(2)}, u32[]{:S(2)}) %collective-permute-start.2) | collective-permute-done | bytes 69664 | tf_op jit(solution)/shard_map/ppermute | solution.py:96
  13.5 0.1 collective-permute-start.5
  13.6 0.0 collective-permute-done.3.refs_3_
  13.6 0.0 collective-permute-done.4.refs_4_
  13.6 1.2 %collective-permute-done.5.refs_5_ = bf16[256,128]{1,0:T(8,128)(2,1)S(1)} collective-permute-done((bf16[256,128]{1,0:T(8,128)(2,1)S(1)}, bf16[256,128]{1,0:T(8,128)(2,1)S(1)}, u32[]{:S(2)}, u32[]{:S(2)}) %collective-permute-start.5) | collective-permute-done | bytes 65568 | tf_op jit(solution)/shard_map/ppermute | solution.py:99
  14.8 0.0 copy-done.1
  14.8 0.0 copy-done
  14.8 2.0 %item_tiles.1 = (bf16[1024,128]{1,0:T(8,128)(2,1)S(1)}, f32[1024,128]{1,0:T(8,128)S(1)}, bf16[3,2,256,128]{3,2,1,0:T(8,128)(2,1)S(1)}, bf16[12,128,128]{2,1,0:T(...) custom-call(s32[16]{0:T(128)} %bitcast.16, s32[16]{0:T(128)} %bitcast.19, s32[4]{0:T(128)} %bitcast.22, ...), custom_call_target="tpu_custom_call" | custom-call | flops 201326592 | bytes 4000000 | tf_op jit(solution)/shard_map/item_tiles/pallas_call | solution.py:34
  16.8 0.2 collective-permute-start.6
  17.0 1.1 %user_tiles.1 = (bf16[512,128]{1,0:T(8,128)(2,1)S(1)}, bf16[512,128]{1,0:T(8,128)(2,1)S(1)}, bf16[512,128]{1,0:T(8,128)(2,1)S(1)}, f32[512,128]{1,0:T(8,128)S(1)}) custom-call(s32[16]{0:T(128)} %bitcast.17, s32[16]{0:T(128)} %bitcast.20, f32[16,128,128]{2,1,0:T(8,128)S(1)} %get-tuple-element.34.utile_ref, f32[2,1024,128]{2,1,0:T(8,128)S(1)} %get-tuple-element.35.uacc_in, ...), custom_call_target="tpu_custom_call" | custom-call | flops 100663296 | bytes 4000000 | tf_op jit(solution)/shard_map/user_tiles/pallas_call | solution.py:34
  18.1 0.3 collective-permute-done.6.recv_ref
  18.4 0.1 fold_half.2
  18.5 1.6 %collective-permute-start.7 = (bf16[512,128]{1,0:T(8,128)(2,1)S(1)}, bf16[512,128]{1,0:T(8,128)(2,1)S(1)}, u32[]{:S(2)}, u32[]{:S(2)}) collective-permute-start(bf16[512,128]{1,0:T(8,128)(2,1)S(1)} %get-tuple-element.54), channel_id=1, source_target_pairs={{0,16},{4,20},{8,24},{12,28},{16,0},{20,4},{24,8},{28,12},{1,17},{... | collective-permute-start | bytes 393224 | tf_op jit(solution)/shard_map/ppermute | solution.py:102
  20.0 0.8 %collective-permute-start.9 = (bf16[512,128]{1,0:T(8,128)(2,1)S(1)}, bf16[512,128]{1,0:T(8,128)(2,1)S(1)}, u32[]{:S(2)}, u32[]{:S(2)}) collective-permute-start(bf16[512,128]{1,0:T(8,128)(2,1)S(1)} %get-tuple-element.58), channel_id=1, source_target_pairs={{0,1},{1,0},{2,3},{3,2},{4,5},{5,4},{6,7},{7,6},{8,9},{9,8},{10,11... | collective-permute-start | bytes 393224 | tf_op jit(solution)/shard_map/ppermute | solution.py:96
  20.8 2.0 %collective-permute-start.10 = (bf16[512,128]{1,0:T(8,128)(2,1)S(1)}, bf16[512,128]{1,0:T(8,128)(2,1)S(1)}, u32[]{:S(2)}, u32[]{:S(2)}) collective-permute-start(bf16[512,128]{1,0:T(8,128)(2,1)S(1)} %get-tuple-element.59), channel_id=1, source_target_pairs={{0,2},{1,3},{2,0},{3,1},{4,6},{5,7},{6,4},{7,5},{8,10},{9,11},{10,... | collective-permute-start | bytes 393224 | tf_op jit(solution)/shard_map/ppermute | solution.py:96
  22.8 1.6 %collective-permute-start.11 = (bf16[512,128]{1,0:T(8,128)(2,1)S(1)}, bf16[512,128]{1,0:T(8,128)(2,1)S(1)}, u32[]{:S(2)}, u32[]{:S(2)}) collective-permute-start(bf16[512,128]{1,0:T(8,128)(2,1)S(1)} %get-tuple-element.60), channel_id=1, source_target_pairs={{0,3},{1,2},{2,1},{3,0},{4,7},{5,6},{6,5},{7,4},{8,11},{9,10},{10,... | collective-permute-start | bytes 393224 | tf_op jit(solution)/shard_map/ppermute | solution.py:96
  24.4 0.0 collective-permute-done.7.recv_ref
  24.5 1.6 %collective-permute-start.8 = (bf16[256,128]{1,0:T(8,128)(2,1)S(1)}, bf16[256,128]{1,0:T(8,128)(2,1)S(1)}, u32[]{:S(2)}, u32[]{:S(2)}) collective-permute-start(bf16[256,128]{1,0:T(8,128)(2,1)S(1)} %get-tuple-element.56), channel_id=1, source_target_pairs={{0,8},{4,12},{8,0},{12,4},{16,24},{20,28},{24,16},{28,20},{1,9},{5... | collective-permute-start | bytes 196616 | tf_op jit(solution)/shard_map/ppermute | solution.py:102
  26.0 2.8 %collective-permute-done.8.recv_ref = bf16[256,128]{1,0:T(8,128)(2,1)S(1)} collective-permute-done((bf16[256,128]{1,0:T(8,128)(2,1)S(1)}, bf16[256,128]{1,0:T(8,128)(2,1)S(1)}, u32[]{:S(2)}, u32[]{:S(2)}) %collective-permute-start.8) | collective-permute-done | bytes 65568 | tf_op jit(solution)/shard_map/ppermute | solution.py:102
  28.8 0.5 %collective-permute-start.12 = (bf16[64,128]{1,0:T(8,128)(2,1)S(1)}, bf16[64,128]{1,0:T(8,128)(2,1)S(1)}, u32[]{:S(2)}, u32[]{:S(2)}) collective-permute-start(bf16[64,128]{1,0:T(8,128)(2,1)S(1)} %get-tuple-element.61), channel_id=1, source_target_pairs={{0,1},{1,0},{2,3},{3,2},{4,5},{5,4},{6,7},{7,6},{8,9},{9,8},{10,11... | collective-permute-start | bytes 49160 | tf_op jit(solution)/shard_map/ppermute | solution.py:96
  29.3 2.3 %collective-permute-start.13 = (bf16[64,128]{1,0:T(8,128)(2,1)S(1)}, bf16[64,128]{1,0:T(8,128)(2,1)S(1)}, u32[]{:S(2)}, u32[]{:S(2)}) collective-permute-start(bf16[64,128]{1,0:T(8,128)(2,1)S(1)} %get-tuple-element.62), channel_id=1, source_target_pairs={{0,2},{1,3},{2,0},{3,1},{4,6},{5,7},{6,4},{7,5},{8,10},{9,11},{10,... | collective-permute-start | bytes 49160 | tf_op jit(solution)/shard_map/ppermute | solution.py:96
  31.6 0.0 collective-permute-done.9.refs_0_
  31.6 1.6 %collective-permute-start.14 = (bf16[64,128]{1,0:T(8,128)(2,1)S(1)}, bf16[64,128]{1,0:T(8,128)(2,1)S(1)}, u32[]{:S(2)}, u32[]{:S(2)}) collective-permute-start(bf16[64,128]{1,0:T(8,128)(2,1)S(1)} %get-tuple-element.63), channel_id=1, source_target_pairs={{0,3},{1,2},{2,1},{3,0},{4,7},{5,6},{6,5},{7,4},{8,11},{9,10},{10,... | collective-permute-start | bytes 49160 | tf_op jit(solution)/shard_map/ppermute | solution.py:96
  33.3 0.7 %collective-permute-done.10.refs_1_ = bf16[512,128]{1,0:T(8,128)(2,1)S(1)} collective-permute-done((bf16[512,128]{1,0:T(8,128)(2,1)S(1)}, bf16[512,128]{1,0:T(8,128)(2,1)S(1)}, u32[]{:S(2)}, u32[]{:S(2)}) %collective-permute-start.10) | collective-permute-done | bytes 131104 | tf_op jit(solution)/shard_map/ppermute | solution.py:96
  33.9 0.0 collective-permute-done.11.refs_2_
  33.9 0.0 collective-permute-done.12.refs_3_
  33.9 2.3 %collective-permute-done.13.refs_4_ = bf16[64,128]{1,0:T(8,128)(2,1)S(1)} collective-permute-done((bf16[64,128]{1,0:T(8,128)(2,1)S(1)}, bf16[64,128]{1,0:T(8,128)(2,1)S(1)}, u32[]{:S(2)}, u32[]{:S(2)}) %collective-permute-start.13) | collective-permute-done | bytes 16416 | tf_op jit(solution)/shard_map/ppermute | solution.py:96
  36.2 0.9 %collective-permute-done.14.refs_5_ = bf16[64,128]{1,0:T(8,128)(2,1)S(1)} collective-permute-done((bf16[64,128]{1,0:T(8,128)(2,1)S(1)}, bf16[64,128]{1,0:T(8,128)(2,1)S(1)}, u32[]{:S(2)}, u32[]{:S(2)}) %collective-permute-start.14) | collective-permute-done | bytes 16416 | tf_op jit(solution)/shard_map/ppermute | solution.py:96
  37.2 0.7 %finish.1 = (f32[256,128]{1,0:T(8,128)}, f32[256,128]{1,0:T(8,128)}, f32[32,128]{1,0:T(8,128)}, f32[32,128]{1,0:T(8,128)}) custom-call(f32[512,128]{1,0:T(8,128)S(1)} %get-tuple-element.50.refs_0_.user_ref, f32[64,128]{1,0:T(8,128)S(1)} %get-tuple-element.57.item_ref, bf16[512,128]{1,0:T(8,128)(2,1)S(1)} %collective-permute-done.9.refs_0_, ...), custom_call_target="tpu_custom_call" | custom-call | bytes 1000000 | tf_op jit(solution)/shard_map/finish/pallas_call | solution.py:34
  (8 shorter events, 0.1 us)
Async XLA Ops:
  1.6 8.9 %collective-permute-start = (bf16[272,128]{1,0:T(8,128)(2,1)S(1)}, bf16[272,128]{1,0:T(8,128)(2,1)S(1)}, u32[]{:S(2)}, u32[]{:S(2)}) collective-permute-start(bf16[272,128]{1,0:T(8,128)(2,1)S(1)} %get-tuple-element.40), channel_id=1, source_target_pairs={{0,1},{1,0},{2,3},{3,2},{4,5},{5,4},{6,7},{7,6},{8,9},{9,8},{10,11... | collective-permute-start | bytes 208904 | tf_op jit(solution)/shard_map/ppermute | solution.py:96
  4.7 7.5 %collective-permute-start.1 = (bf16[272,128]{1,0:T(8,128)(2,1)S(1)}, bf16[272,128]{1,0:T(8,128)(2,1)S(1)}, u32[]{:S(2)}, u32[]{:S(2)}) collective-permute-start(bf16[272,128]{1,0:T(8,128)(2,1)S(1)} %get-tuple-element.41), channel_id=1, source_target_pairs={{0,2},{1,3},{2,0},{3,1},{4,6},{5,7},{6,4},{7,5},{8,10},{9,11},{10,... | collective-permute-start | bytes 208904 | tf_op jit(solution)/shard_map/ppermute | solution.py:96
  7.3 6.2 %collective-permute-start.2 = (bf16[272,128]{1,0:T(8,128)(2,1)S(1)}, bf16[272,128]{1,0:T(8,128)(2,1)S(1)}, u32[]{:S(2)}, u32[]{:S(2)}) collective-permute-start(bf16[272,128]{1,0:T(8,128)(2,1)S(1)} %get-tuple-element.42), channel_id=1, source_target_pairs={{0,3},{1,2},{2,1},{3,0},{4,7},{5,6},{6,5},{7,4},{8,11},{9,10},{10,... | collective-permute-start | bytes 208904 | tf_op jit(solution)/shard_map/ppermute | solution.py:96
  7.3 7.5 %copy-start.1 = (bf16[1024,128]{1,0:T(8,128)(2,1)S(1)}, bf16[1024,128]{1,0:T(8,128)(2,1)}, u32[]{:S(2)}) copy-start(bf16[1024,128]{1,0:T(8,128)(2,1)} %ux_ref.1) | copy-start | bytes 786436
  10.5 4.3 %copy-start = (bf16[1024,128]{1,0:T(8,128)(2,1)S(1)}, bf16[1024,128]{1,0:T(8,128)(2,1)}, u32[]{:S(2)}) copy-start(bf16[1024,128]{1,0:T(8,128)(2,1)} %up_ref.1) | copy-start | bytes 786436
  10.6 3.0 %collective-permute-start.3 = (bf16[256,128]{1,0:T(8,128)(2,1)S(1)}, bf16[256,128]{1,0:T(8,128)(2,1)S(1)}, u32[]{:S(2)}, u32[]{:S(2)}) collective-permute-start(bf16[256,128]{1,0:T(8,128)(2,1)S(1)} %slice_multiply_fusion.2), channel_id=1, source_target_pairs={{0,4},{4,0},{8,12},{12,8},{16,20},{20,16},{24,28},{28,24},{1,5},{5... | collective-permute-start | bytes 196616 | tf_op jit(solution)/shard_map/ppermute | solution.py:99
  12.2 1.4 %collective-permute-start.4 = (bf16[256,128]{1,0:T(8,128)(2,1)S(1)}, bf16[256,128]{1,0:T(8,128)(2,1)S(1)}, u32[]{:S(2)}, u32[]{:S(2)}) collective-permute-start(bf16[256,128]{1,0:T(8,128)(2,1)S(1)} %slice_multiply_fusion.1), channel_id=1, source_target_pairs={{0,4},{4,0},{8,12},{12,8},{16,20},{20,16},{24,28},{28,24},{1,5},{5... | collective-permute-start | bytes 196616 | tf_op jit(solution)/shard_map/ppermute | solution.py:99
  13.5 1.3 %collective-permute-start.5 = (bf16[256,128]{1,0:T(8,128)(2,1)S(1)}, bf16[256,128]{1,0:T(8,128)(2,1)S(1)}, u32[]{:S(2)}, u32[]{:S(2)}) collective-permute-start(bf16[256,128]{1,0:T(8,128)(2,1)S(1)} %slice_multiply_fusion), channel_id=1, source_target_pairs={{0,4},{4,0},{8,12},{12,8},{16,20},{20,16},{24,28},{28,24},{1,5},{5... | collective-permute-start | bytes 196616 | tf_op jit(solution)/shard_map/ppermute | solution.py:99
  16.8 1.6 %collective-permute-start.6 = (bf16[1024,128]{1,0:T(8,128)(2,1)S(1)}, bf16[1024,128]{1,0:T(8,128)(2,1)S(1)}, u32[]{:S(2)}, u32[]{:S(2)}) collective-permute-start(bf16[1024,128]{1,0:T(8,128)(2,1)S(1)} %get-tuple-element.52), channel_id=1, source_target_pairs={{0,4},{4,0},{8,12},{12,8},{16,20},{20,16},{24,28},{28,24},{1,5},{5... | collective-permute-start | bytes 786440 | tf_op jit(solution)/shard_map/ppermute | solution.py:99
  18.5 6.0 %collective-permute-start.7 = (bf16[512,128]{1,0:T(8,128)(2,1)S(1)}, bf16[512,128]{1,0:T(8,128)(2,1)S(1)}, u32[]{:S(2)}, u32[]{:S(2)}) collective-permute-start(bf16[512,128]{1,0:T(8,128)(2,1)S(1)} %get-tuple-element.54), channel_id=1, source_target_pairs={{0,16},{4,20},{8,24},{12,28},{16,0},{20,4},{24,8},{28,12},{1,17},{... | collective-permute-start | bytes 393224 | tf_op jit(solution)/shard_map/ppermute | solution.py:102
  20.0 11.6 %collective-permute-start.9 = (bf16[512,128]{1,0:T(8,128)(2,1)S(1)}, bf16[512,128]{1,0:T(8,128)(2,1)S(1)}, u32[]{:S(2)}, u32[]{:S(2)}) collective-permute-start(bf16[512,128]{1,0:T(8,128)(2,1)S(1)} %get-tuple-element.58), channel_id=1, source_target_pairs={{0,1},{1,0},{2,3},{3,2},{4,5},{5,4},{6,7},{7,6},{8,9},{9,8},{10,11... | collective-permute-start | bytes 393224 | tf_op jit(solution)/shard_map/ppermute | solution.py:96
  20.8 13.1 %collective-permute-start.10 = (bf16[512,128]{1,0:T(8,128)(2,1)S(1)}, bf16[512,128]{1,0:T(8,128)(2,1)S(1)}, u32[]{:S(2)}, u32[]{:S(2)}) collective-permute-start(bf16[512,128]{1,0:T(8,128)(2,1)S(1)} %get-tuple-element.59), channel_id=1, source_target_pairs={{0,2},{1,3},{2,0},{3,1},{4,6},{5,7},{6,4},{7,5},{8,10},{9,11},{10,... | collective-permute-start | bytes 393224 | tf_op jit(solution)/shard_map/ppermute | solution.py:96
  22.8 11.1 %collective-permute-start.11 = (bf16[512,128]{1,0:T(8,128)(2,1)S(1)}, bf16[512,128]{1,0:T(8,128)(2,1)S(1)}, u32[]{:S(2)}, u32[]{:S(2)}) collective-permute-start(bf16[512,128]{1,0:T(8,128)(2,1)S(1)} %get-tuple-element.60), channel_id=1, source_target_pairs={{0,3},{1,2},{2,1},{3,0},{4,7},{5,6},{6,5},{7,4},{8,11},{9,10},{10,... | collective-permute-start | bytes 393224 | tf_op jit(solution)/shard_map/ppermute | solution.py:96
  24.5 4.3 %collective-permute-start.8 = (bf16[256,128]{1,0:T(8,128)(2,1)S(1)}, bf16[256,128]{1,0:T(8,128)(2,1)S(1)}, u32[]{:S(2)}, u32[]{:S(2)}) collective-permute-start(bf16[256,128]{1,0:T(8,128)(2,1)S(1)} %get-tuple-element.56), channel_id=1, source_target_pairs={{0,8},{4,12},{8,0},{12,4},{16,24},{20,28},{24,16},{28,20},{1,9},{5... | collective-permute-start | bytes 196616 | tf_op jit(solution)/shard_map/ppermute | solution.py:102
  28.8 5.1 %collective-permute-start.12 = (bf16[64,128]{1,0:T(8,128)(2,1)S(1)}, bf16[64,128]{1,0:T(8,128)(2,1)S(1)}, u32[]{:S(2)}, u32[]{:S(2)}) collective-permute-start(bf16[64,128]{1,0:T(8,128)(2,1)S(1)} %get-tuple-element.61), channel_id=1, source_target_pairs={{0,1},{1,0},{2,3},{3,2},{4,5},{5,4},{6,7},{7,6},{8,9},{9,8},{10,11... | collective-permute-start | bytes 49160 | tf_op jit(solution)/shard_map/ppermute | solution.py:96
  29.3 6.9 %collective-permute-start.13 = (bf16[64,128]{1,0:T(8,128)(2,1)S(1)}, bf16[64,128]{1,0:T(8,128)(2,1)S(1)}, u32[]{:S(2)}, u32[]{:S(2)}) collective-permute-start(bf16[64,128]{1,0:T(8,128)(2,1)S(1)} %get-tuple-element.62), channel_id=1, source_target_pairs={{0,2},{1,3},{2,0},{3,1},{4,6},{5,7},{6,4},{7,5},{8,10},{9,11},{10,... | collective-permute-start | bytes 49160 | tf_op jit(solution)/shard_map/ppermute | solution.py:96
  31.6 5.5 %collective-permute-start.14 = (bf16[64,128]{1,0:T(8,128)(2,1)S(1)}, bf16[64,128]{1,0:T(8,128)(2,1)S(1)}, u32[]{:S(2)}, u32[]{:S(2)}) collective-permute-start(bf16[64,128]{1,0:T(8,128)(2,1)S(1)} %get-tuple-element.63), channel_id=1, source_target_pairs={{0,3},{1,2},{2,1},{3,0},{4,7},{5,6},{6,5},{7,4},{8,11},{9,10},{10,... | collective-permute-start | bytes 49160 | tf_op jit(solution)/shard_map/ppermute | solution.py:96

commit v4 on v3

--- a/solution.py
+++ b/solution.py
@@ -155,7 +155,7 @@
         ),
     )
     own_count = packed[peers]
-    received = [item_peer(packed[k], k + 1) for k in range(peers)]
+    received = [item_peer(packed[k], k + 1) for k in reversed(range(peers))][::-1]
 
     def observed(logits, imputed, weight, used):
         p = jax.nn.sigmoid(logits)
@@ -243,13 +243,13 @@
             pltpu.VMEM((obs_slots, tile, tile), bf16),
         ),
     )
-    swapped = [core_peer(x[: 2 * half] * one[:1]) for x, one in zip(received, ones)]
+    swapped = [core_peer(x[: 2 * half] * one[:1]) for x, one in zip(received[::-1], ones)][::-1]
 
     slots = peers * obs_slots
 
     def items(ou_hbm, oi_hbm, oc_hbm, up_ref, ux_ref, count_ref, itile_ref, iacc_in, w_ref, *refs):
-        recv = refs[:peers]
-        swap = refs[peers : 2 * peers]
+        recv = refs[:peers][::-1]
+        swap = refs[peers : 2 * peers][::-1]
         send, keep, vbuf, gbuf, hbuf, total_ref = refs[2 * peers : 2 * peers + 6]
         ou_ref, oi_ref, oc_ref, sems, iacc = refs[2 * peers + 6 :]
         copies = [
@@ -324,7 +324,7 @@
             shape((pairs, rank), f32),
         ),
         [HBM, HBM, HBM] + [VM] * (6 + 2 * peers),
-        (*in_hbm(id_args), user_pred, user_imp, own_count, itile, iacc, weights, *received, *swapped),
+        (*in_hbm(id_args), user_pred, user_imp, own_count, itile, iacc, weights, *received[::-1], *swapped[::-1]),
         (4 * slots * 2 * tile**3, 4000000, 2 * slots * tile * tile),
         tuple(pltpu.SMEM(x.shape, x.dtype) for x in id_args)
         + (pltpu.SemaphoreType.DMA((3,)), pltpu.VMEM((2, item_ways * shard_rows, rank), f32)),
@@ -380,66 +380,79 @@
     )
     user_own = results[peers]
     core_recv = core_peer(core_send)
-    user_recv = [item_peer(results[k], k + 1) for k in range(peers)]
+    user_recv = [item_peer(results[k], k + 1) for k in reversed(range(1, peers))]
 
     chip_rows = 2 * item_ways * item_share
 
-    def fold_half(keep_ref, recv_ref, *refs):
-        low_ref, high_ref = refs[-2:]
-        rows = low_ref.shape[0]
-        low_ref[...] = keep_ref[:rows] + recv_ref[:rows].astype(f32)
-        high_ref[...] = (keep_ref[rows:] + recv_ref[rows:].astype(f32)).astype(bf16)
-
-    kept, arrived, after = core_keep, core_recv, (user_own,)
-    step = chips // 2
-    while step:
-        kept, sent = call(
-            fold_half,
-            "fold_half",
-            (shape((step * chip_rows, rank), f32), shape((step * chip_rows, rank), bf16)),
-            [VM, VM] + [VM] * len(after),
-            (kept, arrived, *after),
-            (0, 1000, 0),
-        )
-        arrived, after = chip_peer(sent, step), ()
-        step //= 2
-
-    def fold_chips(own_ref, recv_ref, *outs):
+    def fold_core(keep_ref, recv_ref, after_ref, *outs):
+        for k in range(chips):
+            rows = pl.ds(k * chip_rows, chip_rows)
+            outs[k][...] = (keep_ref[rows] + recv_ref[rows].astype(f32)).astype(outs[k].dtype)
+
+    folded = call(
+        fold_core,
+        "fold_core",
+        (shape((chip_rows, rank), f32),) + tuple(shape((chip_rows, rank), bf16) for _ in range(chips - 1)),
+        [VM, VM, VM],
+        (core_keep, core_recv, user_own),
+        (0, 1000, 0),
+    )
+    chip_recv = [chip_peer(folded[k], k) for k in reversed(range(1, chips))]
+
+    def fold_chips(own_ref, *refs):
+        recv = refs[: chips - 1]
+        outs = refs[chips - 1 :]
         for k in range(item_ways):
             rows = pl.ds(k * 2 * item_share, 2 * item_share)
-            outs[k][...] = (own_ref[rows] + recv_ref[rows].astype(f32)).astype(outs[k].dtype)
+            part = own_ref[rows]
+            for r in recv:
+                part = part + r[rows].astype(f32)
+            outs[k][...] = part.astype(outs[k].dtype)
 
     shares = call(
         fold_chips,
         "fold_chips",
         (shape((2 * item_share, rank), f32),) + tuple(shape((2 * item_share, rank), bf16) for _ in range(peers)),
-        [VM, VM],
-        (kept, arrived),
-        (0, 1000, 0),
-    )
-    item_recv = [item_peer(shares[k], k) for k in range(1, item_ways)]
+        [VM] * chips,
+        (folded[0], *chip_recv),
+        (400000000, 1000, 0),
+    )
+    near_recv = item_peer(results[0], 1)
+    item_recv = [item_peer(shares[k], k) for k in reversed(range(1, item_ways))]
+
+    def sum_users(own_ref, *refs):
+        part = own_ref[...]
+        for r in refs[:-1]:
+            part = part + r[...].astype(f32)
+        refs[-1][...] = part
+
+    (user_sum,) = call(
+        sum_users,
+        "sum_users",
+        (shape((2 * share, rank), f32),),
+        [VM] * peers,
+        (user_own, *user_recv),
+        (1200000000, 1000, 0),
+    )
 
     def finish(user_ref, item_ref, *refs):
-        urecv = refs[:peers]
-        irecv = refs[peers : 2 * peers]
-        outs = refs[2 * peers :]
+        near, irecv, outs = refs[0], refs[1 : peers + 1], refs[peers + 1 :]
         for m in range(2):
-            part = user_ref[m * share : (m + 1) * share]
-            for r in urecv:
-                part = part + r[m * share : (m + 1) * share].astype(f32)
-            outs[m][...] = part
-            part = item_ref[m * item_share : (m + 1) * item_share]
+            rows = pl.ds(m * share, share)
+            outs[m][...] = user_ref[rows] + near[rows].astype(f32)
+            rows = pl.ds(m * item_share, item_share)
+            part = item_ref[rows]
             for r in irecv:
-                part = part + r[m * item_share : (m + 1) * item_share].astype(f32)
+                part = part + r[rows].astype(f32)
             outs[2 + m][...] = part
 
     return call(
         finish,
         "finish",
         (shape((share, rank), f32),) * 2 + (shape((item_share, rank), f32),) * 2,
-        [VM] * (2 + 2 * peers),
-        (user_own, shares[0], *user_recv, *item_recv),
-        (0, 1000000, 0),
+        [VM] * (3 + peers),
+        (user_sum, shares[0], near_recv, *item_recv),
+        (0, 1000, 0),
     )
 
 

time: 38.1 us -> 36 us (0.945)
  waiting for transfers between devices: 10.9 us -> 7.46 us
  starting transfers between devices: 18.1 us -> 19.4 us
    ppermute x9, waiting for transfers between devices: 6.65 us -> 4.55 us  [item_peer(): return lax.ppermute(x, 'item', [(i, i ^ k) for i in range(item_ways)])]
    ppermute x2 -> x3, waiting for transfers between devices: 2.78 us -> 2.01 us  [chip_peer(): lax.ppermute(x, 'user', [(i, i ^ cores * k) for i in range(user_ways)])]
    ppermute x4, starting transfers between devices: 0.43 us -> 1.11 us  [core_peer(): return lax.ppermute(x, 'user', [(i, i ^ 1) for i in range(user_ways)])]
    ppermute x4, waiting for transfers between devices: 1.48 us -> 0.9 us  [core_peer(): return lax.ppermute(x, 'user', [(i, i ^ 1) for i in range(user_ways)])]
    ppermute x2 -> x3, starting transfers between devices: 3.14 us -> 3.55 us  [chip_peer(): lax.ppermute(x, 'user', [(i, i ^ cores * k) for i in range(user_ways)])]
  transfers between devices with their start and end apart: 15 -> 16, of which waited for: 8 -> 8; matrix products, arithmetic and copies ran while one was open for 0% -> 0% of each run, Pallas kernels for 12% -> 12%
where the time goes in v4:
time: 36 us; the launch traced here: 35.8 us
  starting transfers between devices  19.4 us (54%)
  Pallas kernels  8.1 us (22%)
  waiting for transfers between devices  7.46 us (21%)
  between operations  0.77 us (2%)
    ppermute x9, starting transfers between devices, item_peer(): return lax.ppermute(x, 'item', [(i, i ^ k) for i in range(item_ways)])  14.7 us
    pallas_call x8, Pallas kernels, call(): pl.pallas_call(body, out_shape=out_shapes, in_specs=specs, out_specs=tupl...  8.1 us
    ppermute x9, waiting for transfers between devices, item_peer(): return lax.ppermute(x, 'item', [(i, i ^ k) for i in range(item_ways)])  4.55 us
    ppermute x3, starting transfers between devices, chip_peer(): lax.ppermute(x, 'user', [(i, i ^ cores * k) for i in range(user_ways)])  3.55 us
    ppermute x3, waiting for transfers between devices, chip_peer(): lax.ppermute(x, 'user', [(i, i ^ cores * k) for i in range(user_ways)])  2.01 us
    ppermute x4, starting transfers between devices, core_peer(): return lax.ppermute(x, 'user', [(i, i ^ 1) for i in range(user_ways)])  1.11 us
    ppermute x4, waiting for transfers between devices, core_peer(): return lax.ppermute(x, 'user', [(i, i ^ 1) for i in range(user_ways)])  0.9 us
  transfers between devices with their start and end apart: 16, of which 8 were waited for; matrix products, arithmetic and copies ran while one was open for 0% of the time, Pallas kernels for 12%

profile of v4, /device:TPU:0, one launch (start us, length us, event | category | flops | bytes accessed | tf_op | source)
XLA Modules:
  0.0 35.8 jit_solution(13221111331785619926)
XLA Ops:
  0.6 1.0 %pack.1 = (bf16[272,128]{1,0:T(8,128)(2,1)S(1)}, bf16[272,128]{1,0:T(8,128)(2,1)S(1)}, bf16[272,128]{1,0:T(8,128)(2,1)S(1)}, f32[16,128]{1,0:T(8,128)S(1)}) custom-call(s32[64]{0:T(128)} %bitcast.23, s32[64]{0:T(128)} %bitcast.24, bf16[256,128]{1,0:T(8,128)(2,1)} %vp_hbm.3, bf16[256,128]{1,0:T(8,128)(2,1)} %vi_hbm.3), custom_call_target="tpu_custom_call" | custom-call | bytes 400000 | tf_op jit(solution)/shard_map/pack/pallas_call | solution.py:34
  1.6 5.1 %collective-permute-start = (bf16[272,128]{1,0:T(8,128)(2,1)S(1)}, bf16[272,128]{1,0:T(8,128)(2,1)S(1)}, u32[]{:S(2)}, u32[]{:S(2)}) collective-permute-start(bf16[272,128]{1,0:T(8,128)(2,1)S(1)} %get-tuple-element.40), channel_id=1, source_target_pairs={{0,3},{1,2},{2,1},{3,0},{4,7},{5,6},{6,5},{7,4},{8,11},{9,10},{10,... | collective-permute-start | bytes 208904 | tf_op jit(solution)/shard_map/ppermute | solution.py:96
  6.7 0.0 collective-permute-start.1
  6.7 0.6 %collective-permute-start.2 = (bf16[272,128]{1,0:T(8,128)(2,1)S(1)}, bf16[272,128]{1,0:T(8,128)(2,1)S(1)}, u32[]{:S(2)}, u32[]{:S(2)}) collective-permute-start(bf16[272,128]{1,0:T(8,128)(2,1)S(1)} %get-tuple-element.42), channel_id=1, source_target_pairs={{0,1},{1,0},{2,3},{3,2},{4,5},{5,4},{6,7},{7,6},{8,9},{9,8},{10,11... | collective-permute-start | bytes 208904 | tf_op jit(solution)/shard_map/ppermute | solution.py:96
  7.4 0.0 copy-start.1
  7.4 3.2 %local_tiles.1 = (f32[16,128,128]{2,1,0:T(8,128)S(1)}, f32[16,128,128]{2,1,0:T(8,128)S(1)}, f32[2,1024,128]{2,1,0:T(8,128)S(1)}, f32[2,256,128]{2,1,0:T(8,128)S(...) custom-call(s32[16]{0:T(128)} %bitcast.15, ...), custom_call_target="tpu_custom_call" | custom-call | flops 268435456 | bytes 8000000 | tf_op jit(solution)/shard_map/local_tiles/pallas_call | solution.py:34
  10.6 0.0 copy-start
  10.6 0.0 collective-permute-done.refs_0_
  10.6 0.1 collective-permute-start.3
  10.7 1.9 %collective-permute-done.1.refs_1_ = bf16[272,128]{1,0:T(8,128)(2,1)S(1)} collective-permute-done((bf16[272,128]{1,0:T(8,128)(2,1)S(1)}, bf16[272,128]{1,0:T(8,128)(2,1)S(1)}, u32[]{:S(2)}, u32[]{:S(2)}) %collective-permute-start.1) | collective-permute-done | bytes 69664 | tf_op jit(solution)/shard_map/ppermute | solution.py:96
  12.6 0.1 collective-permute-start.4
  12.7 0.0 collective-permute-done.2.refs_2_
  12.7 0.5 %collective-permute-start.5 = (bf16[256,128]{1,0:T(8,128)(2,1)S(1)}, bf16[256,128]{1,0:T(8,128)(2,1)S(1)}, u32[]{:S(2)}, u32[]{:S(2)}) collective-permute-start(bf16[256,128]{1,0:T(8,128)(2,1)S(1)} %slice_multiply_fusion), channel_id=1, source_target_pairs={{0,4},{4,0},{8,12},{12,8},{16,20},{20,16},{24,28},{28,24},{1,5},{5... | collective-permute-start | bytes 196616 | tf_op jit(solution)/shard_map/ppermute | solution.py:99
  13.3 0.0 collective-permute-done.3.refs_3_
  13.3 0.7 %collective-permute-done.4.refs_4_ = bf16[256,128]{1,0:T(8,128)(2,1)S(1)} collective-permute-done((bf16[256,128]{1,0:T(8,128)(2,1)S(1)}, bf16[256,128]{1,0:T(8,128)(2,1)S(1)}, u32[]{:S(2)}, u32[]{:S(2)}) %collective-permute-start.4) | collective-permute-done | bytes 65568 | tf_op jit(solution)/shard_map/ppermute | solution.py:99
  14.0 0.2 collective-permute-done.5.refs_5_
  14.2 0.0 copy-done.1
  14.2 0.0 copy-done
  14.2 2.0 %item_tiles.1 = (bf16[1024,128]{1,0:T(8,128)(2,1)S(1)}, f32[1024,128]{1,0:T(8,128)S(1)}, bf16[3,2,256,128]{3,2,1,0:T(8,128)(2,1)S(1)}, bf16[12,128,128]{2,1,0:T(...) custom-call(s32[16]{0:T(128)} %bitcast.16, s32[16]{0:T(128)} %bitcast.19, s32[4]{0:T(128)} %bitcast.22, ...), custom_call_target="tpu_custom_call" | custom-call | flops 201326592 | bytes 4000000 | tf_op jit(solution)/shard_map/item_tiles/pallas_call | solution.py:34
  16.2 0.4 %collective-permute-start.8 = (bf16[1024,128]{1,0:T(8,128)(2,1)S(1)}, bf16[1024,128]{1,0:T(8,128)(2,1)S(1)}, u32[]{:S(2)}, u32[]{:S(2)}) collective-permute-start(bf16[1024,128]{1,0:T(8,128)(2,1)S(1)} %get-tuple-element.54), channel_id=1, source_target_pairs={{0,4},{4,0},{8,12},{12,8},{16,20},{20,16},{24,28},{28,24},{1,5},{5... | collective-permute-start | bytes 786440 | tf_op jit(solution)/shard_map/ppermute | solution.py:99
  16.6 1.1 %user_tiles.1 = (bf16[512,128]{1,0:T(8,128)(2,1)S(1)}, bf16[512,128]{1,0:T(8,128)(2,1)S(1)}, bf16[512,128]{1,0:T(8,128)(2,1)S(1)}, f32[512,128]{1,0:T(8,128)S(1)}) custom-call(s32[16]{0:T(128)} %bitcast.17, s32[16]{0:T(128)} %bitcast.20, f32[16,128,128]{2,1,0:T(8,128)S(1)} %get-tuple-element.34.utile_ref, f32[2,1024,128]{2,1,0:T(8,128)S(1)} %get-tuple-element.35.uacc_in, ...), custom_call_target="tpu_custom_call" | custom-call | flops 100663296 | bytes 4000000 | tf_op jit(solution)/shard_map/user_tiles/pallas_call | solution.py:34
  17.7 2.8 %collective-permute-start.6 = (bf16[512,128]{1,0:T(8,128)(2,1)S(1)}, bf16[512,128]{1,0:T(8,128)(2,1)S(1)}, u32[]{:S(2)}, u32[]{:S(2)}) collective-permute-start(bf16[512,128]{1,0:T(8,128)(2,1)S(1)} %get-tuple-element.51), channel_id=1, source_target_pairs={{0,3},{1,2},{2,1},{3,0},{4,7},{5,6},{6,5},{7,4},{8,11},{9,10},{10,... | collective-permute-start | bytes 393224 | tf_op jit(solution)/shard_map/ppermute | solution.py:96
  20.5 0.0 collective-permute-start.7
  20.5 0.0 collective-permute-done.8.recv_ref
  20.5 0.1 fold_core.1
  20.6 2.5 %collective-permute-start.9 = (bf16[256,128]{1,0:T(8,128)(2,1)S(1)}, bf16[256,128]{1,0:T(8,128)(2,1)S(1)}, u32[]{:S(2)}, u32[]{:S(2)}) collective-permute-start(bf16[256,128]{1,0:T(8,128)(2,1)S(1)} %get-tuple-element.56), channel_id=1, source_target_pairs={{0,24},{4,28},{8,16},{12,20},{16,8},{20,12},{24,0},{28,4},{1,25},{... | collective-permute-start | bytes 196616 | tf_op jit(solution)/shard_map/ppermute | solution.py:102
  23.1 0.5 %collective-permute-start.10 = (bf16[256,128]{1,0:T(8,128)(2,1)S(1)}, bf16[256,128]{1,0:T(8,128)(2,1)S(1)}, u32[]{:S(2)}, u32[]{:S(2)}) collective-permute-start(bf16[256,128]{1,0:T(8,128)(2,1)S(1)} %get-tuple-element.57), channel_id=1, source_target_pairs={{0,16},{4,20},{8,24},{12,28},{16,0},{20,4},{24,8},{28,12},{1,17},{... | collective-permute-start | bytes 196616 | tf_op jit(solution)/shard_map/ppermute | solution.py:102
  23.6 0.5 %collective-permute-start.11 = (bf16[256,128]{1,0:T(8,128)(2,1)S(1)}, bf16[256,128]{1,0:T(8,128)(2,1)S(1)}, u32[]{:S(2)}, u32[]{:S(2)}) collective-permute-start(bf16[256,128]{1,0:T(8,128)(2,1)S(1)} %get-tuple-element.58), channel_id=1, source_target_pairs={{0,8},{4,12},{8,0},{12,4},{16,24},{20,28},{24,16},{28,20},{1,9},{5... | collective-permute-start | bytes 196616 | tf_op jit(solution)/shard_map/ppermute | solution.py:102
  24.1 1.7 %collective-permute-done.9.refs_0_ = bf16[256,128]{1,0:T(8,128)(2,1)S(1)} collective-permute-done((bf16[256,128]{1,0:T(8,128)(2,1)S(1)}, bf16[256,128]{1,0:T(8,128)(2,1)S(1)}, u32[]{:S(2)}, u32[]{:S(2)}) %collective-permute-start.9) | collective-permute-done | bytes 65568 | tf_op jit(solution)/shard_map/ppermute | solution.py:102
  25.8 1.7 %collective-permute-start.12 = (bf16[512,128]{1,0:T(8,128)(2,1)S(1)}, bf16[512,128]{1,0:T(8,128)(2,1)S(1)}, u32[]{:S(2)}, u32[]{:S(2)}) collective-permute-start(bf16[512,128]{1,0:T(8,128)(2,1)S(1)} %get-tuple-element.60), channel_id=1, source_target_pairs={{0,1},{1,0},{2,3},{3,2},{4,5},{5,4},{6,7},{7,6},{8,9},{9,8},{10,11... | collective-permute-start | bytes 393224 | tf_op jit(solution)/shard_map/ppermute | solution.py:96
  27.6 0.0 collective-permute-done.10.refs_1_
  27.6 0.3 collective-permute-done.11.refs_2_
  27.9 2.5 %collective-permute-start.13 = (bf16[64,128]{1,0:T(8,128)(2,1)S(1)}, bf16[64,128]{1,0:T(8,128)(2,1)S(1)}, u32[]{:S(2)}, u32[]{:S(2)}) collective-permute-start(bf16[64,128]{1,0:T(8,128)(2,1)S(1)} %get-tuple-element.61), channel_id=1, source_target_pairs={{0,3},{1,2},{2,1},{3,0},{4,7},{5,6},{6,5},{7,4},{8,11},{9,10},{10,... | collective-permute-start | bytes 49160 | tf_op jit(solution)/shard_map/ppermute | solution.py:96
  30.4 0.7 %collective-permute-start.14 = (bf16[64,128]{1,0:T(8,128)(2,1)S(1)}, bf16[64,128]{1,0:T(8,128)(2,1)S(1)}, u32[]{:S(2)}, u32[]{:S(2)}) collective-permute-start(bf16[64,128]{1,0:T(8,128)(2,1)S(1)} %get-tuple-element.62), channel_id=1, source_target_pairs={{0,2},{1,3},{2,0},{3,1},{4,6},{5,7},{6,4},{7,5},{8,10},{9,11},{10,... | collective-permute-start | bytes 49160 | tf_op jit(solution)/shard_map/ppermute | solution.py:96
  31.1 0.0 collective-permute-done.6.refs_0_
  31.1 1.3 %collective-permute-start.15 = (bf16[64,128]{1,0:T(8,128)(2,1)S(1)}, bf16[64,128]{1,0:T(8,128)(2,1)S(1)}, u32[]{:S(2)}, u32[]{:S(2)}) collective-permute-start(bf16[64,128]{1,0:T(8,128)(2,1)S(1)} %get-tuple-element.63), channel_id=1, source_target_pairs={{0,1},{1,0},{2,3},{3,2},{4,5},{5,4},{6,7},{7,6},{8,9},{9,8},{10,11... | collective-permute-start | bytes 49160 | tf_op jit(solution)/shard_map/ppermute | solution.py:96
  32.3 0.3 collective-permute-done.7.refs_1_
  32.7 1.3 %collective-permute-done.12.refs_0_ = bf16[512,128]{1,0:T(8,128)(2,1)S(1)} collective-permute-done((bf16[512,128]{1,0:T(8,128)(2,1)S(1)}, bf16[512,128]{1,0:T(8,128)(2,1)S(1)}, u32[]{:S(2)}, u32[]{:S(2)}) %collective-permute-start.12) | collective-permute-done | bytes 131104 | tf_op jit(solution)/shard_map/ppermute | solution.py:96
  33.9 0.0 collective-permute-done.13.refs_1_
  33.9 1.1 %collective-permute-done.14.refs_2_ = bf16[64,128]{1,0:T(8,128)(2,1)S(1)} collective-permute-done((bf16[64,128]{1,0:T(8,128)(2,1)S(1)}, bf16[64,128]{1,0:T(8,128)(2,1)S(1)}, u32[]{:S(2)}, u32[]{:S(2)}) %collective-permute-start.14) | collective-permute-done | bytes 16416 | tf_op jit(solution)/shard_map/ppermute | solution.py:96
  35.0 0.0 collective-permute-done.15.refs_3_
  35.0 0.7 %finish.1 = (f32[256,128]{1,0:T(8,128)}, f32[256,128]{1,0:T(8,128)}, f32[32,128]{1,0:T(8,128)}, f32[32,128]{1,0:T(8,128)}) custom-call(f32[512,128]{1,0:T(8,128)S(1)} %sum_users.1.user_ref, f32[64,128]{1,0:T(8,128)S(1)} %get-tuple-element.59.item_ref, bf16[512,128]{1,0:T(8,128)(2,1)S(1)} %collective-permute-done.12.refs_0_, ...), custom_call_target="tpu_custom_call" | custom-call | bytes 1000 | tf_op jit(solution)/shard_map/finish/pallas_call | solution.py:34
  (8 shorter events, 0.1 us)
Async XLA Ops:
  1.6 9.0 %collective-permute-start = (bf16[272,128]{1,0:T(8,128)(2,1)S(1)}, bf16[272,128]{1,0:T(8,128)(2,1)S(1)}, u32[]{:S(2)}, u32[]{:S(2)}) collective-permute-start(bf16[272,128]{1,0:T(8,128)(2,1)S(1)} %get-tuple-element.40), channel_id=1, source_target_pairs={{0,3},{1,2},{2,1},{3,0},{4,7},{5,6},{6,5},{7,4},{8,11},{9,10},{10,... | collective-permute-start | bytes 208904 | tf_op jit(solution)/shard_map/ppermute | solution.py:96
  6.7 5.9 %collective-permute-start.1 = (bf16[272,128]{1,0:T(8,128)(2,1)S(1)}, bf16[272,128]{1,0:T(8,128)(2,1)S(1)}, u32[]{:S(2)}, u32[]{:S(2)}) collective-permute-start(bf16[272,128]{1,0:T(8,128)(2,1)S(1)} %get-tuple-element.41), channel_id=1, source_target_pairs={{0,2},{1,3},{2,0},{3,1},{4,6},{5,7},{6,4},{7,5},{8,10},{9,11},{10,... | collective-permute-start | bytes 208904 | tf_op jit(solution)/shard_map/ppermute | solution.py:96
  6.7 6.0 %collective-permute-start.2 = (bf16[272,128]{1,0:T(8,128)(2,1)S(1)}, bf16[272,128]{1,0:T(8,128)(2,1)S(1)}, u32[]{:S(2)}, u32[]{:S(2)}) collective-permute-start(bf16[272,128]{1,0:T(8,128)(2,1)S(1)} %get-tuple-element.42), channel_id=1, source_target_pairs={{0,1},{1,0},{2,3},{3,2},{4,5},{5,4},{6,7},{7,6},{8,9},{9,8},{10,11... | collective-permute-start | bytes 208904 | tf_op jit(solution)/shard_map/ppermute | solution.py:96
  7.4 6.8 %copy-start.1 = (bf16[1024,128]{1,0:T(8,128)(2,1)S(1)}, bf16[1024,128]{1,0:T(8,128)(2,1)}, u32[]{:S(2)}) copy-start(bf16[1024,128]{1,0:T(8,128)(2,1)} %ux_ref.1) | copy-start | bytes 786436
  10.6 3.6 %copy-start = (bf16[1024,128]{1,0:T(8,128)(2,1)S(1)}, bf16[1024,128]{1,0:T(8,128)(2,1)}, u32[]{:S(2)}) copy-start(bf16[1024,128]{1,0:T(8,128)(2,1)} %up_ref.1) | copy-start | bytes 786436
  10.6 2.7 %collective-permute-start.3 = (bf16[256,128]{1,0:T(8,128)(2,1)S(1)}, bf16[256,128]{1,0:T(8,128)(2,1)S(1)}, u32[]{:S(2)}, u32[]{:S(2)}) collective-permute-start(bf16[256,128]{1,0:T(8,128)(2,1)S(1)} %slice_multiply_fusion.2), channel_id=1, source_target_pairs={{0,4},{4,0},{8,12},{12,8},{16,20},{20,16},{24,28},{28,24},{1,5},{5... | collective-permute-start | bytes 196616 | tf_op jit(solution)/shard_map/ppermute | solution.py:99
  12.6 1.3 %collective-permute-start.4 = (bf16[256,128]{1,0:T(8,128)(2,1)S(1)}, bf16[256,128]{1,0:T(8,128)(2,1)S(1)}, u32[]{:S(2)}, u32[]{:S(2)}) collective-permute-start(bf16[256,128]{1,0:T(8,128)(2,1)S(1)} %slice_multiply_fusion.1), channel_id=1, source_target_pairs={{0,4},{4,0},{8,12},{12,8},{16,20},{20,16},{24,28},{28,24},{1,5},{5... | collective-permute-start | bytes 196616 | tf_op jit(solution)/shard_map/ppermute | solution.py:99
  12.7 1.5 %collective-permute-start.5 = (bf16[256,128]{1,0:T(8,128)(2,1)S(1)}, bf16[256,128]{1,0:T(8,128)(2,1)S(1)}, u32[]{:S(2)}, u32[]{:S(2)}) collective-permute-start(bf16[256,128]{1,0:T(8,128)(2,1)S(1)} %slice_multiply_fusion), channel_id=1, source_target_pairs={{0,4},{4,0},{8,12},{12,8},{16,20},{20,16},{24,28},{28,24},{1,5},{5... | collective-permute-start | bytes 196616 | tf_op jit(solution)/shard_map/ppermute | solution.py:99
  16.2 4.3 %collective-permute-start.8 = (bf16[1024,128]{1,0:T(8,128)(2,1)S(1)}, bf16[1024,128]{1,0:T(8,128)(2,1)S(1)}, u32[]{:S(2)}, u32[]{:S(2)}) collective-permute-start(bf16[1024,128]{1,0:T(8,128)(2,1)S(1)} %get-tuple-element.54), channel_id=1, source_target_pairs={{0,4},{4,0},{8,12},{12,8},{16,20},{20,16},{24,28},{28,24},{1,5},{5... | collective-permute-start | bytes 786440 | tf_op jit(solution)/shard_map/ppermute | solution.py:99
  17.7 13.4 %collective-permute-start.6 = (bf16[512,128]{1,0:T(8,128)(2,1)S(1)}, bf16[512,128]{1,0:T(8,128)(2,1)S(1)}, u32[]{:S(2)}, u32[]{:S(2)}) collective-permute-start(bf16[512,128]{1,0:T(8,128)(2,1)S(1)} %get-tuple-element.51), channel_id=1, source_target_pairs={{0,3},{1,2},{2,1},{3,0},{4,7},{5,6},{6,5},{7,4},{8,11},{9,10},{10,... | collective-permute-start | bytes 393224 | tf_op jit(solution)/shard_map/ppermute | solution.py:96
  20.5 12.1 %collective-permute-start.7 = (bf16[512,128]{1,0:T(8,128)(2,1)S(1)}, bf16[512,128]{1,0:T(8,128)(2,1)S(1)}, u32[]{:S(2)}, u32[]{:S(2)}) collective-permute-start(bf16[512,128]{1,0:T(8,128)(2,1)S(1)} %get-tuple-element.52), channel_id=1, source_target_pairs={{0,2},{1,3},{2,0},{3,1},{4,6},{5,7},{6,4},{7,5},{8,10},{9,11},{10,... | collective-permute-start | bytes 393224 | tf_op jit(solution)/shard_map/ppermute | solution.py:96
  20.6 5.3 %collective-permute-start.9 = (bf16[256,128]{1,0:T(8,128)(2,1)S(1)}, bf16[256,128]{1,0:T(8,128)(2,1)S(1)}, u32[]{:S(2)}, u32[]{:S(2)}) collective-permute-start(bf16[256,128]{1,0:T(8,128)(2,1)S(1)} %get-tuple-element.56), channel_id=1, source_target_pairs={{0,24},{4,28},{8,16},{12,20},{16,8},{20,12},{24,0},{28,4},{1,25},{... | collective-permute-start | bytes 196616 | tf_op jit(solution)/shard_map/ppermute | solution.py:102
  23.1 4.5 %collective-permute-start.10 = (bf16[256,128]{1,0:T(8,128)(2,1)S(1)}, bf16[256,128]{1,0:T(8,128)(2,1)S(1)}, u32[]{:S(2)}, u32[]{:S(2)}) collective-permute-start(bf16[256,128]{1,0:T(8,128)(2,1)S(1)} %get-tuple-element.57), channel_id=1, source_target_pairs={{0,16},{4,20},{8,24},{12,28},{16,0},{20,4},{24,8},{28,12},{1,17},{... | collective-permute-start | bytes 196616 | tf_op jit(solution)/shard_map/ppermute | solution.py:102
  23.6 4.3 %collective-permute-start.11 = (bf16[256,128]{1,0:T(8,128)(2,1)S(1)}, bf16[256,128]{1,0:T(8,128)(2,1)S(1)}, u32[]{:S(2)}, u32[]{:S(2)}) collective-permute-start(bf16[256,128]{1,0:T(8,128)(2,1)S(1)} %get-tuple-element.58), channel_id=1, source_target_pairs={{0,8},{4,12},{8,0},{12,4},{16,24},{20,28},{24,16},{28,20},{1,9},{5... | collective-permute-start | bytes 196616 | tf_op jit(solution)/shard_map/ppermute | solution.py:102
  25.8 8.1 %collective-permute-start.12 = (bf16[512,128]{1,0:T(8,128)(2,1)S(1)}, bf16[512,128]{1,0:T(8,128)(2,1)S(1)}, u32[]{:S(2)}, u32[]{:S(2)}) collective-permute-start(bf16[512,128]{1,0:T(8,128)(2,1)S(1)} %get-tuple-element.60), channel_id=1, source_target_pairs={{0,1},{1,0},{2,3},{3,2},{4,5},{5,4},{6,7},{7,6},{8,9},{9,8},{10,11... | collective-permute-start | bytes 393224 | tf_op jit(solution)/shard_map/ppermute | solution.py:96
  27.9 6.0 %collective-permute-start.13 = (bf16[64,128]{1,0:T(8,128)(2,1)S(1)}, bf16[64,128]{1,0:T(8,128)(2,1)S(1)}, u32[]{:S(2)}, u32[]{:S(2)}) collective-permute-start(bf16[64,128]{1,0:T(8,128)(2,1)S(1)} %get-tuple-element.61), channel_id=1, source_target_pairs={{0,3},{1,2},{2,1},{3,0},{4,7},{5,6},{6,5},{7,4},{8,11},{9,10},{10,... | collective-permute-start | bytes 49160 | tf_op jit(solution)/shard_map/ppermute | solution.py:96
  30.4 4.6 %collective-permute-start.14 = (bf16[64,128]{1,0:T(8,128)(2,1)S(1)}, bf16[64,128]{1,0:T(8,128)(2,1)S(1)}, u32[]{:S(2)}, u32[]{:S(2)}) collective-permute-start(bf16[64,128]{1,0:T(8,128)(2,1)S(1)} %get-tuple-element.62), channel_id=1, source_target_pairs={{0,2},{1,3},{2,0},{3,1},{4,6},{5,7},{6,4},{7,5},{8,10},{9,11},{10,... | collective-permute-start | bytes 49160 | tf_op jit(solution)/shard_map/ppermute | solution.py:96
  31.1 3.9 %collective-permute-start.15 = (bf16[64,128]{1,0:T(8,128)(2,1)S(1)}, bf16[64,128]{1,0:T(8,128)(2,1)S(1)}, u32[]{:S(2)}, u32[]{:S(2)}) collective-permute-start(bf16[64,128]{1,0:T(8,128)(2,1)S(1)} %get-tuple-element.63), channel_id=1, source_target_pairs={{0,1},{1,0},{2,3},{3,2},{4,5},{5,4},{6,7},{7,6},{8,9},{9,8},{10,11... | collective-permute-start | bytes 49160 | tf_op jit(solution)/shard_map/ppermute | solution.py:96

commit v5 on v4

--- a/solution.py
+++ b/solution.py
@@ -247,118 +247,95 @@
 
     slots = peers * obs_slots
 
-    def items(ou_hbm, oi_hbm, oc_hbm, up_ref, ux_ref, count_ref, itile_ref, iacc_in, w_ref, *refs):
+    near = range(peers)
+
+    def start_ids(sources, targets, sems):
+        copies = [pltpu.make_async_copy(a, b, sems.at[n]) for n, (a, b) in enumerate(zip(sources, targets))]
+        for c in copies:
+            c.start()
+        return copies
+
+    def unpack(vbuf, recv, swap):
+        core = lax.rem(lax.axis_index("user"), cores)
+        mine = pl.multiple_of(core * half, half)
+        other = pl.multiple_of((1 - core) * half, half)
+        for m in range(2):
+            vbuf[m, pl.ds(mine, half)] = recv[m * half : (m + 1) * half]
+            vbuf[m, pl.ds(other, half)] = swap[m * half : (m + 1) * half]
+
+    def tiles(k, ou_ref, oi_ref, oc_ref, up_ref, ux_ref, w_ref, vbuf, gbuf, hbuf, first):
+        places = []
+        group = lax.bitwise_xor(lax.axis_index("item"), k + 1)
+        for s in range(obs_slots):
+            at = group * obs_slots + s
+            urows = pl.ds(pl.multiple_of(ou_ref[at] * tile, tile), tile)
+            brows = pl.ds(pl.multiple_of(oi_ref[at] * tile, tile), tile)
+            used = jnp.where(s < oc_ref[group], 1.0, 0.0)
+            logits = rows_by_cols(up_ref[urows], vbuf[0, brows])
+            imputed = rows_by_cols(ux_ref[urows], vbuf[1, brows])
+            gbuf[first + s], hbuf[first + s] = observed(logits, imputed, w_ref[at], used)
+            places.append((urows, brows, oi_ref[at] * tile, first + s))
+        return places
+
+    id_args = (obs_user, obs_item, obs_count)
+    id_scratch = tuple(pltpu.SMEM(x.shape, x.dtype) for x in id_args) + (pltpu.SemaphoreType.DMA((3,)),)
+    def other_tiles(
+        ou_hbm, oi_hbm, oc_hbm, up_ref, ux_ref, count_ref, itile_ref, iacc_in, w_ref, utile_ref, uacc_in, *refs
+    ):
         recv = refs[:peers][::-1]
         swap = refs[peers : 2 * peers][::-1]
-        send, keep, vbuf, gbuf, hbuf, total_ref = refs[2 * peers : 2 * peers + 6]
-        ou_ref, oi_ref, oc_ref, sems, iacc = refs[2 * peers + 6 :]
-        copies = [
-            pltpu.make_async_copy(ou_hbm, ou_ref, sems.at[0]),
-            pltpu.make_async_copy(oi_hbm, oi_ref, sems.at[1]),
-            pltpu.make_async_copy(oc_hbm, oc_ref, sems.at[2]),
-        ]
-        for c in copies:
-            c.start()
+        send, keep, *outs = refs[2 * peers : 3 * peers + 3]
+        ou_ref, oi_ref, oc_ref, sems, vbuf, gbuf, hbuf, iacc, uacc = refs[3 * peers + 3 :]
+        copies = start_ids((ou_hbm, oi_hbm, oc_hbm), (ou_ref, oi_ref, oc_ref), sems)
         pos = lax.axis_index("item")
         user = lax.axis_index("user")
         core = lax.rem(user, cores)
         chip = lax.div(user, cores)
-        mine = pl.multiple_of(core * half, half)
-        other = pl.multiple_of((1 - core) * half, half)
         count = count_ref[...]
-        for k in range(peers):
-            count = count + recv[k][2 * half :].astype(f32)
-            for m in range(2):
-                vbuf[k, m, pl.ds(mine, half)] = recv[k][m * half : (m + 1) * half]
-                vbuf[k, m, pl.ds(other, half)] = swap[k][m * half : (m + 1) * half]
-        total_ref[...] = count
-        own = pl.ds(pl.multiple_of(pos * shard_rows, shard_rows), shard_rows)
-        iacc[...] = jnp.zeros_like(iacc)
-        iacc[1, own] = iacc_in[1]
+        for r in recv:
+            count = count + r[2 * half :].astype(f32)
+        for k in near:
+            unpack(vbuf.at[k], recv[k], swap[k])
+        iacc[1, :shard_rows] = iacc_in[1]
         for b in range(item_blocks):
-            total = iacc_in[0, b * tile : (b + 1) * tile]
+            rows = pl.ds(b * tile, tile)
+            total = iacc_in[0, rows]
             for u in range(user_blocks):
                 t = u * item_blocks + b
                 total = total + itile_ref[t] * count[t : t + 1]
-            iacc[0, pl.ds(pl.multiple_of(pos * shard_rows + b * tile, tile), tile)] = total
+            iacc[0, rows] = total
+        for u in range(user_blocks):
+            rows = pl.ds(u * tile, tile)
+            total = uacc_in[0, rows]
+            for b in range(item_blocks):
+                t = u * item_blocks + b
+                total = total + utile_ref[t] * count[t : t + 1]
+            uacc[0, rows] = total
+        uacc[1] = uacc_in[1]
+        for m in range(2):
+            iacc[m, shard_rows:] = jnp.zeros((peers * shard_rows, rank), f32)
         for c in copies:
             c.wait()
         places = []
-        for k in range(peers):
-            group = lax.bitwise_xor(pos, k + 1)
-            for s in range(obs_slots):
-                at = group * obs_slots + s
-                urows = pl.ds(pl.multiple_of(ou_ref[at] * tile, tile), tile)
-                brows = pl.ds(pl.multiple_of(oi_ref[at] * tile, tile), tile)
-                irows = pl.ds(pl.multiple_of(group * shard_rows + oi_ref[at] * tile, tile), tile)
-                places.append((urows, irows))
-                used = jnp.where(s < oc_ref[group], 1.0, 0.0)
-                logits = rows_by_cols(up_ref[urows], vbuf[k, 0, brows])
-                imputed = rows_by_cols(ux_ref[urows], vbuf[k, 1, brows])
-                t = k * obs_slots + s
-                gbuf[t], hbuf[t] = observed(logits, imputed, w_ref[at], used)
-        for t, (urows, irows) in enumerate(places):
+        for k in near:
+            for p in tiles(k, ou_ref, oi_ref, oc_ref, up_ref, ux_ref, w_ref, vbuf.at[k], gbuf, hbuf, k * obs_slots):
+                places.append((k, p))
+        for k, (urows, _, block, t) in places:
+            irows = pl.ds(pl.multiple_of((k + 1) * shard_rows + block, tile), tile)
             iacc[0, irows] += over_rows(gbuf[t], up_ref[urows])
             iacc[1, irows] += over_rows(hbuf[t], ux_ref[urows])
+        for k, (urows, brows, _, t) in places:
+            uacc[0, urows] += plain(gbuf[t], vbuf[k, 0, brows])
+            uacc[1, urows] += plain(hbuf[t], vbuf[k, 1, brows])
         for q in range(chips):
             for r in range(item_ways):
                 for m in range(2):
                     at = ((q * item_ways + r) * 2 + m) * item_share
-                    base = lax.bitwise_xor(pos, r) * shard_rows + lax.bitwise_xor(chip, q) * cores * item_share
+                    base = r * shard_rows + lax.bitwise_xor(chip, q) * cores * item_share
                     to_keep = pl.ds(pl.multiple_of(base + core * item_share, item_share), item_share)
                     to_send = pl.ds(pl.multiple_of(base + (1 - core) * item_share, item_share), item_share)
                     keep[at : at + item_share] = iacc[m, to_keep]
-                    send[at : at + item_share] = iacc[m, to_send].astype(bf16)
-
-    core_rows = 2 * item_ways * chips * item_share
-    id_args = (obs_user, obs_item, obs_count)
-    core_send, core_keep, vbuf, gbuf, hbuf, count = call(
-        items,
-        "item_tiles",
-        (
-            shape((core_rows, rank), bf16),
-            shape((core_rows, rank), f32),
-            shape((peers, 2, shard_rows, rank), bf16),
-            shape((slots, tile, tile), bf16),
-            shape((slots, tile, tile), bf16),
-            shape((pairs, rank), f32),
-        ),
-        [HBM, HBM, HBM] + [VM] * (6 + 2 * peers),
-        (*in_hbm(id_args), user_pred, user_imp, own_count, itile, iacc, weights, *received[::-1], *swapped[::-1]),
-        (4 * slots * 2 * tile**3, 4000000, 2 * slots * tile * tile),
-        tuple(pltpu.SMEM(x.shape, x.dtype) for x in id_args)
-        + (pltpu.SemaphoreType.DMA((3,)), pltpu.VMEM((2, item_ways * shard_rows, rank), f32)),
-    )
-
-    def users(ou_hbm, oi_hbm, utile_ref, uacc_in, count_ref, vbuf, gbuf, hbuf, *refs):
-        outs = refs[: peers + 1]
-        ou_ref, oi_ref, sems, uacc = refs[peers + 1 :]
-        copies = [
-            pltpu.make_async_copy(ou_hbm, ou_ref, sems.at[0]),
-            pltpu.make_async_copy(oi_hbm, oi_ref, sems.at[1]),
-        ]
-        for c in copies:
-            c.start()
-        pos = lax.axis_index("item")
-        count = count_ref[...]
-        for u in range(user_blocks):
-            total = uacc_in[0, u * tile : (u + 1) * tile]
-            for b in range(item_blocks):
-                t = u * item_blocks + b
-                total = total + utile_ref[t] * count[t : t + 1]
-            uacc[0, u * tile : (u + 1) * tile] = total
-        uacc[1] = uacc_in[1]
-        for c in copies:
-            c.wait()
-        for k in range(peers):
-            group = lax.bitwise_xor(pos, k + 1)
-            for s in range(obs_slots):
-                at = group * obs_slots + s
-                t = k * obs_slots + s
-                urows = pl.ds(pl.multiple_of(ou_ref[at] * tile, tile), tile)
-                brows = pl.ds(pl.multiple_of(oi_ref[at] * tile, tile), tile)
-                uacc[0, urows] += plain(gbuf[t], vbuf[k, 0, brows])
-                uacc[1, urows] += plain(hbuf[t], vbuf[k, 1, brows])
+                    send[at : at + item_share] = iacc[m, to_send]
         for k in range(item_ways):
             rows = pl.ds(pl.multiple_of(lax.bitwise_xor(pos, k) * share, share), share)
             for m in range(2):
@@ -368,15 +345,27 @@
                 else:
                     outs[k - 1][m * share : (m + 1) * share] = part.astype(bf16)
 
-    results = call(
-        users,
-        "user_tiles",
-        tuple(shape((2 * share, rank), bf16) for _ in range(peers)) + (shape((2 * share, rank), f32),),
-        [HBM, HBM] + [VM] * 6,
-        (*in_hbm(id_args[:2]), utile, uacc, count, vbuf, gbuf, hbuf),
-        (2 * slots * 2 * tile**3, 4000000, 0),
-        tuple(pltpu.SMEM(x.shape, x.dtype) for x in id_args[:2])
-        + (pltpu.SemaphoreType.DMA((2,)), pltpu.VMEM((2, user_rows, rank), f32)),
+    core_rows = 2 * item_ways * chips * item_share
+    core_send, core_keep, *results = call(
+        other_tiles,
+        "other_tiles",
+        (shape((core_rows, rank), f32),) * 2
+        + tuple(shape((2 * share, rank), bf16) for _ in range(peers))
+        + (shape((2 * share, rank), f32),),
+        [HBM, HBM, HBM] + [VM] * (8 + 2 * peers),
+        (
+            *in_hbm(id_args), user_pred, user_imp, own_count, itile, iacc, weights, utile, uacc,
+            *received[::-1], *swapped[::-1],
+        ),
+        (6 * slots * 2 * tile**3, 4000000, 2 * slots * tile * tile),
+        id_scratch
+        + (
+            pltpu.VMEM((peers, 2, shard_rows, rank), bf16),
+            pltpu.VMEM((slots, tile, tile), bf16),
+            pltpu.VMEM((slots, tile, tile), bf16),
+            pltpu.VMEM((2, item_ways * shard_rows, rank), f32),
+            pltpu.VMEM((2, user_rows, rank), f32),
+        ),
     )
     user_own = results[peers]
     core_recv = core_peer(core_send)
@@ -384,17 +373,17 @@
 
     chip_rows = 2 * item_ways * item_share
 
-    def fold_core(keep_ref, recv_ref, after_ref, *outs):
+    def fold_core(keep_ref, recv_ref, *outs):
         for k in range(chips):
             rows = pl.ds(k * chip_rows, chip_rows)
-            outs[k][...] = (keep_ref[rows] + recv_ref[rows].astype(f32)).astype(outs[k].dtype)
+            outs[k][...] = (keep_ref[rows] + recv_ref[rows]).astype(outs[k].dtype)
 
     folded = call(
         fold_core,
         "fold_core",
         (shape((chip_rows, rank), f32),) + tuple(shape((chip_rows, rank), bf16) for _ in range(chips - 1)),
-        [VM, VM, VM],
-        (core_keep, core_recv, user_own),
+        [VM, VM],
+        (core_keep, core_recv),
         (0, 1000, 0),
     )
     chip_recv = [chip_peer(folded[k], k) for k in reversed(range(1, chips))]

time: 36 us -> 35.1 us (0.975)
  Pallas kernels: 8.1 us -> 7.28 us
    pallas_call x8 -> x7, Pallas kernels: 8.1 us -> 7.28 us  [call(): pl.pallas_call(body, out_shape=out_shapes, in_specs=specs, out_specs=tupl...]
  transfers between devices with their start and end apart: 16 -> 16, of which waited for: 8 -> 8; matrix products, arithmetic and copies ran while one was open for 0% -> 0% of each run, Pallas kernels for 12% -> 10%
where the time goes in v5:
time: 35.1 us; the launch traced here: 34.9 us
  starting transfers between devices  19.3 us (55%)
  waiting for transfers between devices  7.47 us (21%)
  Pallas kernels  7.28 us (21%)
  between operations  0.76 us (2%)
    ppermute x9, starting transfers between devices, item_peer(): return lax.ppermute(x, 'item', [(i, i ^ k) for i in range(item_ways)])  14.7 us
    pallas_call x7, Pallas kernels, call(): pl.pallas_call(body, out_shape=out_shapes, in_specs=specs, out_specs=tupl...  7.28 us
    ppermute x9, waiting for transfers between devices, item_peer(): return lax.ppermute(x, 'item', [(i, i ^ k) for i in range(item_ways)])  4.56 us
    ppermute x3, starting transfers between devices, chip_peer(): lax.ppermute(x, 'user', [(i, i ^ cores * k) for i in range(user_ways)])  3.55 us
    ppermute x3, waiting for transfers between devices, chip_peer(): lax.ppermute(x, 'user', [(i, i ^ cores * k) for i in range(user_ways)])  2.01 us
    ppermute x4, starting transfers between devices, core_peer(): return lax.ppermute(x, 'user', [(i, i ^ 1) for i in range(user_ways)])  1.11 us
    ppermute x4, waiting for transfers between devices, core_peer(): return lax.ppermute(x, 'user', [(i, i ^ 1) for i in range(user_ways)])  0.9 us
  transfers between devices with their start and end apart: 16, of which 8 were waited for; matrix products, arithmetic and copies ran while one was open for 0% of the time, Pallas kernels for 10%

profile of v5, /device:TPU:0, one launch (start us, length us, event | category | flops | bytes accessed | tf_op | source)
XLA Modules:
  0.0 34.9 jit_solution(18116311262700974071)
XLA Ops:
  0.6 1.0 %pack.1 = (bf16[272,128]{1,0:T(8,128)(2,1)S(1)}, bf16[272,128]{1,0:T(8,128)(2,1)S(1)}, bf16[272,128]{1,0:T(8,128)(2,1)S(1)}, f32[16,128]{1,0:T(8,128)S(1)}) custom-call(s32[64]{0:T(128)} %bitcast.21, s32[64]{0:T(128)} %bitcast.22, bf16[256,128]{1,0:T(8,128)(2,1)} %vp_hbm.3, bf16[256,128]{1,0:T(8,128)(2,1)} %vi_hbm.3), custom_call_target="tpu_custom_call" | custom-call | bytes 400000 | tf_op jit(solution)/shard_map/pack/pallas_call | solution.py:34
  1.6 5.1 %collective-permute-start = (bf16[272,128]{1,0:T(8,128)(2,1)S(1)}, bf16[272,128]{1,0:T(8,128)(2,1)S(1)}, u32[]{:S(2)}, u32[]{:S(2)}) collective-permute-start(bf16[272,128]{1,0:T(8,128)(2,1)S(1)} %get-tuple-element.36), channel_id=1, source_target_pairs={{0,3},{1,2},{2,1},{3,0},{4,7},{5,6},{6,5},{7,4},{8,11},{9,10},{10,... | collective-permute-start | bytes 208904 | tf_op jit(solution)/shard_map/ppermute | solution.py:96
  6.7 0.0 collective-permute-start.1
  6.7 0.6 %collective-permute-start.2 = (bf16[272,128]{1,0:T(8,128)(2,1)S(1)}, bf16[272,128]{1,0:T(8,128)(2,1)S(1)}, u32[]{:S(2)}, u32[]{:S(2)}) collective-permute-start(bf16[272,128]{1,0:T(8,128)(2,1)S(1)} %get-tuple-element.38), channel_id=1, source_target_pairs={{0,1},{1,0},{2,3},{3,2},{4,5},{5,4},{6,7},{7,6},{8,9},{9,8},{10,11... | collective-permute-start | bytes 208904 | tf_op jit(solution)/shard_map/ppermute | solution.py:96
  7.4 0.0 copy-start.1
  7.4 3.2 %local_tiles.1 = (f32[16,128,128]{2,1,0:T(8,128)S(1)}, f32[16,128,128]{2,1,0:T(8,128)S(1)}, f32[2,1024,128]{2,1,0:T(8,128)S(1)}, f32[2,256,128]{2,1,0:T(8,128)S(...) custom-call(s32[16]{0:T(128)} %bitcast.15, ...), custom_call_target="tpu_custom_call" | custom-call | flops 268435456 | bytes 8000000 | tf_op jit(solution)/shard_map/local_tiles/pallas_call | solution.py:34
  10.6 0.0 copy-start
  10.6 0.0 collective-permute-done.refs_0_
  10.6 0.1 collective-permute-start.3
  10.7 1.9 %collective-permute-done.1.refs_1_ = bf16[272,128]{1,0:T(8,128)(2,1)S(1)} collective-permute-done((bf16[272,128]{1,0:T(8,128)(2,1)S(1)}, bf16[272,128]{1,0:T(8,128)(2,1)S(1)}, u32[]{:S(2)}, u32[]{:S(2)}) %collective-permute-start.1) | collective-permute-done | bytes 69664 | tf_op jit(solution)/shard_map/ppermute | solution.py:96
  12.6 0.1 collective-permute-start.4
  12.7 0.0 collective-permute-done.2.refs_2_
  12.7 0.5 %collective-permute-start.5 = (bf16[256,128]{1,0:T(8,128)(2,1)S(1)}, bf16[256,128]{1,0:T(8,128)(2,1)S(1)}, u32[]{:S(2)}, u32[]{:S(2)}) collective-permute-start(bf16[256,128]{1,0:T(8,128)(2,1)S(1)} %slice_multiply_fusion), channel_id=1, source_target_pairs={{0,4},{4,0},{8,12},{12,8},{16,20},{20,16},{24,28},{28,24},{1,5},{5... | collective-permute-start | bytes 196616 | tf_op jit(solution)/shard_map/ppermute | solution.py:99
  13.3 0.0 collective-permute-done.3.refs_3_
  13.3 0.7 %collective-permute-done.4.refs_4_ = bf16[256,128]{1,0:T(8,128)(2,1)S(1)} collective-permute-done((bf16[256,128]{1,0:T(8,128)(2,1)S(1)}, bf16[256,128]{1,0:T(8,128)(2,1)S(1)}, u32[]{:S(2)}, u32[]{:S(2)}) %collective-permute-start.4) | collective-permute-done | bytes 65568 | tf_op jit(solution)/shard_map/ppermute | solution.py:99
  14.0 0.2 collective-permute-done.5.refs_5_
  14.2 0.0 copy-done.1
  14.2 0.0 copy-done
  14.2 2.3 %other_tiles.1 = (f32[1024,128]{1,0:T(8,128)S(1)}, f32[1024,128]{1,0:T(8,128)S(1)}, bf16[512,128]{1,0:T(8,128)(2,1)S(1)}, bf16[512,128]{1,0:T(8,128)(2,1)S(1)}, ...) custom-call(s32[16]{0:T(128)} %bitcast.16, s32[16]{0:T(128)} %bitcast.18, s32[4]{0:T(128)} %bitcast.20, ...), custom_call_target="tpu_custom_call" | custom-call | flops 301989888 | bytes 4000000 | tf_op jit(solution)/shard_map/other_tiles/pallas_call | solution.py:34
  16.5 0.4 %collective-permute-start.8 = (f32[1024,128]{1,0:T(8,128)S(1)}, f32[1024,128]{1,0:T(8,128)S(1)}, u32[]{:S(2)}, u32[]{:S(2)}) collective-permute-start(f32[1024,128]{1,0:T(8,128)S(1)} %get-tuple-element.46), channel_id=1, source_target_pairs={{0,4},{4,0},{8,12},{12,8},{16,20},{20,16},{24,28},{28,24},{1,5},{5... | collective-permute-start | bytes 1572872 | tf_op jit(solution)/shard_map/ppermute | solution.py:99
  16.9 2.7 %collective-permute-start.6 = (bf16[512,128]{1,0:T(8,128)(2,1)S(1)}, bf16[512,128]{1,0:T(8,128)(2,1)S(1)}, u32[]{:S(2)}, u32[]{:S(2)}) collective-permute-start(bf16[512,128]{1,0:T(8,128)(2,1)S(1)} %get-tuple-element.43), channel_id=1, source_target_pairs={{0,3},{1,2},{2,1},{3,0},{4,7},{5,6},{6,5},{7,4},{8,11},{9,10},{10,... | collective-permute-start | bytes 393224 | tf_op jit(solution)/shard_map/ppermute | solution.py:96
  19.6 0.0 collective-permute-start.7
  19.6 0.0 collective-permute-done.8.recv_ref
  19.6 0.1 fold_core.1
  19.7 2.5 %collective-permute-start.9 = (bf16[256,128]{1,0:T(8,128)(2,1)S(1)}, bf16[256,128]{1,0:T(8,128)(2,1)S(1)}, u32[]{:S(2)}, u32[]{:S(2)}) collective-permute-start(bf16[256,128]{1,0:T(8,128)(2,1)S(1)} %get-tuple-element.48), channel_id=1, source_target_pairs={{0,24},{4,28},{8,16},{12,20},{16,8},{20,12},{24,0},{28,4},{1,25},{... | collective-permute-start | bytes 196616 | tf_op jit(solution)/shard_map/ppermute | solution.py:102
  22.2 0.5 %collective-permute-start.10 = (bf16[256,128]{1,0:T(8,128)(2,1)S(1)}, bf16[256,128]{1,0:T(8,128)(2,1)S(1)}, u32[]{:S(2)}, u32[]{:S(2)}) collective-permute-start(bf16[256,128]{1,0:T(8,128)(2,1)S(1)} %get-tuple-element.49), channel_id=1, source_target_pairs={{0,16},{4,20},{8,24},{12,28},{16,0},{20,4},{24,8},{28,12},{1,17},{... | collective-permute-start | bytes 196616 | tf_op jit(solution)/shard_map/ppermute | solution.py:102
  22.7 0.5 %collective-permute-start.11 = (bf16[256,128]{1,0:T(8,128)(2,1)S(1)}, bf16[256,128]{1,0:T(8,128)(2,1)S(1)}, u32[]{:S(2)}, u32[]{:S(2)}) collective-permute-start(bf16[256,128]{1,0:T(8,128)(2,1)S(1)} %get-tuple-element.50), channel_id=1, source_target_pairs={{0,8},{4,12},{8,0},{12,4},{16,24},{20,28},{24,16},{28,20},{1,9},{5... | collective-permute-start | bytes 196616 | tf_op jit(solution)/shard_map/ppermute | solution.py:102
  23.2 1.7 %collective-permute-done.9.refs_0_ = bf16[256,128]{1,0:T(8,128)(2,1)S(1)} collective-permute-done((bf16[256,128]{1,0:T(8,128)(2,1)S(1)}, bf16[256,128]{1,0:T(8,128)(2,1)S(1)}, u32[]{:S(2)}, u32[]{:S(2)}) %collective-permute-start.9) | collective-permute-done | bytes 65568 | tf_op jit(solution)/shard_map/ppermute | solution.py:102
  25.0 1.7 %collective-permute-start.12 = (bf16[512,128]{1,0:T(8,128)(2,1)S(1)}, bf16[512,128]{1,0:T(8,128)(2,1)S(1)}, u32[]{:S(2)}, u32[]{:S(2)}) collective-permute-start(bf16[512,128]{1,0:T(8,128)(2,1)S(1)} %get-tuple-element.52), channel_id=1, source_target_pairs={{0,1},{1,0},{2,3},{3,2},{4,5},{5,4},{6,7},{7,6},{8,9},{9,8},{10,11... | collective-permute-start | bytes 393224 | tf_op jit(solution)/shard_map/ppermute | solution.py:96
  26.7 0.0 collective-permute-done.10.refs_1_
  26.7 0.3 collective-permute-done.11.refs_2_
  27.0 2.5 %collective-permute-start.13 = (bf16[64,128]{1,0:T(8,128)(2,1)S(1)}, bf16[64,128]{1,0:T(8,128)(2,1)S(1)}, u32[]{:S(2)}, u32[]{:S(2)}) collective-permute-start(bf16[64,128]{1,0:T(8,128)(2,1)S(1)} %get-tuple-element.53), channel_id=1, source_target_pairs={{0,3},{1,2},{2,1},{3,0},{4,7},{5,6},{6,5},{7,4},{8,11},{9,10},{10,... | collective-permute-start | bytes 49160 | tf_op jit(solution)/shard_map/ppermute | solution.py:96
  29.5 0.7 %collective-permute-start.14 = (bf16[64,128]{1,0:T(8,128)(2,1)S(1)}, bf16[64,128]{1,0:T(8,128)(2,1)S(1)}, u32[]{:S(2)}, u32[]{:S(2)}) collective-permute-start(bf16[64,128]{1,0:T(8,128)(2,1)S(1)} %get-tuple-element.54), channel_id=1, source_target_pairs={{0,2},{1,3},{2,0},{3,1},{4,6},{5,7},{6,4},{7,5},{8,10},{9,11},{10,... | collective-permute-start | bytes 49160 | tf_op jit(solution)/shard_map/ppermute | solution.py:96
  30.2 0.0 collective-permute-done.6.refs_0_
  30.2 1.3 %collective-permute-start.15 = (bf16[64,128]{1,0:T(8,128)(2,1)S(1)}, bf16[64,128]{1,0:T(8,128)(2,1)S(1)}, u32[]{:S(2)}, u32[]{:S(2)}) collective-permute-start(bf16[64,128]{1,0:T(8,128)(2,1)S(1)} %get-tuple-element.55), channel_id=1, source_target_pairs={{0,1},{1,0},{2,3},{3,2},{4,5},{5,4},{6,7},{7,6},{8,9},{9,8},{10,11... | collective-permute-start | bytes 49160 | tf_op jit(solution)/shard_map/ppermute | solution.py:96
  31.4 0.3 collective-permute-done.7.refs_1_
  31.8 1.3 %collective-permute-done.12.refs_0_ = bf16[512,128]{1,0:T(8,128)(2,1)S(1)} collective-permute-done((bf16[512,128]{1,0:T(8,128)(2,1)S(1)}, bf16[512,128]{1,0:T(8,128)(2,1)S(1)}, u32[]{:S(2)}, u32[]{:S(2)}) %collective-permute-start.12) | collective-permute-done | bytes 131104 | tf_op jit(solution)/shard_map/ppermute | solution.py:96
  33.0 0.0 collective-permute-done.13.refs_1_
  33.0 1.1 %collective-permute-done.14.refs_2_ = bf16[64,128]{1,0:T(8,128)(2,1)S(1)} collective-permute-done((bf16[64,128]{1,0:T(8,128)(2,1)S(1)}, bf16[64,128]{1,0:T(8,128)(2,1)S(1)}, u32[]{:S(2)}, u32[]{:S(2)}) %collective-permute-start.14) | collective-permute-done | bytes 16416 | tf_op jit(solution)/shard_map/ppermute | solution.py:96
  34.1 0.0 collective-permute-done.15.refs_3_
  34.1 0.7 %finish.1 = (f32[256,128]{1,0:T(8,128)}, f32[256,128]{1,0:T(8,128)}, f32[32,128]{1,0:T(8,128)}, f32[32,128]{1,0:T(8,128)}) custom-call(f32[512,128]{1,0:T(8,128)S(1)} %sum_users.1.user_ref, f32[64,128]{1,0:T(8,128)S(1)} %get-tuple-element.51.item_ref, bf16[512,128]{1,0:T(8,128)(2,1)S(1)} %collective-permute-done.12.refs_0_, ...), custom_call_target="tpu_custom_call" | custom-call | bytes 1000 | tf_op jit(solution)/shard_map/finish/pallas_call | solution.py:34
  (8 shorter events, 0.1 us)
Async XLA Ops:
  1.6 9.0 %collective-permute-start = (bf16[272,128]{1,0:T(8,128)(2,1)S(1)}, bf16[272,128]{1,0:T(8,128)(2,1)S(1)}, u32[]{:S(2)}, u32[]{:S(2)}) collective-permute-start(bf16[272,128]{1,0:T(8,128)(2,1)S(1)} %get-tuple-element.36), channel_id=1, source_target_pairs={{0,3},{1,2},{2,1},{3,0},{4,7},{5,6},{6,5},{7,4},{8,11},{9,10},{10,... | collective-permute-start | bytes 208904 | tf_op jit(solution)/shard_map/ppermute | solution.py:96
  6.7 5.9 %collective-permute-start.1 = (bf16[272,128]{1,0:T(8,128)(2,1)S(1)}, bf16[272,128]{1,0:T(8,128)(2,1)S(1)}, u32[]{:S(2)}, u32[]{:S(2)}) collective-permute-start(bf16[272,128]{1,0:T(8,128)(2,1)S(1)} %get-tuple-element.37), channel_id=1, source_target_pairs={{0,2},{1,3},{2,0},{3,1},{4,6},{5,7},{6,4},{7,5},{8,10},{9,11},{10,... | collective-permute-start | bytes 208904 | tf_op jit(solution)/shard_map/ppermute | solution.py:96
  6.7 6.0 %collective-permute-start.2 = (bf16[272,128]{1,0:T(8,128)(2,1)S(1)}, bf16[272,128]{1,0:T(8,128)(2,1)S(1)}, u32[]{:S(2)}, u32[]{:S(2)}) collective-permute-start(bf16[272,128]{1,0:T(8,128)(2,1)S(1)} %get-tuple-element.38), channel_id=1, source_target_pairs={{0,1},{1,0},{2,3},{3,2},{4,5},{5,4},{6,7},{7,6},{8,9},{9,8},{10,11... | collective-permute-start | bytes 208904 | tf_op jit(solution)/shard_map/ppermute | solution.py:96
  7.4 6.8 %copy-start.1 = (bf16[1024,128]{1,0:T(8,128)(2,1)S(1)}, bf16[1024,128]{1,0:T(8,128)(2,1)}, u32[]{:S(2)}) copy-start(bf16[1024,128]{1,0:T(8,128)(2,1)} %ux_ref.1) | copy-start | bytes 786436
  10.6 3.6 %copy-start = (bf16[1024,128]{1,0:T(8,128)(2,1)S(1)}, bf16[1024,128]{1,0:T(8,128)(2,1)}, u32[]{:S(2)}) copy-start(bf16[1024,128]{1,0:T(8,128)(2,1)} %up_ref.1) | copy-start | bytes 786436
  10.6 2.7 %collective-permute-start.3 = (bf16[256,128]{1,0:T(8,128)(2,1)S(1)}, bf16[256,128]{1,0:T(8,128)(2,1)S(1)}, u32[]{:S(2)}, u32[]{:S(2)}) collective-permute-start(bf16[256,128]{1,0:T(8,128)(2,1)S(1)} %slice_multiply_fusion.2), channel_id=1, source_target_pairs={{0,4},{4,0},{8,12},{12,8},{16,20},{20,16},{24,28},{28,24},{1,5},{5... | collective-permute-start | bytes 196616 | tf_op jit(solution)/shard_map/ppermute | solution.py:99
  12.6 1.3 %collective-permute-start.4 = (bf16[256,128]{1,0:T(8,128)(2,1)S(1)}, bf16[256,128]{1,0:T(8,128)(2,1)S(1)}, u32[]{:S(2)}, u32[]{:S(2)}) collective-permute-start(bf16[256,128]{1,0:T(8,128)(2,1)S(1)} %slice_multiply_fusion.1), channel_id=1, source_target_pairs={{0,4},{4,0},{8,12},{12,8},{16,20},{20,16},{24,28},{28,24},{1,5},{5... | collective-permute-start | bytes 196616 | tf_op jit(solution)/shard_map/ppermute | solution.py:99
  12.7 1.5 %collective-permute-start.5 = (bf16[256,128]{1,0:T(8,128)(2,1)S(1)}, bf16[256,128]{1,0:T(8,128)(2,1)S(1)}, u32[]{:S(2)}, u32[]{:S(2)}) collective-permute-start(bf16[256,128]{1,0:T(8,128)(2,1)S(1)} %slice_multiply_fusion), channel_id=1, source_target_pairs={{0,4},{4,0},{8,12},{12,8},{16,20},{20,16},{24,28},{28,24},{1,5},{5... | collective-permute-start | bytes 196616 | tf_op jit(solution)/shard_map/ppermute | solution.py:99
  16.5 3.1 %collective-permute-start.8 = (f32[1024,128]{1,0:T(8,128)S(1)}, f32[1024,128]{1,0:T(8,128)S(1)}, u32[]{:S(2)}, u32[]{:S(2)}) collective-permute-start(f32[1024,128]{1,0:T(8,128)S(1)} %get-tuple-element.46), channel_id=1, source_target_pairs={{0,4},{4,0},{8,12},{12,8},{16,20},{20,16},{24,28},{28,24},{1,5},{5... | collective-permute-start | bytes 1572872 | tf_op jit(solution)/shard_map/ppermute | solution.py:99
  16.9 13.3 %collective-permute-start.6 = (bf16[512,128]{1,0:T(8,128)(2,1)S(1)}, bf16[512,128]{1,0:T(8,128)(2,1)S(1)}, u32[]{:S(2)}, u32[]{:S(2)}) collective-permute-start(bf16[512,128]{1,0:T(8,128)(2,1)S(1)} %get-tuple-element.43), channel_id=1, source_target_pairs={{0,3},{1,2},{2,1},{3,0},{4,7},{5,6},{6,5},{7,4},{8,11},{9,10},{10,... | collective-permute-start | bytes 393224 | tf_op jit(solution)/shard_map/ppermute | solution.py:96
  19.6 12.1 %collective-permute-start.7 = (bf16[512,128]{1,0:T(8,128)(2,1)S(1)}, bf16[512,128]{1,0:T(8,128)(2,1)S(1)}, u32[]{:S(2)}, u32[]{:S(2)}) collective-permute-start(bf16[512,128]{1,0:T(8,128)(2,1)S(1)} %get-tuple-element.44), channel_id=1, source_target_pairs={{0,2},{1,3},{2,0},{3,1},{4,6},{5,7},{6,4},{7,5},{8,10},{9,11},{10,... | collective-permute-start | bytes 393224 | tf_op jit(solution)/shard_map/ppermute | solution.py:96
  19.7 5.3 %collective-permute-start.9 = (bf16[256,128]{1,0:T(8,128)(2,1)S(1)}, bf16[256,128]{1,0:T(8,128)(2,1)S(1)}, u32[]{:S(2)}, u32[]{:S(2)}) collective-permute-start(bf16[256,128]{1,0:T(8,128)(2,1)S(1)} %get-tuple-element.48), channel_id=1, source_target_pairs={{0,24},{4,28},{8,16},{12,20},{16,8},{20,12},{24,0},{28,4},{1,25},{... | collective-permute-start | bytes 196616 | tf_op jit(solution)/shard_map/ppermute | solution.py:102
  22.2 4.5 %collective-permute-start.10 = (bf16[256,128]{1,0:T(8,128)(2,1)S(1)}, bf16[256,128]{1,0:T(8,128)(2,1)S(1)}, u32[]{:S(2)}, u32[]{:S(2)}) collective-permute-start(bf16[256,128]{1,0:T(8,128)(2,1)S(1)} %get-tuple-element.49), channel_id=1, source_target_pairs={{0,16},{4,20},{8,24},{12,28},{16,0},{20,4},{24,8},{28,12},{1,17},{... | collective-permute-start | bytes 196616 | tf_op jit(solution)/shard_map/ppermute | solution.py:102
  22.7 4.3 %collective-permute-start.11 = (bf16[256,128]{1,0:T(8,128)(2,1)S(1)}, bf16[256,128]{1,0:T(8,128)(2,1)S(1)}, u32[]{:S(2)}, u32[]{:S(2)}) collective-permute-start(bf16[256,128]{1,0:T(8,128)(2,1)S(1)} %get-tuple-element.50), channel_id=1, source_target_pairs={{0,8},{4,12},{8,0},{12,4},{16,24},{20,28},{24,16},{28,20},{1,9},{5... | collective-permute-start | bytes 196616 | tf_op jit(solution)/shard_map/ppermute | solution.py:102
  25.0 8.1 %collective-permute-start.12 = (bf16[512,128]{1,0:T(8,128)(2,1)S(1)}, bf16[512,128]{1,0:T(8,128)(2,1)S(1)}, u32[]{:S(2)}, u32[]{:S(2)}) collective-permute-start(bf16[512,128]{1,0:T(8,128)(2,1)S(1)} %get-tuple-element.52), channel_id=1, source_target_pairs={{0,1},{1,0},{2,3},{3,2},{4,5},{5,4},{6,7},{7,6},{8,9},{9,8},{10,11... | collective-permute-start | bytes 393224 | tf_op jit(solution)/shard_map/ppermute | solution.py:96
  27.0 6.1 %collective-permute-start.13 = (bf16[64,128]{1,0:T(8,128)(2,1)S(1)}, bf16[64,128]{1,0:T(8,128)(2,1)S(1)}, u32[]{:S(2)}, u32[]{:S(2)}) collective-permute-start(bf16[64,128]{1,0:T(8,128)(2,1)S(1)} %get-tuple-element.53), channel_id=1, source_target_pairs={{0,3},{1,2},{2,1},{3,0},{4,7},{5,6},{6,5},{7,4},{8,11},{9,10},{10,... | collective-permute-start | bytes 49160 | tf_op jit(solution)/shard_map/ppermute | solution.py:96
  29.5 4.6 %collective-permute-start.14 = (bf16[64,128]{1,0:T(8,128)(2,1)S(1)}, bf16[64,128]{1,0:T(8,128)(2,1)S(1)}, u32[]{:S(2)}, u32[]{:S(2)}) collective-permute-start(bf16[64,128]{1,0:T(8,128)(2,1)S(1)} %get-tuple-element.54), channel_id=1, source_target_pairs={{0,2},{1,3},{2,0},{3,1},{4,6},{5,7},{6,4},{7,5},{8,10},{9,11},{10,... | collective-permute-start | bytes 49160 | tf_op jit(solution)/shard_map/ppermute | solution.py:96
  30.2 4.0 %collective-permute-start.15 = (bf16[64,128]{1,0:T(8,128)(2,1)S(1)}, bf16[64,128]{1,0:T(8,128)(2,1)S(1)}, u32[]{:S(2)}, u32[]{:S(2)}) collective-permute-start(bf16[64,128]{1,0:T(8,128)(2,1)S(1)} %get-tuple-element.55), channel_id=1, source_target_pairs={{0,1},{1,0},{2,3},{3,2},{4,5},{5,4},{6,7},{7,6},{8,9},{9,8},{10,11... | collective-permute-start | bytes 49160 | tf_op jit(solution)/shard_map/ppermute | solution.py:96

commit v6 on v5

--- a/solution.py
+++ b/solution.py
@@ -243,11 +243,12 @@
             pltpu.VMEM((obs_slots, tile, tile), bf16),
         ),
     )
-    swapped = [core_peer(x[: 2 * half] * one[:1]) for x, one in zip(received[::-1], ones)][::-1]
+    swapped = [core_peer(x[: 2 * half] * one[:1]) for x, one in zip(received, ones)]
 
     slots = peers * obs_slots
 
     near = range(peers)
+    first_order = [peers - 1, *range(peers - 1)]
 
     def start_ids(sources, targets, sems):
         copies = [pltpu.make_async_copy(a, b, sems.at[n]) for n, (a, b) in enumerate(zip(sources, targets))]
@@ -282,8 +283,8 @@
     def other_tiles(
         ou_hbm, oi_hbm, oc_hbm, up_ref, ux_ref, count_ref, itile_ref, iacc_in, w_ref, utile_ref, uacc_in, *refs
     ):
-        recv = refs[:peers][::-1]
-        swap = refs[peers : 2 * peers][::-1]
+        recv = [refs[first_order.index(k)] for k in range(peers)]
+        swap = [refs[peers + first_order.index(k)] for k in range(peers)]
         send, keep, *outs = refs[2 * peers : 3 * peers + 3]
         ou_ref, oi_ref, oc_ref, sems, vbuf, gbuf, hbuf, iacc, uacc = refs[3 * peers + 3 :]
         copies = start_ids((ou_hbm, oi_hbm, oc_hbm), (ou_ref, oi_ref, oc_ref), sems)
@@ -355,7 +356,7 @@
         [HBM, HBM, HBM] + [VM] * (8 + 2 * peers),
         (
             *in_hbm(id_args), user_pred, user_imp, own_count, itile, iacc, weights, utile, uacc,
-            *received[::-1], *swapped[::-1],
+            *(received[k] for k in first_order), *(swapped[k] for k in first_order),
         ),
         (6 * slots * 2 * tile**3, 4000000, 2 * slots * tile * tile),
         id_scratch

time: 35.1 us -> 34.7 us (0.989)
  starting transfers between devices: 19.3 us -> 18.6 us
    ppermute x4, starting transfers between devices: 1.11 us -> 0.43 us  [core_peer(): return lax.ppermute(x, 'user', [(i, i ^ 1) for i in range(user_ways)])]
  transfers between devices with their start and end apart: 16 -> 16, of which waited for: 8 -> 10; matrix products, arithmetic and copies ran while one was open for 0% -> 0% of each run, Pallas kernels for 10% -> 10%
where the time goes in v6:
time: 34.7 us; the launch traced here: 34.5 us
  starting transfers between devices  18.6 us (54%)
  waiting for transfers between devices  7.8 us (22%)
  Pallas kernels  7.28 us (21%)
  between operations  0.77 us (2%)
    ppermute x9, starting transfers between devices, item_peer(): return lax.ppermute(x, 'item', [(i, i ^ k) for i in range(item_ways)])  14.6 us
    pallas_call x7, Pallas kernels, call(): pl.pallas_call(body, out_shape=out_shapes, in_specs=specs, out_specs=tupl...  7.28 us
    ppermute x9, waiting for transfers between devices, item_peer(): return lax.ppermute(x, 'item', [(i, i ^ k) for i in range(item_ways)])  4.23 us
    ppermute x3, starting transfers between devices, chip_peer(): lax.ppermute(x, 'user', [(i, i ^ cores * k) for i in range(user_ways)])  3.55 us
    ppermute x3, waiting for transfers between devices, chip_peer(): lax.ppermute(x, 'user', [(i, i ^ cores * k) for i in range(user_ways)])  2.34 us
    ppermute x4, waiting for transfers between devices, core_peer(): return lax.ppermute(x, 'user', [(i, i ^ 1) for i in range(user_ways)])  1.24 us
  transfers between devices with their start and end apart: 16, of which 10 were waited for; matrix products, arithmetic and copies ran while one was open for 0% of the time, Pallas kernels for 10%

profile of v6, /device:TPU:0, one launch (start us, length us, event | category | flops | bytes accessed | tf_op | source)
XLA Modules:
  0.0 34.5 jit_solution(9705003326452638533)
XLA Ops:
  0.6 1.0 %pack.1 = (bf16[272,128]{1,0:T(8,128)(2,1)S(1)}, bf16[272,128]{1,0:T(8,128)(2,1)S(1)}, bf16[272,128]{1,0:T(8,128)(2,1)S(1)}, f32[16,128]{1,0:T(8,128)S(1)}) custom-call(s32[64]{0:T(128)} %bitcast.21, s32[64]{0:T(128)} %bitcast.22, bf16[256,128]{1,0:T(8,128)(2,1)} %vp_hbm.3, bf16[256,128]{1,0:T(8,128)(2,1)} %vi_hbm.3), custom_call_target="tpu_custom_call" | custom-call | bytes 400000 | tf_op jit(solution)/shard_map/pack/pallas_call | solution.py:34
  1.6 5.1 %collective-permute-start = (bf16[272,128]{1,0:T(8,128)(2,1)S(1)}, bf16[272,128]{1,0:T(8,128)(2,1)S(1)}, u32[]{:S(2)}, u32[]{:S(2)}) collective-permute-start(bf16[272,128]{1,0:T(8,128)(2,1)S(1)} %get-tuple-element.36), channel_id=1, source_target_pairs={{0,3},{1,2},{2,1},{3,0},{4,7},{5,6},{6,5},{7,4},{8,11},{9,10},{10,... | collective-permute-start | bytes 208904 | tf_op jit(solution)/shard_map/ppermute | solution.py:96
  6.7 0.0 collective-permute-start.1
  6.7 0.6 %collective-permute-start.2 = (bf16[272,128]{1,0:T(8,128)(2,1)S(1)}, bf16[272,128]{1,0:T(8,128)(2,1)S(1)}, u32[]{:S(2)}, u32[]{:S(2)}) collective-permute-start(bf16[272,128]{1,0:T(8,128)(2,1)S(1)} %get-tuple-element.38), channel_id=1, source_target_pairs={{0,2},{1,3},{2,0},{3,1},{4,6},{5,7},{6,4},{7,5},{8,10},{9,11},{10,... | collective-permute-start | bytes 208904 | tf_op jit(solution)/shard_map/ppermute | solution.py:96
  7.4 0.0 copy-start.1
  7.4 3.2 %local_tiles.1 = (f32[16,128,128]{2,1,0:T(8,128)S(1)}, f32[16,128,128]{2,1,0:T(8,128)S(1)}, f32[2,1024,128]{2,1,0:T(8,128)S(1)}, f32[2,256,128]{2,1,0:T(8,128)S(...) custom-call(s32[16]{0:T(128)} %bitcast.15, ...), custom_call_target="tpu_custom_call" | custom-call | flops 268435456 | bytes 8000000 | tf_op jit(solution)/shard_map/local_tiles/pallas_call | solution.py:34
  10.6 0.0 copy-start
  10.6 0.0 collective-permute-done.refs_0_
  10.6 0.1 collective-permute-start.3
  10.7 0.8 %collective-permute-done.1.refs_1_ = bf16[272,128]{1,0:T(8,128)(2,1)S(1)} collective-permute-done((bf16[272,128]{1,0:T(8,128)(2,1)S(1)}, bf16[272,128]{1,0:T(8,128)(2,1)S(1)}, u32[]{:S(2)}, u32[]{:S(2)}) %collective-permute-start.1) | collective-permute-done | bytes 69664 | tf_op jit(solution)/shard_map/ppermute | solution.py:96
  11.6 0.1 collective-permute-start.4
  11.7 0.8 %collective-permute-done.2.refs_2_ = bf16[272,128]{1,0:T(8,128)(2,1)S(1)} collective-permute-done((bf16[272,128]{1,0:T(8,128)(2,1)S(1)}, bf16[272,128]{1,0:T(8,128)(2,1)S(1)}, u32[]{:S(2)}, u32[]{:S(2)}) %collective-permute-start.2) | collective-permute-done | bytes 69664 | tf_op jit(solution)/shard_map/ppermute | solution.py:96
  12.4 0.1 collective-permute-start.5
  12.5 0.0 collective-permute-done.3.refs_3_
  12.5 0.4 %collective-permute-done.4.refs_4_ = bf16[256,128]{1,0:T(8,128)(2,1)S(1)} collective-permute-done((bf16[256,128]{1,0:T(8,128)(2,1)S(1)}, bf16[256,128]{1,0:T(8,128)(2,1)S(1)}, u32[]{:S(2)}, u32[]{:S(2)}) %collective-permute-start.4) | collective-permute-done | bytes 65568 | tf_op jit(solution)/shard_map/ppermute | solution.py:99
  12.9 0.9 %collective-permute-done.5.refs_5_ = bf16[256,128]{1,0:T(8,128)(2,1)S(1)} collective-permute-done((bf16[256,128]{1,0:T(8,128)(2,1)S(1)}, bf16[256,128]{1,0:T(8,128)(2,1)S(1)}, u32[]{:S(2)}, u32[]{:S(2)}) %collective-permute-start.5) | collective-permute-done | bytes 65568 | tf_op jit(solution)/shard_map/ppermute | solution.py:99
  13.8 0.0 copy-done.1
  13.8 0.0 copy-done
  13.8 2.3 %other_tiles.1 = (f32[1024,128]{1,0:T(8,128)S(1)}, f32[1024,128]{1,0:T(8,128)S(1)}, bf16[512,128]{1,0:T(8,128)(2,1)S(1)}, bf16[512,128]{1,0:T(8,128)(2,1)S(1)}, ...) custom-call(s32[16]{0:T(128)} %bitcast.16, s32[16]{0:T(128)} %bitcast.18, s32[4]{0:T(128)} %bitcast.20, ...), custom_call_target="tpu_custom_call" | custom-call | flops 301989888 | bytes 4000000 | tf_op jit(solution)/shard_map/other_tiles/pallas_call | solution.py:34
  16.0 0.2 collective-permute-start.8
  16.3 3.0 %collective-permute-start.6 = (bf16[512,128]{1,0:T(8,128)(2,1)S(1)}, bf16[512,128]{1,0:T(8,128)(2,1)S(1)}, u32[]{:S(2)}, u32[]{:S(2)}) collective-permute-start(bf16[512,128]{1,0:T(8,128)(2,1)S(1)} %get-tuple-element.43), channel_id=1, source_target_pairs={{0,3},{1,2},{2,1},{3,0},{4,7},{5,6},{6,5},{7,4},{8,11},{9,10},{10,... | collective-permute-start | bytes 393224 | tf_op jit(solution)/shard_map/ppermute | solution.py:96
  19.3 0.0 collective-permute-start.7
  19.3 0.0 collective-permute-done.8.recv_ref
  19.3 0.1 fold_core.1
  19.4 2.5 %collective-permute-start.9 = (bf16[256,128]{1,0:T(8,128)(2,1)S(1)}, bf16[256,128]{1,0:T(8,128)(2,1)S(1)}, u32[]{:S(2)}, u32[]{:S(2)}) collective-permute-start(bf16[256,128]{1,0:T(8,128)(2,1)S(1)} %get-tuple-element.48), channel_id=1, source_target_pairs={{0,24},{4,28},{8,16},{12,20},{16,8},{20,12},{24,0},{28,4},{1,25},{... | collective-permute-start | bytes 196616 | tf_op jit(solution)/shard_map/ppermute | solution.py:102
  21.9 0.5 %collective-permute-start.10 = (bf16[256,128]{1,0:T(8,128)(2,1)S(1)}, bf16[256,128]{1,0:T(8,128)(2,1)S(1)}, u32[]{:S(2)}, u32[]{:S(2)}) collective-permute-start(bf16[256,128]{1,0:T(8,128)(2,1)S(1)} %get-tuple-element.49), channel_id=1, source_target_pairs={{0,16},{4,20},{8,24},{12,28},{16,0},{20,4},{24,8},{28,12},{1,17},{... | collective-permute-start | bytes 196616 | tf_op jit(solution)/shard_map/ppermute | solution.py:102
  22.4 0.5 %collective-permute-start.11 = (bf16[256,128]{1,0:T(8,128)(2,1)S(1)}, bf16[256,128]{1,0:T(8,128)(2,1)S(1)}, u32[]{:S(2)}, u32[]{:S(2)}) collective-permute-start(bf16[256,128]{1,0:T(8,128)(2,1)S(1)} %get-tuple-element.50), channel_id=1, source_target_pairs={{0,8},{4,12},{8,0},{12,4},{16,24},{20,28},{24,16},{28,20},{1,9},{5... | collective-permute-start | bytes 196616 | tf_op jit(solution)/shard_map/ppermute | solution.py:102
  22.9 1.7 %collective-permute-done.9.refs_0_ = bf16[256,128]{1,0:T(8,128)(2,1)S(1)} collective-permute-done((bf16[256,128]{1,0:T(8,128)(2,1)S(1)}, bf16[256,128]{1,0:T(8,128)(2,1)S(1)}, u32[]{:S(2)}, u32[]{:S(2)}) %collective-permute-start.9) | collective-permute-done | bytes 65568 | tf_op jit(solution)/shard_map/ppermute | solution.py:102
  24.6 1.4 %collective-permute-start.12 = (bf16[512,128]{1,0:T(8,128)(2,1)S(1)}, bf16[512,128]{1,0:T(8,128)(2,1)S(1)}, u32[]{:S(2)}, u32[]{:S(2)}) collective-permute-start(bf16[512,128]{1,0:T(8,128)(2,1)S(1)} %get-tuple-element.52), channel_id=1, source_target_pairs={{0,1},{1,0},{2,3},{3,2},{4,5},{5,4},{6,7},{7,6},{8,9},{9,8},{10,11... | collective-permute-start | bytes 393224 | tf_op jit(solution)/shard_map/ppermute | solution.py:96
  26.0 0.1 collective-permute-done.10.refs_1_
  26.1 0.5 %collective-permute-done.11.refs_2_ = bf16[256,128]{1,0:T(8,128)(2,1)S(1)} collective-permute-done((bf16[256,128]{1,0:T(8,128)(2,1)S(1)}, bf16[256,128]{1,0:T(8,128)(2,1)S(1)}, u32[]{:S(2)}, u32[]{:S(2)}) %collective-permute-start.11) | collective-permute-done | bytes 65568 | tf_op jit(solution)/shard_map/ppermute | solution.py:102
  26.7 2.5 %collective-permute-start.13 = (bf16[64,128]{1,0:T(8,128)(2,1)S(1)}, bf16[64,128]{1,0:T(8,128)(2,1)S(1)}, u32[]{:S(2)}, u32[]{:S(2)}) collective-permute-start(bf16[64,128]{1,0:T(8,128)(2,1)S(1)} %get-tuple-element.53), channel_id=1, source_target_pairs={{0,3},{1,2},{2,1},{3,0},{4,7},{5,6},{6,5},{7,4},{8,11},{9,10},{10,... | collective-permute-start | bytes 49160 | tf_op jit(solution)/shard_map/ppermute | solution.py:96
  29.1 0.6 %collective-permute-start.14 = (bf16[64,128]{1,0:T(8,128)(2,1)S(1)}, bf16[64,128]{1,0:T(8,128)(2,1)S(1)}, u32[]{:S(2)}, u32[]{:S(2)}) collective-permute-start(bf16[64,128]{1,0:T(8,128)(2,1)S(1)} %get-tuple-element.54), channel_id=1, source_target_pairs={{0,2},{1,3},{2,0},{3,1},{4,6},{5,7},{6,4},{7,5},{8,10},{9,11},{10,... | collective-permute-start | bytes 49160 | tf_op jit(solution)/shard_map/ppermute | solution.py:96
  29.7 0.0 collective-permute-done.6.refs_0_
  29.7 1.4 %collective-permute-start.15 = (bf16[64,128]{1,0:T(8,128)(2,1)S(1)}, bf16[64,128]{1,0:T(8,128)(2,1)S(1)}, u32[]{:S(2)}, u32[]{:S(2)}) collective-permute-start(bf16[64,128]{1,0:T(8,128)(2,1)S(1)} %get-tuple-element.55), channel_id=1, source_target_pairs={{0,1},{1,0},{2,3},{3,2},{4,5},{5,4},{6,7},{7,6},{8,9},{9,8},{10,11... | collective-permute-start | bytes 49160 | tf_op jit(solution)/shard_map/ppermute | solution.py:96
  31.1 1.0 %collective-permute-done.7.refs_1_ = bf16[512,128]{1,0:T(8,128)(2,1)S(1)} collective-permute-done((bf16[512,128]{1,0:T(8,128)(2,1)S(1)}, bf16[512,128]{1,0:T(8,128)(2,1)S(1)}, u32[]{:S(2)}, u32[]{:S(2)}) %collective-permute-start.7) | collective-permute-done | bytes 131104 | tf_op jit(solution)/shard_map/ppermute | solution.py:96
  32.2 0.8 %collective-permute-done.12.refs_0_ = bf16[512,128]{1,0:T(8,128)(2,1)S(1)} collective-permute-done((bf16[512,128]{1,0:T(8,128)(2,1)S(1)}, bf16[512,128]{1,0:T(8,128)(2,1)S(1)}, u32[]{:S(2)}, u32[]{:S(2)}) %collective-permute-start.12) | collective-permute-done | bytes 131104 | tf_op jit(solution)/shard_map/ppermute | solution.py:96
  33.0 0.0 collective-permute-done.13.refs_1_
  33.0 0.8 %collective-permute-done.14.refs_2_ = bf16[64,128]{1,0:T(8,128)(2,1)S(1)} collective-permute-done((bf16[64,128]{1,0:T(8,128)(2,1)S(1)}, bf16[64,128]{1,0:T(8,128)(2,1)S(1)}, u32[]{:S(2)}, u32[]{:S(2)}) %collective-permute-start.14) | collective-permute-done | bytes 16416 | tf_op jit(solution)/shard_map/ppermute | solution.py:96
  33.8 0.0 collective-permute-done.15.refs_3_
  33.8 0.7 %finish.1 = (f32[256,128]{1,0:T(8,128)}, f32[256,128]{1,0:T(8,128)}, f32[32,128]{1,0:T(8,128)}, f32[32,128]{1,0:T(8,128)}) custom-call(f32[512,128]{1,0:T(8,128)S(1)} %sum_users.1.user_ref, f32[64,128]{1,0:T(8,128)S(1)} %get-tuple-element.51.item_ref, bf16[512,128]{1,0:T(8,128)(2,1)S(1)} %collective-permute-done.12.refs_0_, ...), custom_call_target="tpu_custom_call" | custom-call | bytes 1000 | tf_op jit(solution)/shard_map/finish/pallas_call | solution.py:34
  (8 shorter events, 0.1 us)
Async XLA Ops:
  1.6 9.0 %collective-permute-start = (bf16[272,128]{1,0:T(8,128)(2,1)S(1)}, bf16[272,128]{1,0:T(8,128)(2,1)S(1)}, u32[]{:S(2)}, u32[]{:S(2)}) collective-permute-start(bf16[272,128]{1,0:T(8,128)(2,1)S(1)} %get-tuple-element.36), channel_id=1, source_target_pairs={{0,3},{1,2},{2,1},{3,0},{4,7},{5,6},{6,5},{7,4},{8,11},{9,10},{10,... | collective-permute-start | bytes 208904 | tf_op jit(solution)/shard_map/ppermute | solution.py:96
  6.7 4.9 %collective-permute-start.1 = (bf16[272,128]{1,0:T(8,128)(2,1)S(1)}, bf16[272,128]{1,0:T(8,128)(2,1)S(1)}, u32[]{:S(2)}, u32[]{:S(2)}) collective-permute-start(bf16[272,128]{1,0:T(8,128)(2,1)S(1)} %get-tuple-element.37), channel_id=1, source_target_pairs={{0,1},{1,0},{2,3},{3,2},{4,5},{5,4},{6,7},{7,6},{8,9},{9,8},{10,11... | collective-permute-start | bytes 208904 | tf_op jit(solution)/shard_map/ppermute | solution.py:96
  6.7 5.7 %collective-permute-start.2 = (bf16[272,128]{1,0:T(8,128)(2,1)S(1)}, bf16[272,128]{1,0:T(8,128)(2,1)S(1)}, u32[]{:S(2)}, u32[]{:S(2)}) collective-permute-start(bf16[272,128]{1,0:T(8,128)(2,1)S(1)} %get-tuple-element.38), channel_id=1, source_target_pairs={{0,2},{1,3},{2,0},{3,1},{4,6},{5,7},{6,4},{7,5},{8,10},{9,11},{10,... | collective-permute-start | bytes 208904 | tf_op jit(solution)/shard_map/ppermute | solution.py:96
  7.4 6.4 %copy-start.1 = (bf16[1024,128]{1,0:T(8,128)(2,1)S(1)}, bf16[1024,128]{1,0:T(8,128)(2,1)}, u32[]{:S(2)}) copy-start(bf16[1024,128]{1,0:T(8,128)(2,1)} %ux_ref.1) | copy-start | bytes 786436
  10.6 3.2 %copy-start = (bf16[1024,128]{1,0:T(8,128)(2,1)S(1)}, bf16[1024,128]{1,0:T(8,128)(2,1)}, u32[]{:S(2)}) copy-start(bf16[1024,128]{1,0:T(8,128)(2,1)} %up_ref.1) | copy-start | bytes 786436
  10.6 1.9 %collective-permute-start.3 = (bf16[256,128]{1,0:T(8,128)(2,1)S(1)}, bf16[256,128]{1,0:T(8,128)(2,1)S(1)}, u32[]{:S(2)}, u32[]{:S(2)}) collective-permute-start(bf16[256,128]{1,0:T(8,128)(2,1)S(1)} %slice_multiply_fusion.2), channel_id=1, source_target_pairs={{0,4},{4,0},{8,12},{12,8},{16,20},{20,16},{24,28},{28,24},{1,5},{5... | collective-permute-start | bytes 196616 | tf_op jit(solution)/shard_map/ppermute | solution.py:99
  11.6 1.3 %collective-permute-start.4 = (bf16[256,128]{1,0:T(8,128)(2,1)S(1)}, bf16[256,128]{1,0:T(8,128)(2,1)S(1)}, u32[]{:S(2)}, u32[]{:S(2)}) collective-permute-start(bf16[256,128]{1,0:T(8,128)(2,1)S(1)} %slice_multiply_fusion.1), channel_id=1, source_target_pairs={{0,4},{4,0},{8,12},{12,8},{16,20},{20,16},{24,28},{28,24},{1,5},{5... | collective-permute-start | bytes 196616 | tf_op jit(solution)/shard_map/ppermute | solution.py:99
  12.4 1.3 %collective-permute-start.5 = (bf16[256,128]{1,0:T(8,128)(2,1)S(1)}, bf16[256,128]{1,0:T(8,128)(2,1)S(1)}, u32[]{:S(2)}, u32[]{:S(2)}) collective-permute-start(bf16[256,128]{1,0:T(8,128)(2,1)S(1)} %slice_multiply_fusion), channel_id=1, source_target_pairs={{0,4},{4,0},{8,12},{12,8},{16,20},{20,16},{24,28},{28,24},{1,5},{5... | collective-permute-start | bytes 196616 | tf_op jit(solution)/shard_map/ppermute | solution.py:99
  16.0 3.3 %collective-permute-start.8 = (f32[1024,128]{1,0:T(8,128)S(1)}, f32[1024,128]{1,0:T(8,128)S(1)}, u32[]{:S(2)}, u32[]{:S(2)}) collective-permute-start(f32[1024,128]{1,0:T(8,128)S(1)} %get-tuple-element.46), channel_id=1, source_target_pairs={{0,4},{4,0},{8,12},{12,8},{16,20},{20,16},{24,28},{28,24},{1,5},{5... | collective-permute-start | bytes 1572872 | tf_op jit(solution)/shard_map/ppermute | solution.py:99
  16.3 13.5 %collective-permute-start.6 = (bf16[512,128]{1,0:T(8,128)(2,1)S(1)}, bf16[512,128]{1,0:T(8,128)(2,1)S(1)}, u32[]{:S(2)}, u32[]{:S(2)}) collective-permute-start(bf16[512,128]{1,0:T(8,128)(2,1)S(1)} %get-tuple-element.43), channel_id=1, source_target_pairs={{0,3},{1,2},{2,1},{3,0},{4,7},{5,6},{6,5},{7,4},{8,11},{9,10},{10,... | collective-permute-start | bytes 393224 | tf_op jit(solution)/shard_map/ppermute | solution.py:96
  19.3 12.9 %collective-permute-start.7 = (bf16[512,128]{1,0:T(8,128)(2,1)S(1)}, bf16[512,128]{1,0:T(8,128)(2,1)S(1)}, u32[]{:S(2)}, u32[]{:S(2)}) collective-permute-start(bf16[512,128]{1,0:T(8,128)(2,1)S(1)} %get-tuple-element.44), channel_id=1, source_target_pairs={{0,2},{1,3},{2,0},{3,1},{4,6},{5,7},{6,4},{7,5},{8,10},{9,11},{10,... | collective-permute-start | bytes 393224 | tf_op jit(solution)/shard_map/ppermute | solution.py:96
  19.4 5.3 %collective-permute-start.9 = (bf16[256,128]{1,0:T(8,128)(2,1)S(1)}, bf16[256,128]{1,0:T(8,128)(2,1)S(1)}, u32[]{:S(2)}, u32[]{:S(2)}) collective-permute-start(bf16[256,128]{1,0:T(8,128)(2,1)S(1)} %get-tuple-element.48), channel_id=1, source_target_pairs={{0,24},{4,28},{8,16},{12,20},{16,8},{20,12},{24,0},{28,4},{1,25},{... | collective-permute-start | bytes 196616 | tf_op jit(solution)/shard_map/ppermute | solution.py:102
  21.9 4.3 %collective-permute-start.10 = (bf16[256,128]{1,0:T(8,128)(2,1)S(1)}, bf16[256,128]{1,0:T(8,128)(2,1)S(1)}, u32[]{:S(2)}, u32[]{:S(2)}) collective-permute-start(bf16[256,128]{1,0:T(8,128)(2,1)S(1)} %get-tuple-element.49), channel_id=1, source_target_pairs={{0,16},{4,20},{8,24},{12,28},{16,0},{20,4},{24,8},{28,12},{1,17},{... | collective-permute-start | bytes 196616 | tf_op jit(solution)/shard_map/ppermute | solution.py:102
  22.4 4.3 %collective-permute-start.11 = (bf16[256,128]{1,0:T(8,128)(2,1)S(1)}, bf16[256,128]{1,0:T(8,128)(2,1)S(1)}, u32[]{:S(2)}, u32[]{:S(2)}) collective-permute-start(bf16[256,128]{1,0:T(8,128)(2,1)S(1)} %get-tuple-element.50), channel_id=1, source_target_pairs={{0,8},{4,12},{8,0},{12,4},{16,24},{20,28},{24,16},{28,20},{1,9},{5... | collective-permute-start | bytes 196616 | tf_op jit(solution)/shard_map/ppermute | solution.py:102
  24.6 8.4 %collective-permute-start.12 = (bf16[512,128]{1,0:T(8,128)(2,1)S(1)}, bf16[512,128]{1,0:T(8,128)(2,1)S(1)}, u32[]{:S(2)}, u32[]{:S(2)}) collective-permute-start(bf16[512,128]{1,0:T(8,128)(2,1)S(1)} %get-tuple-element.52), channel_id=1, source_target_pairs={{0,1},{1,0},{2,3},{3,2},{4,5},{5,4},{6,7},{7,6},{8,9},{9,8},{10,11... | collective-permute-start | bytes 393224 | tf_op jit(solution)/shard_map/ppermute | solution.py:96
  26.7 6.3 %collective-permute-start.13 = (bf16[64,128]{1,0:T(8,128)(2,1)S(1)}, bf16[64,128]{1,0:T(8,128)(2,1)S(1)}, u32[]{:S(2)}, u32[]{:S(2)}) collective-permute-start(bf16[64,128]{1,0:T(8,128)(2,1)S(1)} %get-tuple-element.53), channel_id=1, source_target_pairs={{0,3},{1,2},{2,1},{3,0},{4,7},{5,6},{6,5},{7,4},{8,11},{9,10},{10,... | collective-permute-start | bytes 49160 | tf_op jit(solution)/shard_map/ppermute | solution.py:96
  29.1 4.6 %collective-permute-start.14 = (bf16[64,128]{1,0:T(8,128)(2,1)S(1)}, bf16[64,128]{1,0:T(8,128)(2,1)S(1)}, u32[]{:S(2)}, u32[]{:S(2)}) collective-permute-start(bf16[64,128]{1,0:T(8,128)(2,1)S(1)} %get-tuple-element.54), channel_id=1, source_target_pairs={{0,2},{1,3},{2,0},{3,1},{4,6},{5,7},{6,4},{7,5},{8,10},{9,11},{10,... | collective-permute-start | bytes 49160 | tf_op jit(solution)/shard_map/ppermute | solution.py:96
  29.7 4.0 %collective-permute-start.15 = (bf16[64,128]{1,0:T(8,128)(2,1)S(1)}, bf16[64,128]{1,0:T(8,128)(2,1)S(1)}, u32[]{:S(2)}, u32[]{:S(2)}) collective-permute-start(bf16[64,128]{1,0:T(8,128)(2,1)S(1)} %get-tuple-element.55), channel_id=1, source_target_pairs={{0,1},{1,0},{2,3},{3,2},{4,5},{5,4},{6,7},{7,6},{8,9},{9,8},{10,11... | collective-permute-start | bytes 49160 | tf_op jit(solution)/shard_map/ppermute | solution.py:96

commit v7 on v6

--- a/solution.py
+++ b/solution.py
@@ -387,7 +387,9 @@
         (core_keep, core_recv),
         (0, 1000, 0),
     )
-    chip_recv = [chip_peer(folded[k], k) for k in reversed(range(1, chips))]
+    middle = chips // 2
+    chip_order = [middle, *reversed(range(middle + 1, chips)), *reversed(range(1, middle))]
+    chip_recv = [chip_peer(folded[k], k) for k in chip_order]
 
     def fold_chips(own_ref, *refs):
         recv = refs[: chips - 1]

time: 34.7 us -> 34.5 us (level)
  no operation moved by 1% of the time
where the time goes in v7:
time: 34.5 us; the launch traced here: 34.3 us
  starting transfers between devices  18.6 us (54%)
  waiting for transfers between devices  7.63 us (22%)
  Pallas kernels  7.28 us (21%)
  between operations  0.78 us (2%)
    ppermute x9, starting transfers between devices, item_peer(): return lax.ppermute(x, 'item', [(i, i ^ k) for i in range(item_ways)])  14.6 us
    pallas_call x7, Pallas kernels, call(): pl.pallas_call(body, out_shape=out_shapes, in_specs=specs, out_specs=tupl...  7.28 us
    ppermute x9, waiting for transfers between devices, item_peer(): return lax.ppermute(x, 'item', [(i, i ^ k) for i in range(item_ways)])  3.89 us
    ppermute x3, starting transfers between devices, chip_peer(): lax.ppermute(x, 'user', [(i, i ^ cores * k) for i in range(user_ways)])  3.55 us
    ppermute x3, waiting for transfers between devices, chip_peer(): lax.ppermute(x, 'user', [(i, i ^ cores * k) for i in range(user_ways)])  2.51 us
    ppermute x4, waiting for transfers between devices, core_peer(): return lax.ppermute(x, 'user', [(i, i ^ 1) for i in range(user_ways)])  1.24 us
  transfers between devices with their start and end apart: 16, of which 10 were waited for; matrix products, arithmetic and copies ran while one was open for 0% of the time, Pallas kernels for 10%

profile of v7, /device:TPU:0, one launch (start us, length us, event | category | flops | bytes accessed | tf_op | source)
XLA Modules:
  0.0 34.3 jit_solution(4362095232117142120)
XLA Ops:
  0.6 1.0 %pack.1 = (bf16[272,128]{1,0:T(8,128)(2,1)S(1)}, bf16[272,128]{1,0:T(8,128)(2,1)S(1)}, bf16[272,128]{1,0:T(8,128)(2,1)S(1)}, f32[16,128]{1,0:T(8,128)S(1)}) custom-call(s32[64]{0:T(128)} %bitcast.21, s32[64]{0:T(128)} %bitcast.22, bf16[256,128]{1,0:T(8,128)(2,1)} %vp_hbm.3, bf16[256,128]{1,0:T(8,128)(2,1)} %vi_hbm.3), custom_call_target="tpu_custom_call" | custom-call | bytes 400000 | tf_op jit(solution)/shard_map/pack/pallas_call | solution.py:34
  1.6 5.1 %collective-permute-start = (bf16[272,128]{1,0:T(8,128)(2,1)S(1)}, bf16[272,128]{1,0:T(8,128)(2,1)S(1)}, u32[]{:S(2)}, u32[]{:S(2)}) collective-permute-start(bf16[272,128]{1,0:T(8,128)(2,1)S(1)} %get-tuple-element.36), channel_id=1, source_target_pairs={{0,3},{1,2},{2,1},{3,0},{4,7},{5,6},{6,5},{7,4},{8,11},{9,10},{10,... | collective-permute-start | bytes 208904 | tf_op jit(solution)/shard_map/ppermute | solution.py:96
  6.7 0.0 collective-permute-start.1
  6.7 0.6 %collective-permute-start.2 = (bf16[272,128]{1,0:T(8,128)(2,1)S(1)}, bf16[272,128]{1,0:T(8,128)(2,1)S(1)}, u32[]{:S(2)}, u32[]{:S(2)}) collective-permute-start(bf16[272,128]{1,0:T(8,128)(2,1)S(1)} %get-tuple-element.38), channel_id=1, source_target_pairs={{0,2},{1,3},{2,0},{3,1},{4,6},{5,7},{6,4},{7,5},{8,10},{9,11},{10,... | collective-permute-start | bytes 208904 | tf_op jit(solution)/shard_map/ppermute | solution.py:96
  7.4 0.0 copy-start.1
  7.4 3.2 %local_tiles.1 = (f32[16,128,128]{2,1,0:T(8,128)S(1)}, f32[16,128,128]{2,1,0:T(8,128)S(1)}, f32[2,1024,128]{2,1,0:T(8,128)S(1)}, f32[2,256,128]{2,1,0:T(8,128)S(...) custom-call(s32[16]{0:T(128)} %bitcast.15, ...), custom_call_target="tpu_custom_call" | custom-call | flops 268435456 | bytes 8000000 | tf_op jit(solution)/shard_map/local_tiles/pallas_call | solution.py:34
  10.6 0.0 copy-start
  10.6 0.0 collective-permute-done.refs_0_
  10.6 0.1 collective-permute-start.3
  10.7 0.8 %collective-permute-done.1.refs_1_ = bf16[272,128]{1,0:T(8,128)(2,1)S(1)} collective-permute-done((bf16[272,128]{1,0:T(8,128)(2,1)S(1)}, bf16[272,128]{1,0:T(8,128)(2,1)S(1)}, u32[]{:S(2)}, u32[]{:S(2)}) %collective-permute-start.1) | collective-permute-done | bytes 69664 | tf_op jit(solution)/shard_map/ppermute | solution.py:96
  11.6 0.1 collective-permute-start.4
  11.7 0.8 %collective-permute-done.2.refs_2_ = bf16[272,128]{1,0:T(8,128)(2,1)S(1)} collective-permute-done((bf16[272,128]{1,0:T(8,128)(2,1)S(1)}, bf16[272,128]{1,0:T(8,128)(2,1)S(1)}, u32[]{:S(2)}, u32[]{:S(2)}) %collective-permute-start.2) | collective-permute-done | bytes 69664 | tf_op jit(solution)/shard_map/ppermute | solution.py:96
  12.4 0.1 collective-permute-start.5
  12.5 0.0 collective-permute-done.3.refs_3_
  12.5 0.4 %collective-permute-done.4.refs_4_ = bf16[256,128]{1,0:T(8,128)(2,1)S(1)} collective-permute-done((bf16[256,128]{1,0:T(8,128)(2,1)S(1)}, bf16[256,128]{1,0:T(8,128)(2,1)S(1)}, u32[]{:S(2)}, u32[]{:S(2)}) %collective-permute-start.4) | collective-permute-done | bytes 65568 | tf_op jit(solution)/shard_map/ppermute | solution.py:99
  12.9 0.9 %collective-permute-done.5.refs_5_ = bf16[256,128]{1,0:T(8,128)(2,1)S(1)} collective-permute-done((bf16[256,128]{1,0:T(8,128)(2,1)S(1)}, bf16[256,128]{1,0:T(8,128)(2,1)S(1)}, u32[]{:S(2)}, u32[]{:S(2)}) %collective-permute-start.5) | collective-permute-done | bytes 65568 | tf_op jit(solution)/shard_map/ppermute | solution.py:99
  13.8 0.0 copy-done.1
  13.8 0.0 copy-done
  13.8 2.3 %other_tiles.1 = (f32[1024,128]{1,0:T(8,128)S(1)}, f32[1024,128]{1,0:T(8,128)S(1)}, bf16[512,128]{1,0:T(8,128)(2,1)S(1)}, bf16[512,128]{1,0:T(8,128)(2,1)S(1)}, ...) custom-call(s32[16]{0:T(128)} %bitcast.16, s32[16]{0:T(128)} %bitcast.18, s32[4]{0:T(128)} %bitcast.20, ...), custom_call_target="tpu_custom_call" | custom-call | flops 301989888 | bytes 4000000 | tf_op jit(solution)/shard_map/other_tiles/pallas_call | solution.py:34
  16.0 0.2 collective-permute-start.8
  16.3 3.0 %collective-permute-start.6 = (bf16[512,128]{1,0:T(8,128)(2,1)S(1)}, bf16[512,128]{1,0:T(8,128)(2,1)S(1)}, u32[]{:S(2)}, u32[]{:S(2)}) collective-permute-start(bf16[512,128]{1,0:T(8,128)(2,1)S(1)} %get-tuple-element.43), channel_id=1, source_target_pairs={{0,3},{1,2},{2,1},{3,0},{4,7},{5,6},{6,5},{7,4},{8,11},{9,10},{10,... | collective-permute-start | bytes 393224 | tf_op jit(solution)/shard_map/ppermute | solution.py:96
  19.3 0.0 collective-permute-start.7
  19.3 0.0 collective-permute-done.8.recv_ref
  19.3 0.1 fold_core.1
  19.4 1.6 %collective-permute-start.9 = (bf16[256,128]{1,0:T(8,128)(2,1)S(1)}, bf16[256,128]{1,0:T(8,128)(2,1)S(1)}, u32[]{:S(2)}, u32[]{:S(2)}) collective-permute-start(bf16[256,128]{1,0:T(8,128)(2,1)S(1)} %get-tuple-element.48), channel_id=1, source_target_pairs={{0,16},{4,20},{8,24},{12,28},{16,0},{20,4},{24,8},{28,12},{1,17},{... | collective-permute-start | bytes 196616 | tf_op jit(solution)/shard_map/ppermute | solution.py:102
  20.9 1.4 %collective-permute-start.10 = (bf16[256,128]{1,0:T(8,128)(2,1)S(1)}, bf16[256,128]{1,0:T(8,128)(2,1)S(1)}, u32[]{:S(2)}, u32[]{:S(2)}) collective-permute-start(bf16[256,128]{1,0:T(8,128)(2,1)S(1)} %get-tuple-element.49), channel_id=1, source_target_pairs={{0,24},{4,28},{8,16},{12,20},{16,8},{20,12},{24,0},{28,4},{1,25},{... | collective-permute-start | bytes 196616 | tf_op jit(solution)/shard_map/ppermute | solution.py:102
  22.4 0.5 %collective-permute-start.11 = (bf16[256,128]{1,0:T(8,128)(2,1)S(1)}, bf16[256,128]{1,0:T(8,128)(2,1)S(1)}, u32[]{:S(2)}, u32[]{:S(2)}) collective-permute-start(bf16[256,128]{1,0:T(8,128)(2,1)S(1)} %get-tuple-element.50), channel_id=1, source_target_pairs={{0,8},{4,12},{8,0},{12,4},{16,24},{20,28},{24,16},{28,20},{1,9},{5... | collective-permute-start | bytes 196616 | tf_op jit(solution)/shard_map/ppermute | solution.py:102
  22.9 0.8 %collective-permute-done.9.refs_0_ = bf16[256,128]{1,0:T(8,128)(2,1)S(1)} collective-permute-done((bf16[256,128]{1,0:T(8,128)(2,1)S(1)}, bf16[256,128]{1,0:T(8,128)(2,1)S(1)}, u32[]{:S(2)}, u32[]{:S(2)}) %collective-permute-start.9) | collective-permute-done | bytes 65568 | tf_op jit(solution)/shard_map/ppermute | solution.py:102
  23.7 1.4 %collective-permute-start.12 = (bf16[512,128]{1,0:T(8,128)(2,1)S(1)}, bf16[512,128]{1,0:T(8,128)(2,1)S(1)}, u32[]{:S(2)}, u32[]{:S(2)}) collective-permute-start(bf16[512,128]{1,0:T(8,128)(2,1)S(1)} %get-tuple-element.52), channel_id=1, source_target_pairs={{0,1},{1,0},{2,3},{3,2},{4,5},{5,4},{6,7},{7,6},{8,9},{9,8},{10,11... | collective-permute-start | bytes 393224 | tf_op jit(solution)/shard_map/ppermute | solution.py:96
  25.0 1.7 %collective-permute-done.10.refs_1_ = bf16[256,128]{1,0:T(8,128)(2,1)S(1)} collective-permute-done((bf16[256,128]{1,0:T(8,128)(2,1)S(1)}, bf16[256,128]{1,0:T(8,128)(2,1)S(1)}, u32[]{:S(2)}, u32[]{:S(2)}) %collective-permute-start.10) | collective-permute-done | bytes 65568 | tf_op jit(solution)/shard_map/ppermute | solution.py:102
  26.8 0.0 collective-permute-done.11.refs_2_
  26.8 2.0 %collective-permute-start.13 = (bf16[64,128]{1,0:T(8,128)(2,1)S(1)}, bf16[64,128]{1,0:T(8,128)(2,1)S(1)}, u32[]{:S(2)}, u32[]{:S(2)}) collective-permute-start(bf16[64,128]{1,0:T(8,128)(2,1)S(1)} %get-tuple-element.53), channel_id=1, source_target_pairs={{0,3},{1,2},{2,1},{3,0},{4,7},{5,6},{6,5},{7,4},{8,11},{9,10},{10,... | collective-permute-start | bytes 49160 | tf_op jit(solution)/shard_map/ppermute | solution.py:96
  28.8 1.0 %collective-permute-start.14 = (bf16[64,128]{1,0:T(8,128)(2,1)S(1)}, bf16[64,128]{1,0:T(8,128)(2,1)S(1)}, u32[]{:S(2)}, u32[]{:S(2)}) collective-permute-start(bf16[64,128]{1,0:T(8,128)(2,1)S(1)} %get-tuple-element.54), channel_id=1, source_target_pairs={{0,2},{1,3},{2,0},{3,1},{4,6},{5,7},{6,4},{7,5},{8,10},{9,11},{10,... | collective-permute-start | bytes 49160 | tf_op jit(solution)/shard_map/ppermute | solution.py:96
  29.7 0.0 collective-permute-done.6.refs_0_
  29.7 1.5 %collective-permute-start.15 = (bf16[64,128]{1,0:T(8,128)(2,1)S(1)}, bf16[64,128]{1,0:T(8,128)(2,1)S(1)}, u32[]{:S(2)}, u32[]{:S(2)}) collective-permute-start(bf16[64,128]{1,0:T(8,128)(2,1)S(1)} %get-tuple-element.55), channel_id=1, source_target_pairs={{0,1},{1,0},{2,3},{3,2},{4,5},{5,4},{6,7},{7,6},{8,9},{9,8},{10,11... | collective-permute-start | bytes 49160 | tf_op jit(solution)/shard_map/ppermute | solution.py:96
  31.3 0.8 %collective-permute-done.7.refs_1_ = bf16[512,128]{1,0:T(8,128)(2,1)S(1)} collective-permute-done((bf16[512,128]{1,0:T(8,128)(2,1)S(1)}, bf16[512,128]{1,0:T(8,128)(2,1)S(1)}, u32[]{:S(2)}, u32[]{:S(2)}) %collective-permute-start.7) | collective-permute-done | bytes 131104 | tf_op jit(solution)/shard_map/ppermute | solution.py:96
  32.2 0.0 collective-permute-done.12.refs_0_
  32.2 0.4 %collective-permute-done.13.refs_1_ = bf16[64,128]{1,0:T(8,128)(2,1)S(1)} collective-permute-done((bf16[64,128]{1,0:T(8,128)(2,1)S(1)}, bf16[64,128]{1,0:T(8,128)(2,1)S(1)}, u32[]{:S(2)}, u32[]{:S(2)}) %collective-permute-start.13) | collective-permute-done | bytes 16416 | tf_op jit(solution)/shard_map/ppermute | solution.py:96
  32.6 0.9 %collective-permute-done.14.refs_2_ = bf16[64,128]{1,0:T(8,128)(2,1)S(1)} collective-permute-done((bf16[64,128]{1,0:T(8,128)(2,1)S(1)}, bf16[64,128]{1,0:T(8,128)(2,1)S(1)}, u32[]{:S(2)}, u32[]{:S(2)}) %collective-permute-start.14) | collective-permute-done | bytes 16416 | tf_op jit(solution)/shard_map/ppermute | solution.py:96
  33.4 0.2 collective-permute-done.15.refs_3_
  33.6 0.7 %finish.1 = (f32[256,128]{1,0:T(8,128)}, f32[256,128]{1,0:T(8,128)}, f32[32,128]{1,0:T(8,128)}, f32[32,128]{1,0:T(8,128)}) custom-call(f32[512,128]{1,0:T(8,128)S(1)} %sum_users.1.user_ref, f32[64,128]{1,0:T(8,128)S(1)} %get-tuple-element.51.item_ref, bf16[512,128]{1,0:T(8,128)(2,1)S(1)} %collective-permute-done.12.refs_0_, ...), custom_call_target="tpu_custom_call" | custom-call | bytes 1000 | tf_op jit(solution)/shard_map/finish/pallas_call | solution.py:34
  (8 shorter events, 0.1 us)
Async XLA Ops:
  1.6 9.0 %collective-permute-start = (bf16[272,128]{1,0:T(8,128)(2,1)S(1)}, bf16[272,128]{1,0:T(8,128)(2,1)S(1)}, u32[]{:S(2)}, u32[]{:S(2)}) collective-permute-start(bf16[272,128]{1,0:T(8,128)(2,1)S(1)} %get-tuple-element.36), channel_id=1, source_target_pairs={{0,3},{1,2},{2,1},{3,0},{4,7},{5,6},{6,5},{7,4},{8,11},{9,10},{10,... | collective-permute-start | bytes 208904 | tf_op jit(solution)/shard_map/ppermute | solution.py:96
  6.7 4.9 %collective-permute-start.1 = (bf16[272,128]{1,0:T(8,128)(2,1)S(1)}, bf16[272,128]{1,0:T(8,128)(2,1)S(1)}, u32[]{:S(2)}, u32[]{:S(2)}) collective-permute-start(bf16[272,128]{1,0:T(8,128)(2,1)S(1)} %get-tuple-element.37), channel_id=1, source_target_pairs={{0,1},{1,0},{2,3},{3,2},{4,5},{5,4},{6,7},{7,6},{8,9},{9,8},{10,11... | collective-permute-start | bytes 208904 | tf_op jit(solution)/shard_map/ppermute | solution.py:96
  6.7 5.7 %collective-permute-start.2 = (bf16[272,128]{1,0:T(8,128)(2,1)S(1)}, bf16[272,128]{1,0:T(8,128)(2,1)S(1)}, u32[]{:S(2)}, u32[]{:S(2)}) collective-permute-start(bf16[272,128]{1,0:T(8,128)(2,1)S(1)} %get-tuple-element.38), channel_id=1, source_target_pairs={{0,2},{1,3},{2,0},{3,1},{4,6},{5,7},{6,4},{7,5},{8,10},{9,11},{10,... | collective-permute-start | bytes 208904 | tf_op jit(solution)/shard_map/ppermute | solution.py:96
  7.4 6.4 %copy-start.1 = (bf16[1024,128]{1,0:T(8,128)(2,1)S(1)}, bf16[1024,128]{1,0:T(8,128)(2,1)}, u32[]{:S(2)}) copy-start(bf16[1024,128]{1,0:T(8,128)(2,1)} %ux_ref.1) | copy-start | bytes 786436
  10.6 3.2 %copy-start = (bf16[1024,128]{1,0:T(8,128)(2,1)S(1)}, bf16[1024,128]{1,0:T(8,128)(2,1)}, u32[]{:S(2)}) copy-start(bf16[1024,128]{1,0:T(8,128)(2,1)} %up_ref.1) | copy-start | bytes 786436
  10.6 1.9 %collective-permute-start.3 = (bf16[256,128]{1,0:T(8,128)(2,1)S(1)}, bf16[256,128]{1,0:T(8,128)(2,1)S(1)}, u32[]{:S(2)}, u32[]{:S(2)}) collective-permute-start(bf16[256,128]{1,0:T(8,128)(2,1)S(1)} %slice_multiply_fusion.2), channel_id=1, source_target_pairs={{0,4},{4,0},{8,12},{12,8},{16,20},{20,16},{24,28},{28,24},{1,5},{5... | collective-permute-start | bytes 196616 | tf_op jit(solution)/shard_map/ppermute | solution.py:99
  11.6 1.3 %collective-permute-start.4 = (bf16[256,128]{1,0:T(8,128)(2,1)S(1)}, bf16[256,128]{1,0:T(8,128)(2,1)S(1)}, u32[]{:S(2)}, u32[]{:S(2)}) collective-permute-start(bf16[256,128]{1,0:T(8,128)(2,1)S(1)} %slice_multiply_fusion.1), channel_id=1, source_target_pairs={{0,4},{4,0},{8,12},{12,8},{16,20},{20,16},{24,28},{28,24},{1,5},{5... | collective-permute-start | bytes 196616 | tf_op jit(solution)/shard_map/ppermute | solution.py:99
  12.4 1.3 %collective-permute-start.5 = (bf16[256,128]{1,0:T(8,128)(2,1)S(1)}, bf16[256,128]{1,0:T(8,128)(2,1)S(1)}, u32[]{:S(2)}, u32[]{:S(2)}) collective-permute-start(bf16[256,128]{1,0:T(8,128)(2,1)S(1)} %slice_multiply_fusion), channel_id=1, source_target_pairs={{0,4},{4,0},{8,12},{12,8},{16,20},{20,16},{24,28},{28,24},{1,5},{5... | collective-permute-start | bytes 196616 | tf_op jit(solution)/shard_map/ppermute | solution.py:99
  16.0 3.3 %collective-permute-start.8 = (f32[1024,128]{1,0:T(8,128)S(1)}, f32[1024,128]{1,0:T(8,128)S(1)}, u32[]{:S(2)}, u32[]{:S(2)}) collective-permute-start(f32[1024,128]{1,0:T(8,128)S(1)} %get-tuple-element.46), channel_id=1, source_target_pairs={{0,4},{4,0},{8,12},{12,8},{16,20},{20,16},{24,28},{28,24},{1,5},{5... | collective-permute-start | bytes 1572872 | tf_op jit(solution)/shard_map/ppermute | solution.py:99
  16.3 13.5 %collective-permute-start.6 = (bf16[512,128]{1,0:T(8,128)(2,1)S(1)}, bf16[512,128]{1,0:T(8,128)(2,1)S(1)}, u32[]{:S(2)}, u32[]{:S(2)}) collective-permute-start(bf16[512,128]{1,0:T(8,128)(2,1)S(1)} %get-tuple-element.43), channel_id=1, source_target_pairs={{0,3},{1,2},{2,1},{3,0},{4,7},{5,6},{6,5},{7,4},{8,11},{9,10},{10,... | collective-permute-start | bytes 393224 | tf_op jit(solution)/shard_map/ppermute | solution.py:96
  19.3 12.8 %collective-permute-start.7 = (bf16[512,128]{1,0:T(8,128)(2,1)S(1)}, bf16[512,128]{1,0:T(8,128)(2,1)S(1)}, u32[]{:S(2)}, u32[]{:S(2)}) collective-permute-start(bf16[512,128]{1,0:T(8,128)(2,1)S(1)} %get-tuple-element.44), channel_id=1, source_target_pairs={{0,2},{1,3},{2,0},{3,1},{4,6},{5,7},{6,4},{7,5},{8,10},{9,11},{10,... | collective-permute-start | bytes 393224 | tf_op jit(solution)/shard_map/ppermute | solution.py:96
  19.4 4.3 %collective-permute-start.9 = (bf16[256,128]{1,0:T(8,128)(2,1)S(1)}, bf16[256,128]{1,0:T(8,128)(2,1)S(1)}, u32[]{:S(2)}, u32[]{:S(2)}) collective-permute-start(bf16[256,128]{1,0:T(8,128)(2,1)S(1)} %get-tuple-element.48), channel_id=1, source_target_pairs={{0,16},{4,20},{8,24},{12,28},{16,0},{20,4},{24,8},{28,12},{1,17},{... | collective-permute-start | bytes 196616 | tf_op jit(solution)/shard_map/ppermute | solution.py:102
  20.9 5.8 %collective-permute-start.10 = (bf16[256,128]{1,0:T(8,128)(2,1)S(1)}, bf16[256,128]{1,0:T(8,128)(2,1)S(1)}, u32[]{:S(2)}, u32[]{:S(2)}) collective-permute-start(bf16[256,128]{1,0:T(8,128)(2,1)S(1)} %get-tuple-element.49), channel_id=1, source_target_pairs={{0,24},{4,28},{8,16},{12,20},{16,8},{20,12},{24,0},{28,4},{1,25},{... | collective-permute-start | bytes 196616 | tf_op jit(solution)/shard_map/ppermute | solution.py:102
  22.4 4.4 %collective-permute-start.11 = (bf16[256,128]{1,0:T(8,128)(2,1)S(1)}, bf16[256,128]{1,0:T(8,128)(2,1)S(1)}, u32[]{:S(2)}, u32[]{:S(2)}) collective-permute-start(bf16[256,128]{1,0:T(8,128)(2,1)S(1)} %get-tuple-element.50), channel_id=1, source_target_pairs={{0,8},{4,12},{8,0},{12,4},{16,24},{20,28},{24,16},{28,20},{1,9},{5... | collective-permute-start | bytes 196616 | tf_op jit(solution)/shard_map/ppermute | solution.py:102
  23.7 8.5 %collective-permute-start.12 = (bf16[512,128]{1,0:T(8,128)(2,1)S(1)}, bf16[512,128]{1,0:T(8,128)(2,1)S(1)}, u32[]{:S(2)}, u32[]{:S(2)}) collective-permute-start(bf16[512,128]{1,0:T(8,128)(2,1)S(1)} %get-tuple-element.52), channel_id=1, source_target_pairs={{0,1},{1,0},{2,3},{3,2},{4,5},{5,4},{6,7},{7,6},{8,9},{9,8},{10,11... | collective-permute-start | bytes 393224 | tf_op jit(solution)/shard_map/ppermute | solution.py:96
  26.8 5.8 %collective-permute-start.13 = (bf16[64,128]{1,0:T(8,128)(2,1)S(1)}, bf16[64,128]{1,0:T(8,128)(2,1)S(1)}, u32[]{:S(2)}, u32[]{:S(2)}) collective-permute-start(bf16[64,128]{1,0:T(8,128)(2,1)S(1)} %get-tuple-element.53), channel_id=1, source_target_pairs={{0,3},{1,2},{2,1},{3,0},{4,7},{5,6},{6,5},{7,4},{8,11},{9,10},{10,... | collective-permute-start | bytes 49160 | tf_op jit(solution)/shard_map/ppermute | solution.py:96
  28.8 4.6 %collective-permute-start.14 = (bf16[64,128]{1,0:T(8,128)(2,1)S(1)}, bf16[64,128]{1,0:T(8,128)(2,1)S(1)}, u32[]{:S(2)}, u32[]{:S(2)}) collective-permute-start(bf16[64,128]{1,0:T(8,128)(2,1)S(1)} %get-tuple-element.54), channel_id=1, source_target_pairs={{0,2},{1,3},{2,0},{3,1},{4,6},{5,7},{6,4},{7,5},{8,10},{9,11},{10,... | collective-permute-start | bytes 49160 | tf_op jit(solution)/shard_map/ppermute | solution.py:96
  29.7 3.8 %collective-permute-start.15 = (bf16[64,128]{1,0:T(8,128)(2,1)S(1)}, bf16[64,128]{1,0:T(8,128)(2,1)S(1)}, u32[]{:S(2)}, u32[]{:S(2)}) collective-permute-start(bf16[64,128]{1,0:T(8,128)(2,1)S(1)} %get-tuple-element.55), channel_id=1, source_target_pairs={{0,1},{1,0},{2,3},{3,2},{4,5},{5,4},{6,7},{7,6},{8,9},{9,8},{10,11... | collective-permute-start | bytes 49160 | tf_op jit(solution)/shard_map/ppermute | solution.py:96
